TPU v7x, 32 devices: a whole 2x2x4 slice. The times are simulated.
32 devices in a mesh: group: 4 (over x, core), batch: 8 (over z, y).
Axes of the slice: x: 2, y: 2, z: 4, core: 2. Of those that a mesh axis runs over, the one named last changes fastest.
Arguments:
- panel_alleles: int32 [32, 131072], P('group', 'batch'), may hold values 0 or 1
- recomb_rates: float32 [32], P('group'), may hold values from 0.001 to 0.3
- genotypes: int32 [2, 32], P(None, 'group'), may hold values from 0 to 2, as said below
Outputs:
- dosage: float32 [2, 32], P(None, 'group')
- log_likelihood: float32 [2], replicated
Inputs may be any that keep to these rules, and one draw needn't show every extreme that they name: `genotypes`: 2 marks a marker at which the target's allele is missing; 0 and 1 are observed alleles.
All inputs are finite; a program needn't handle non-finite values. No bound on the sum of `panel_alleles` on one device may be relied on, other than what follows from the above.
Results may differ from a plain program's by a relative error of at most 0.0003.
Values sent between devices are 32-bit elements; how exact they have to be, the bound alone decides.
No kernel may reach another device: no remote copies, remote signals or barrier semaphores. Data moves between devices by JAX's collectives and lax.ppermute only.
A program may use at most 64 MiB of HBM per device.

v0:
```python
import jax
import jax.numpy as jnp
from jax import lax
from jax.sharding import PartitionSpec as P

K = 131072


MISMATCH = 0.05
HIGHEST = lax.Precision.HIGHEST


def from_behind(x, axis, by):
    peers = lax.axis_size(axis)
    pairs = [(i, i + by) for i in range(peers) if 0 <= i + by < peers]
    return lax.ppermute(x, axis, pairs)


def emission(panel_rows, geno_col):
    observed = geno_col[:, None]
    agrees = jnp.where(panel_rows == observed, 1.0 - MISMATCH, MISMATCH)
    return jnp.where(observed == 2, 1.0, agrees).astype(jnp.float32)


def forward_terms(panel_rows, geno_col, switches):
    emitted = emission(panel_rows, geno_col)
    retain = emitted * (1.0 - switches)[:, None]
    inject = emitted * (switches / K)[:, None]
    return (retain, inject, None)


def backward_terms(panel_rows, geno_col, switches):
    emitted = emission(panel_rows, geno_col)[::-1]
    flipped = switches[::-1]
    retain = emitted * (1.0 - flipped)[:, None]
    inject = jnp.broadcast_to((flipped / K)[:, None], emitted.shape)
    return (retain, inject, emitted)


def partial_sums(entering, retain, inject, weight, extent):
    logs = jnp.cumsum(jnp.log(retain), axis=0)
    shifted = jnp.concatenate([jnp.zeros_like(entering)[None], logs[: extent - 1]], axis=0)
    before = jnp.exp(shifted)
    left_side = before if weight is None else weight * before
    leading = jnp.einsum("jk,k->j", left_side, entering, precision=HIGHEST)
    anchor = shifted[0]
    right_side = inject * jnp.exp(anchor[None] - logs)
    nearby = jnp.exp(jnp.minimum(shifted - anchor[None], 0.0))
    nearby = nearby if weight is None else weight * nearby
    columns = [jnp.einsum("jk,tk->jt", nearby, right_side, precision=HIGHEST)]
    coupling = jnp.concatenate(columns, axis=1)
    return (leading, coupling)


def solve_sums(leading, coupling):
    columns = coupling.shape[1]

    def settle(marker, sigmas):
        below = jnp.arange(columns) < marker
        update = leading[marker] + jnp.sum(
            jnp.where(below, coupling[marker] * sigmas[:columns], 0.0)
        )
        return sigmas.at[marker].set(update)

    return lax.fori_loop(0, leading.shape[0], settle, jnp.zeros_like(leading))


def advance(entering, retain, inject, sigmas, keep_states):

    def advance_single(current, pieces):
        current = pieces[0] * current + pieces[1] * pieces[2]
        return (current, current if keep_states else None)

    return lax.scan(advance_single, entering, (retain, inject, sigmas[: retain.shape[0]]))


def place_rows(store, block, active):
    return jnp.where(active, block, store)


def on_device(panel_alleles, recomb_rates, genotypes):
    chain_size = lax.axis_size("group")
    position = lax.axis_index("group")
    markers, width = panel_alleles.shape
    targets = genotypes.shape[0]
    bundles = targets // targets
    uniform = jnp.full((targets, width), 1.0 / K, jnp.float32)
    first_row = position == 0
    last_row = position == chain_size - 1

    def local_sums(active, arrivals, geno_rows, maker, extent):

        def local_compute():

            def local_single(pieces):
                retain, inject, weight = maker(panel_alleles, pieces[1], recomb_rates)
                return partial_sums(pieces[0], retain, inject, weight, extent)

            return lax.map(local_single, (arrivals, geno_rows))

        def local_skipped():
            return (
                jnp.zeros((targets, extent), jnp.float32),
                jnp.zeros((targets, extent, markers), jnp.float32),
            )

        return lax.cond(active, local_compute, local_skipped)

    def outgoing(active, arrivals, geno_rows, sigmas, maker, scale_row):

        def outgoing_compute():

            def outgoing_single(pieces):
                retain, inject, weight = maker(panel_alleles, pieces[1], recomb_rates)
                ending, unused = advance(pieces[0], retain, inject, pieces[2], False)
                return ending / pieces[2][scale_row]

            return lax.map(outgoing_single, (arrivals, geno_rows, sigmas))

        def outgoing_skipped():
            return jnp.zeros((targets, width), jnp.float32)

        return lax.cond(active, outgoing_compute, outgoing_skipped)

    def moment_step(moment, carried_state):
        (
            sent_forward,
            sent_backward,
            sent_running,
            store_forward,
            store_backward,
            sigma_forward,
            sigma_backward,
            log_terms,
        ) = carried_state
        got_forward = from_behind(sent_forward, "group", 1)
        got_backward = from_behind(sent_backward, "group", -1)
        entering_forward = jnp.where(first_row, uniform, got_forward)
        entering_backward = jnp.where(last_row, uniform, got_backward)
        index_forward = moment - position
        index_backward = moment - (chain_size - 1 - position)
        active_forward = (index_forward >= 0) & (index_forward < bundles)
        active_backward = (index_backward >= 0) & (index_backward < bundles)
        lead_forward, couple_forward = local_sums(
            active_forward, entering_forward, genotypes, forward_terms, markers + 1
        )
        lead_backward, couple_backward = local_sums(
            active_backward, entering_backward, genotypes, backward_terms, markers
        )
        lead_forward, couple_forward, lead_backward, couple_backward = lax.psum(
            (lead_forward, couple_forward, lead_backward, couple_backward), "batch"
        )
        sigmas_forward = jax.vmap(solve_sums)(lead_forward, couple_forward)
        sigmas_backward = jax.vmap(solve_sums)(lead_backward, couple_backward)
        next_forward = outgoing(
            active_forward, entering_forward, genotypes, sigmas_forward, forward_terms, markers
        )
        next_backward = outgoing(
            active_backward,
            entering_backward,
            genotypes,
            sigmas_backward,
            backward_terms,
            markers - 1,
        )
        guarded = jnp.where(active_forward, sigmas_forward[:, markers], 1.0)
        running = jnp.log(guarded)
        store_forward = place_rows(store_forward, entering_forward, active_forward)
        store_backward = place_rows(store_backward, entering_backward, active_backward)
        sigma_forward = place_rows(sigma_forward, sigmas_forward, active_forward)
        sigma_backward = place_rows(sigma_backward, sigmas_backward, active_backward)
        log_terms = place_rows(log_terms, running, active_forward)
        return (
            next_forward,
            next_backward,
            running,
            store_forward,
            store_backward,
            sigma_forward,
            sigma_backward,
            log_terms,
        )

    initial = (
        jnp.zeros((targets, width), jnp.float32),
        jnp.zeros((targets, width), jnp.float32),
        jnp.zeros((targets,), jnp.float32),
        jnp.zeros((targets, width), jnp.float32),
        jnp.zeros((targets, width), jnp.float32),
        jnp.zeros((targets, markers + 1), jnp.float32),
        jnp.zeros((targets, markers), jnp.float32),
        jnp.zeros((targets,), jnp.float32),
    )
    final_state = lax.fori_loop(0, chain_size + bundles - 1, moment_step, initial)
    store_forward, store_backward, sigma_forward, sigma_backward, log_terms = final_state[3:]
    whole_log = lax.psum(log_terms, "group")
    log_likelihood = whole_log / (markers * chain_size)

    def posterior(pieces):
        entering_ahead, entering_behind, geno_col, sigmas_ahead, sigmas_behind = pieces
        retain, inject, weight = forward_terms(panel_alleles, geno_col, recomb_rates)
        unused_f, forward_states = advance(entering_ahead, retain, inject, sigmas_ahead, True)
        forward_rows = forward_states / sigmas_ahead[1:, None]
        retain, inject, weight = backward_terms(panel_alleles, geno_col, recomb_rates)
        unused_b, backward_states = advance(entering_behind, retain, inject, sigmas_behind, True)
        scaled_back = backward_states[:-1] / sigmas_behind[:-1, None]
        backward_rows = jnp.concatenate([entering_behind[None], scaled_back], axis=0)[::-1]
        product = forward_rows * backward_rows
        numerator = jnp.sum(jnp.where(panel_alleles == 1, product, 0.0), axis=1)
        return (numerator, jnp.sum(product, axis=1))

    numerator, denominator = lax.map(
        posterior, (store_forward, store_backward, genotypes, sigma_forward, sigma_backward)
    )
    numerator, denominator = lax.psum((numerator, denominator), "batch")
    return (numerator / denominator, log_likelihood)


def solution(mesh):
    placed = (P("group", "batch"), P("group"), P(None, "group"))
    return jax.shard_map(
        on_device, mesh=mesh, in_specs=placed, out_specs=(P(None, "group"), P()), check_vma=False
    )
```

profile of v0, /device:TPU:0, one launch (start us, length us, event | category | flops | bytes accessed | tf_op | source)
XLA Modules:
  0.0 583.4 jit_solution(1752994374807820899)
XLA Ops:
  2.1 479.0 %while.198 = (s32[]{:T(128)}, f32[2,16384]{1,0:T(2,128)}, f32[2,16384]{1,0:T(2,128)}, f32[2,16384]{1,0:T(2,128)S(1)}, f32[2,16384]{1,0:T(2,128)S(1)}, /*index=5*...) while((s32[]{:T(128)}, f32[2,16384]{1,0:T(2,128)}, ...), condition=%wide.region_35.36_spmd.clone, body=%wide.region_0.35_spmd.clone.sunk | while | flops 36192892 | bytes 22367984 | solution.py:194
  6.1 11.2 %conditional.12 = (f32[2,9]{1,0:T(2,128)}, f32[2,9,8]{1,2,0:T(8,128)}) conditional(s32[]{:T(128)} %convert_element_type.22, () %tuple.345, (s32[2,8]{1,0:T(2,128)S(1)}, s32[8,16384]{1,0:T(8,128)S(1)}, f32[8]{0:T(128)S(1)}, f32[2,16384]{1,0:T(2,128)S(1)}) %tuple.424), branch_computations={%region_1.1_spmd, %region_2.5_spmd} | conditional | flops 18169880 | bytes 4003897 | solution.py:107
  6.1 11.1 %while.181 = (s32[]{:T(128)}, f32[2,9]{1,0:T(2,128)}, f32[2,9,8]{1,2,0:T(8,128)}, s32[2,8]{1,0:T(2,128)S(1)}, s32[8,16384]{1,0:T(8,128)S(1)}, /*index=5*/f32[8]{...) while((s32[]{:T(128)}, f32[2,9]{1,0:T(2,128)}, f32[2,9,8]{1,2,0:T(8,128)}, ...), condition=%wide.region_5.4_spmd, body=%wide.region_3.3_spmd.sunk | while | flops 18169880 | bytes 4003793 | solution.py:99
  20.1 38.9 %all-reduce.5 = (f32[2,9]{1,0:T(2,128)S(1)}, f32[2,9,8]{2,0,1:T(2,128)S(1)}, f32[2,8]{1,0:T(2,128)S(1)}, f32[2,8,8]{2,0,1:T(2,128)S(1)}) all-reduce(f32[2,9]{1,0:T(2,128)} %get-tuple-element.1830, f32[2,9,8]{2,0,1:T(2,128)S(1)} %copy.29, f32[2,8]{1,0:T(2,128)} %get-tuple-element.1833, ...), channel_id=1, replica_groups=mesh['group'=4,'batch'=8] {'batch'}, use_global_device_ids=true, to_apply=%region_6.6 | all-reduce | flops 306 | bytes 2448 | tf_op jit(solution)/shard_map/while/body/eval_jaxpr/psum | solution.py:150
  59.0 17.9 %while.201 = (s32[]{:T(128)}, f32[2,9]{1,0:T(2,128)S(1)}, f32[2,9]{1,0:T(2,128)S(1)}, f32[2,9,8]{2,0,1:T(2,128)S(1)}, s32[]{:T(128)}, /*index=5*/s32[1]{0:T(128)}, s32[]{:T(128)}) while((s32[]{:T(128)}, f32[2,9]{1,0:T(2,128)S(1)}, f32[2,9]{1,0:T(2,128)S(1)}, f32[2,9,8]{2,0,1:T(2,128)S(1)}, s32[]{:T(128)}, /*index=5*/s32[1]{0:T(128)}, ...), condition=%wide.region_11.11_spmd, body=%wide.region_8.10_spmd.sunk | while | flops 73 | bytes 623 | solution.py:65
  77.1 15.7 %while.202 = (s32[]{:T(128)}, f32[2,8]{1,0:T(2,128)S(1)}, f32[2,8]{1,0:T(2,128)S(1)}, f32[2,8,8]{2,0,1:T(2,128)S(1)}, s32[]{:T(128)}, /*index=5*/s32[1]{0:T(128)}, s32[]{:T(128)}) while((s32[]{:T(128)}, f32[2,8]{1,0:T(2,128)S(1)}, f32[2,8]{1,0:T(2,128)S(1)}, f32[2,8,8]{2,0,1:T(2,128)S(1)}, s32[]{:T(128)}, /*index=5*/s32[1]{0:T(128)}, ...), condition=%wide.region_28.28_spmd, body=%wide.region_25.27_spmd.sunk | while | flops 73 | bytes 591 | solution.py:65
  93.5 27.6 %conditional.14 = (f32[2,16384]{1,0:T(2,128)}) conditional(s32[]{:T(128)} %convert_element_type.22, () %tuple.344, (f32[2,16384]{1,0:T(2,128)S(1)}, s32[2,8]{1,0:T(2,128)S(1)}, s32[8,16384]{1,0:T(8,128)S(1)}, f32[8]{0:T(128)S(1)}, f32[2,9]{1,0:T(2,128)S(1)}) %tuple.427), branch_computations={%region_12.12_spmd, %region_13.17_spmd} | conditional | flops 983068 | bytes 2753298 | solution.py:123
  93.5 27.6 %while.184 = (s32[]{:T(128)}, f32[2,16384]{1,0:T(2,128)}, f32[2,16384]{1,0:T(2,128)S(1)}, s32[2,8]{1,0:T(2,128)S(1)}, s32[8,16384]{1,0:T(8,128)S(1)}, /*index=5*...) while((s32[]{:T(128)}, f32[2,16384]{1,0:T(2,128)}, f32[2,16384]{1,0:T(2,128)S(1)}, ...), condition=%wide.region_17.16_spmd, body=%wide.region_14.15_spmd.sunk | while | flops 983068 | bytes 2753202 | solution.py:118
  93.9 10.4 %while.204 = (s32[]{:T(128)}, f32[16384]{0:T(1024)S(1)}, f32[8,16384]{1,0:T(8,128)S(1)}, f32[8,16384]{1,0:T(8,128)S(1)}, f32[8]{0:T(128)S(1)}, /*index=5*/s32[]{:T(128)}) while((s32[]{:T(128)}, f32[16384]{0:T(1024)S(1)}, f32[8,16384]{1,0:T(8,128)S(1)}, f32[8,16384]{1,0:T(8,128)S(1)}, f32[8]{0:T(128)S(1)}, /*index=5*/s32[]{:T(128)}) %tuple.430), condition=%wide.region_16.14_spmd, body=%wide.region_15.13_spmd.sunk | while | flops 49154 | bytes 524377 | solution.py:74
  107.7 10.4 %while.204 = (s32[]{:T(128)}, f32[16384]{0:T(1024)S(1)}, f32[8,16384]{1,0:T(8,128)S(1)}, f32[8,16384]{1,0:T(8,128)S(1)}, f32[8]{0:T(128)S(1)}, /*index=5*/s32[]{:T(128)}) while((s32[]{:T(128)}, f32[16384]{0:T(1024)S(1)}, f32[8,16384]{1,0:T(8,128)S(1)}, f32[8,16384]{1,0:T(8,128)S(1)}, f32[8]{0:T(128)S(1)}, /*index=5*/s32[]{:T(128)}) %tuple.430), condition=%wide.region_16.14_spmd, body=%wide.region_15.13_spmd.sunk | while | flops 49154 | bytes 524377 | solution.py:74
  128.1 33.6 %all-reduce.5 = (f32[2,9]{1,0:T(2,128)S(1)}, f32[2,9,8]{2,0,1:T(2,128)S(1)}, f32[2,8]{1,0:T(2,128)S(1)}, f32[2,8,8]{2,0,1:T(2,128)S(1)}) all-reduce(f32[2,9]{1,0:T(2,128)} %get-tuple-element.1830, f32[2,9,8]{2,0,1:T(2,128)S(1)} %copy.29, f32[2,8]{1,0:T(2,128)} %get-tuple-element.1833, ...), channel_id=1, replica_groups=mesh['group'=4,'batch'=8] {'batch'}, use_global_device_ids=true, to_apply=%region_6.6 | all-reduce | flops 306 | bytes 2448 | tf_op jit(solution)/shard_map/while/body/eval_jaxpr/psum | solution.py:150
  161.7 17.9 %while.201 = (s32[]{:T(128)}, f32[2,9]{1,0:T(2,128)S(1)}, f32[2,9]{1,0:T(2,128)S(1)}, f32[2,9,8]{2,0,1:T(2,128)S(1)}, s32[]{:T(128)}, /*index=5*/s32[1]{0:T(128)}, s32[]{:T(128)}) while((s32[]{:T(128)}, f32[2,9]{1,0:T(2,128)S(1)}, f32[2,9]{1,0:T(2,128)S(1)}, f32[2,9,8]{2,0,1:T(2,128)S(1)}, s32[]{:T(128)}, /*index=5*/s32[1]{0:T(128)}, ...), condition=%wide.region_11.11_spmd, body=%wide.region_8.10_spmd.sunk | while | flops 73 | bytes 623 | solution.py:65
  179.7 15.7 %while.202 = (s32[]{:T(128)}, f32[2,8]{1,0:T(2,128)S(1)}, f32[2,8]{1,0:T(2,128)S(1)}, f32[2,8,8]{2,0,1:T(2,128)S(1)}, s32[]{:T(128)}, /*index=5*/s32[1]{0:T(128)}, s32[]{:T(128)}) while((s32[]{:T(128)}, f32[2,8]{1,0:T(2,128)S(1)}, f32[2,8]{1,0:T(2,128)S(1)}, f32[2,8,8]{2,0,1:T(2,128)S(1)}, s32[]{:T(128)}, /*index=5*/s32[1]{0:T(128)}, ...), condition=%wide.region_28.28_spmd, body=%wide.region_25.27_spmd.sunk | while | flops 73 | bytes 591 | solution.py:65
  196.8 33.2 %collective-permute-start = (f32[2,16384]{1,0:T(2,128)}, f32[2,16384]{1,0:T(2,128)S(1)}, u32[]{:S(2)}, u32[]{:S(2)}) collective-permute-start(f32[2,16384]{1,0:T(2,128)} %get-tuple-element.2213), channel_id=1, source_target_pairs={{0,8},{8,16},{16,24},{1,9},{9,17},{17,25},{2,10},{10,18},{18,26},{... | collective-permute-start | bytes 393224 | tf_op jit(solution)/shard_map/while/body/eval_jaxpr/ppermute | solution.py:16
  233.4 16.5 %collective-permute-done.1 = f32[2,16384]{1,0:T(2,128)S(1)} collective-permute-done((f32[2,16384]{1,0:T(2,128)}, f32[2,16384]{1,0:T(2,128)S(1)}, u32[]{:S(2)}, u32[]{:S(2)}) %collective-permute-start.1) | collective-permute-done | bytes 131104 | tf_op jit(solution)/shard_map/while/body/eval_jaxpr/ppermute | solution.py:16
  252.0 33.6 %all-reduce.5 = (f32[2,9]{1,0:T(2,128)S(1)}, f32[2,9,8]{2,0,1:T(2,128)S(1)}, f32[2,8]{1,0:T(2,128)S(1)}, f32[2,8,8]{2,0,1:T(2,128)S(1)}) all-reduce(f32[2,9]{1,0:T(2,128)} %get-tuple-element.1830, f32[2,9,8]{2,0,1:T(2,128)S(1)} %copy.29, f32[2,8]{1,0:T(2,128)} %get-tuple-element.1833, ...), channel_id=1, replica_groups=mesh['group'=4,'batch'=8] {'batch'}, use_global_device_ids=true, to_apply=%region_6.6 | all-reduce | flops 306 | bytes 2448 | tf_op jit(solution)/shard_map/while/body/eval_jaxpr/psum | solution.py:150
  285.6 17.9 %while.201 = (s32[]{:T(128)}, f32[2,9]{1,0:T(2,128)S(1)}, f32[2,9]{1,0:T(2,128)S(1)}, f32[2,9,8]{2,0,1:T(2,128)S(1)}, s32[]{:T(128)}, /*index=5*/s32[1]{0:T(128)}, s32[]{:T(128)}) while((s32[]{:T(128)}, f32[2,9]{1,0:T(2,128)S(1)}, f32[2,9]{1,0:T(2,128)S(1)}, f32[2,9,8]{2,0,1:T(2,128)S(1)}, s32[]{:T(128)}, /*index=5*/s32[1]{0:T(128)}, ...), condition=%wide.region_11.11_spmd, body=%wide.region_8.10_spmd.sunk | while | flops 73 | bytes 623 | solution.py:65
  303.6 15.7 %while.202 = (s32[]{:T(128)}, f32[2,8]{1,0:T(2,128)S(1)}, f32[2,8]{1,0:T(2,128)S(1)}, f32[2,8,8]{2,0,1:T(2,128)S(1)}, s32[]{:T(128)}, /*index=5*/s32[1]{0:T(128)}, s32[]{:T(128)}) while((s32[]{:T(128)}, f32[2,8]{1,0:T(2,128)S(1)}, f32[2,8]{1,0:T(2,128)S(1)}, f32[2,8,8]{2,0,1:T(2,128)S(1)}, s32[]{:T(128)}, /*index=5*/s32[1]{0:T(128)}, ...), condition=%wide.region_28.28_spmd, body=%wide.region_25.27_spmd.sunk | while | flops 73 | bytes 591 | solution.py:65
  320.7 42.4 %collective-permute-start = (f32[2,16384]{1,0:T(2,128)}, f32[2,16384]{1,0:T(2,128)S(1)}, u32[]{:S(2)}, u32[]{:S(2)}) collective-permute-start(f32[2,16384]{1,0:T(2,128)} %get-tuple-element.2213), channel_id=1, source_target_pairs={{0,8},{8,16},{16,24},{1,9},{9,17},{17,25},{2,10},{10,18},{18,26},{... | collective-permute-start | bytes 393224 | tf_op jit(solution)/shard_map/while/body/eval_jaxpr/ppermute | solution.py:16
  366.7 14.6 %conditional.13 = (f32[2,8]{1,0:T(2,128)}, f32[2,8,8]{2,1,0:T(8,128)}) conditional(s32[]{:T(128)} %convert_element_type.23, () %tuple.347, (s32[2,8]{1,0:T(2,128)S(1)}, s32[8,16384]{1,0:T(8,128)S(1)}, f32[8]{0:T(128)S(1)}, f32[2,16384]{1,0:T(2,128)S(1)}) %tuple.425), branch_computations={%region_18.18_spmd, %region_19.22_spmd} | conditional | flops 16252954 | bytes 6821005 | solution.py:107
  366.8 14.6 %while.185 = (s32[]{:T(128)}, f32[2,8]{1,0:T(2,128)}, f32[2,8,8]{2,1,0:T(8,128)}, s32[2,8]{1,0:T(2,128)S(1)}, s32[8,16384]{1,0:T(8,128)S(1)}, /*index=5*/f32[8]{...) while((s32[]{:T(128)}, f32[2,8]{1,0:T(2,128)}, f32[2,8,8]{2,1,0:T(8,128)}, ...), condition=%wide.region_22.21_spmd, body=%wide.region_20.20_spmd.sunk | while | flops 16252954 | bytes 6820901 | solution.py:99
  382.1 33.6 %all-reduce.5 = (f32[2,9]{1,0:T(2,128)S(1)}, f32[2,9,8]{2,0,1:T(2,128)S(1)}, f32[2,8]{1,0:T(2,128)S(1)}, f32[2,8,8]{2,0,1:T(2,128)S(1)}) all-reduce(f32[2,9]{1,0:T(2,128)} %get-tuple-element.1830, f32[2,9,8]{2,0,1:T(2,128)S(1)} %copy.29, f32[2,8]{1,0:T(2,128)} %get-tuple-element.1833, ...), channel_id=1, replica_groups=mesh['group'=4,'batch'=8] {'batch'}, use_global_device_ids=true, to_apply=%region_6.6 | all-reduce | flops 306 | bytes 2448 | tf_op jit(solution)/shard_map/while/body/eval_jaxpr/psum | solution.py:150
  415.6 17.9 %while.201 = (s32[]{:T(128)}, f32[2,9]{1,0:T(2,128)S(1)}, f32[2,9]{1,0:T(2,128)S(1)}, f32[2,9,8]{2,0,1:T(2,128)S(1)}, s32[]{:T(128)}, /*index=5*/s32[1]{0:T(128)}, s32[]{:T(128)}) while((s32[]{:T(128)}, f32[2,9]{1,0:T(2,128)S(1)}, f32[2,9]{1,0:T(2,128)S(1)}, f32[2,9,8]{2,0,1:T(2,128)S(1)}, s32[]{:T(128)}, /*index=5*/s32[1]{0:T(128)}, ...), condition=%wide.region_11.11_spmd, body=%wide.region_8.10_spmd.sunk | while | flops 73 | bytes 623 | solution.py:65
  433.7 15.7 %while.202 = (s32[]{:T(128)}, f32[2,8]{1,0:T(2,128)S(1)}, f32[2,8]{1,0:T(2,128)S(1)}, f32[2,8,8]{2,0,1:T(2,128)S(1)}, s32[]{:T(128)}, /*index=5*/s32[1]{0:T(128)}, s32[]{:T(128)}) while((s32[]{:T(128)}, f32[2,8]{1,0:T(2,128)S(1)}, f32[2,8]{1,0:T(2,128)S(1)}, f32[2,8,8]{2,0,1:T(2,128)S(1)}, s32[]{:T(128)}, /*index=5*/s32[1]{0:T(128)}, ...), condition=%wide.region_28.28_spmd, body=%wide.region_25.27_spmd.sunk | while | flops 73 | bytes 591 | solution.py:65
  449.4 31.0 %conditional.15 = (f32[2,16384]{1,0:T(2,128)}) conditional(s32[]{:T(128)} %convert_element_type.23, () %tuple.351, (f32[2,16384]{1,0:T(2,128)S(1)}, s32[2,8]{1,0:T(2,128)S(1)}, s32[8,16384]{1,0:T(8,128)S(1)}, f32[8]{0:T(128)S(1)}, f32[2,8]{1,0:T(2,128)S(1)}) %tuple.426), branch_computations={%region_29.29_spmd, %region_30.34_spmd} | conditional | flops 589852 | bytes 4588358 | solution.py:123
  449.4 31.0 %while.188 = (s32[]{:T(128)}, f32[2,16384]{1,0:T(2,128)}, f32[2,16384]{1,0:T(2,128)S(1)}, s32[2,8]{1,0:T(2,128)S(1)}, s32[8,16384]{1,0:T(8,128)S(1)}, /*index=5*...) while((s32[]{:T(128)}, f32[2,16384]{1,0:T(2,128)}, f32[2,16384]{1,0:T(2,128)S(1)}, ...), condition=%wide.region_34.33_spmd, body=%wide.region_31.32_spmd.sunk | while | flops 589852 | bytes 4588262 | solution.py:118
  481.6 77.3 %while.195 = (s32[]{:T(128)}, f32[2,8]{1,0:T(2,128)S(1)}, f32[2,8]{1,0:T(2,128)S(1)}, s32[8,16384]{1,0:T(8,128)}, f32[2,16384]{1,0:T(2,128)S(1)}, /*index=5*/s32...) while((s32[]{:T(128)}, f32[2,8]{1,0:T(2,128)S(1)}, ...), condition=%wide.region_43.44_spmd, body=%wide.region_36.43_spmd.sunk | while | flops 1916958 | bytes 14681779 | solution.py:212
  485.3 16.0 %while.199 = (s32[]{:T(128)}, f32[16384]{0:T(1024)S(1)}, f32[8,16384]{1,0:T(8,128)S(1)}, f32[8,16384]{1,0:T(8,128)S(1)}, f32[8,16384]{1,0:T(8,128)S(1)}, /*index=5*/f32[8]{0:T(128)S(1)}, s32[]{:T(128)}, s32[]{:T(128)}) while((s32[]{:T(128)}, f32[16384]{0:T(1024)S(1)}, f32[8,16384]{1,0:T(8,128)S(1)}, f32[8,16384]{1,0:T(8,128)S(1)}, ...), condition=%wide.region_40.40_spmd, body=%wide.region_39.39_spmd.sunk | while | flops 49154 | bytes 655469 | solution.py:74
  503.7 16.0 %while.200 = (s32[]{:T(128)}, f32[16384]{0:T(1024)S(1)}, f32[8,16384]{1,0:T(8,128)S(1)}, f32[8,16384]{1,0:T(8,128)S(1)}, f32[8,16384]{1,0:T(8,128)S(1)}, /*index=5*/f32[8]{0:T(128)S(1)}, s32[]{:T(128)}, s32[]{:T(128)}) while((s32[]{:T(128)}, f32[16384]{0:T(1024)S(1)}, f32[8,16384]{1,0:T(8,128)S(1)}, f32[8,16384]{1,0:T(8,128)S(1)}, ...), condition=%wide.region_38.38_spmd, body=%wide.region_37.37_spmd.sunk | while | flops 49154 | bytes 655469 | solution.py:74
  523.9 16.0 %while.199 = (s32[]{:T(128)}, f32[16384]{0:T(1024)S(1)}, f32[8,16384]{1,0:T(8,128)S(1)}, f32[8,16384]{1,0:T(8,128)S(1)}, f32[8,16384]{1,0:T(8,128)S(1)}, /*index=5*/f32[8]{0:T(128)S(1)}, s32[]{:T(128)}, s32[]{:T(128)}) while((s32[]{:T(128)}, f32[16384]{0:T(1024)S(1)}, f32[8,16384]{1,0:T(8,128)S(1)}, f32[8,16384]{1,0:T(8,128)S(1)}, ...), condition=%wide.region_40.40_spmd, body=%wide.region_39.39_spmd.sunk | while | flops 49154 | bytes 655469 | solution.py:74
  542.4 16.0 %while.200 = (s32[]{:T(128)}, f32[16384]{0:T(1024)S(1)}, f32[8,16384]{1,0:T(8,128)S(1)}, f32[8,16384]{1,0:T(8,128)S(1)}, f32[8,16384]{1,0:T(8,128)S(1)}, /*index=5*/f32[8]{0:T(128)S(1)}, s32[]{:T(128)}, s32[]{:T(128)}) while((s32[]{:T(128)}, f32[16384]{0:T(1024)S(1)}, f32[8,16384]{1,0:T(8,128)S(1)}, f32[8,16384]{1,0:T(8,128)S(1)}, ...), condition=%wide.region_38.38_spmd, body=%wide.region_37.37_spmd.sunk | while | flops 49154 | bytes 655469 | solution.py:74
  558.9 17.1 %all-reduce.3 = (f32[2,8]{1,0:T(2,128)S(1)}, f32[2,8]{1,0:T(2,128)S(1)}) all-reduce(f32[2,8]{1,0:T(2,128)S(1)} %get-tuple-element.921, f32[2,8]{1,0:T(2,128)S(1)} %get-tuple-element.922), channel_id=1, replica_groups=mesh['group'=4,'batch'=8] {'batch'}, use_global_device_ids=true, to_apply=%region_44.45 | all-reduce | flops 32 | bytes 256 | tf_op jit(solution)/shard_map/psum | solution.py:215
  (1087 shorter events, 361.3 us)
Async XLA Ops:
  1.4 0.7 copy-start.2
  1.4 0.7 copy-start.5
  2.1 4.0 copy-start
  2.1 3.8 collective-permute-start
  4.6 13.5 %collective-permute-start.1 = (f32[2,16384]{1,0:T(2,128)}, f32[2,16384]{1,0:T(2,128)S(1)}, u32[]{:S(2)}, u32[]{:S(2)}) collective-permute-start(f32[2,16384]{1,0:T(2,128)} %get-tuple-element.2214), channel_id=1, source_target_pairs={{8,0},{16,8},{24,16},{9,1},{17,9},{25,17},{10,2},{18,10},{26,18},{... | collective-permute-start | bytes 393224 | tf_op jit(solution)/shard_map/while/body/eval_jaxpr/ppermute | solution.py:16
  121.1 2.9 copy-start
  121.1 2.8 collective-permute-start
  122.6 3.5 collective-permute-start.1
  196.8 34.7 %copy-start = (s32[8,16384]{1,0:T(8,128)S(1)}, s32[8,16384]{1,0:T(8,128)}, u32[]{:S(2)}) copy-start(s32[8,16384]{1,0:T(8,128)} %get-tuple-element.2247) | copy-start | bytes 1572868 | tf_op jit(solution)/shard_map/while
  196.8 34.5 %collective-permute-start = (f32[2,16384]{1,0:T(2,128)}, f32[2,16384]{1,0:T(2,128)S(1)}, u32[]{:S(2)}, u32[]{:S(2)}) collective-permute-start(f32[2,16384]{1,0:T(2,128)} %get-tuple-element.2213), channel_id=1, source_target_pairs={{0,8},{8,16},{16,24},{1,9},{9,17},{17,25},{2,10},{10,18},{18,26},{... | collective-permute-start | bytes 393224 | tf_op jit(solution)/shard_map/while/body/eval_jaxpr/ppermute | solution.py:16
  230.0 19.9 %collective-permute-start.1 = (f32[2,16384]{1,0:T(2,128)}, f32[2,16384]{1,0:T(2,128)S(1)}, u32[]{:S(2)}, u32[]{:S(2)}) collective-permute-start(f32[2,16384]{1,0:T(2,128)} %get-tuple-element.2214), channel_id=1, source_target_pairs={{8,0},{16,8},{24,16},{9,1},{17,9},{25,17},{10,2},{18,10},{26,18},{... | collective-permute-start | bytes 393224 | tf_op jit(solution)/shard_map/while/body/eval_jaxpr/ppermute | solution.py:16
  320.7 43.9 %copy-start = (s32[8,16384]{1,0:T(8,128)S(1)}, s32[8,16384]{1,0:T(8,128)}, u32[]{:S(2)}) copy-start(s32[8,16384]{1,0:T(8,128)} %get-tuple-element.2247) | copy-start | bytes 1572868 | tf_op jit(solution)/shard_map/while
  320.7 43.7 %collective-permute-start = (f32[2,16384]{1,0:T(2,128)}, f32[2,16384]{1,0:T(2,128)S(1)}, u32[]{:S(2)}, u32[]{:S(2)}) collective-permute-start(f32[2,16384]{1,0:T(2,128)} %get-tuple-element.2213), channel_id=1, source_target_pairs={{0,8},{8,16},{16,24},{1,9},{9,17},{17,25},{2,10},{10,18},{18,26},{... | collective-permute-start | bytes 393224 | tf_op jit(solution)/shard_map/while/body/eval_jaxpr/ppermute | solution.py:16
  363.1 3.5 collective-permute-start.1
  481.1 0.5 copy-start.3
  503.7 16.1 %copy-start.1 = (s32[8,16384]{1,0:T(8,128)S(1)}, s32[8,16384]{1,0:T(8,128)}, u32[]{:S(2)}) copy-start(s32[8,16384]{1,0:T(8,128)} %get-tuple-element.2297) | copy-start | bytes 1572868 | tf_op jit(solution)/shard_map/while
  542.4 16.1 %copy-start.1 = (s32[8,16384]{1,0:T(8,128)S(1)}, s32[8,16384]{1,0:T(8,128)}, u32[]{:S(2)}) copy-start(s32[8,16384]{1,0:T(8,128)} %get-tuple-element.2297) | copy-start | bytes 1572868 | tf_op jit(solution)/shard_map/while
  576.6 0.6 copy-start.4
where the time goes:
time: 586 us; the launch traced here: 583 us
  other arithmetic  170 us (29%)
  blocking collectives  162 us (28%)
  local copies, waits for them, and re-layouts  131 us (22%)
  starting transfers between devices  84.7 us (14%)
  waiting for transfers between devices  16.5 us (3%)
  matrix products  13.5 us (2%)
    psum x4, blocking collectives, moment_step(): lax.psum((lead_forward, couple_forward, lead_backward, couple_backward),...  140 us
    another operation x144, other arithmetic  92.7 us
    ppermute x8, starting transfers between devices, from_behind(): return lax.ppermute(x, axis, pairs)  84.7 us
    mul x64, other arithmetic, advance_single(): current = pieces[0] * current + pieces[1] * pieces[2]  45.9 us
    dynamic_slice x64, local copies, waits for them, and re-layouts, advance(): lax.scan(advance_single, entering, (retain, inject, sigmas[:retain.shape[...  39.4 us
    another operation x236, local copies, waits for them, and re-layouts  31 us
    psum x1, blocking collectives, on_device(): numerator, denominator = lax.psum((numerator, denominator), 'batch')  17.1 us
    ppermute x8, waiting for transfers between devices, from_behind(): return lax.ppermute(x, axis, pairs)  16.5 us
  transfers between devices with their start and end apart: 8, of which 1 were waited for; matrix products, arithmetic and copies ran while one was open for 3% of the time, Pallas kernels for 0%

commit v1 on v0

--- a/solution.py
+++ b/solution.py
@@ -1,13 +1,19 @@
+import functools
+import math
+
 import jax
 import jax.numpy as jnp
 from jax import lax
+from jax.experimental import pallas as pl
+from jax.experimental.pallas import tpu as pltpu
 from jax.sharding import PartitionSpec as P
-
-K = 131072
-
 
 MISMATCH = 0.05
 HIGHEST = lax.Precision.HIGHEST
+
+
+def haplotypes(panel_rows):
+    return panel_rows.shape[1] * lax.axis_size("batch")
 
 
 def from_behind(x, axis, by):
@@ -25,7 +31,7 @@
 def forward_terms(panel_rows, geno_col, switches):
     emitted = emission(panel_rows, geno_col)
     retain = emitted * (1.0 - switches)[:, None]
-    inject = emitted * (switches / K)[:, None]
+    inject = emitted * (switches / haplotypes(panel_rows))[:, None]
     return (retain, inject, None)
 
 
@@ -33,7 +39,7 @@
     emitted = emission(panel_rows, geno_col)[::-1]
     flipped = switches[::-1]
     retain = emitted * (1.0 - flipped)[:, None]
-    inject = jnp.broadcast_to((flipped / K)[:, None], emitted.shape)
+    inject = jnp.broadcast_to((flipped / haplotypes(panel_rows))[:, None], emitted.shape)
     return (retain, inject, emitted)
 
 
@@ -78,13 +84,13 @@
     return jnp.where(active, block, store)
 
 
-def on_device(panel_alleles, recomb_rates, genotypes):
+def on_device_chain(panel_alleles, recomb_rates, genotypes):
     chain_size = lax.axis_size("group")
     position = lax.axis_index("group")
     markers, width = panel_alleles.shape
     targets = genotypes.shape[0]
     bundles = targets // targets
-    uniform = jnp.full((targets, width), 1.0 / K, jnp.float32)
+    uniform = jnp.full((targets, width), 1.0 / haplotypes(panel_alleles), jnp.float32)
     first_row = position == 0
     last_row = position == chain_size - 1
 
@@ -216,6 +222,309 @@
     return (numerator / denominator, log_likelihood)
 
 
+ROWS, LANES = 8, 128
+HALF = LANES // 2
+GROUPS = 4
+MISSING = 2
+SCALE = math.sqrt(MISMATCH * (1.0 - MISMATCH))
+HALF_STEP = 0.5 * math.log((1.0 - MISMATCH) / MISMATCH)
+VMEM = pl.BlockSpec(memory_space=pltpu.VMEM)
+SMEM = pl.BlockSpec(memory_space=pltpu.SMEM)
+F32, BF16 = jnp.float32, jnp.bfloat16
+
+
+def iota(shape, axis):
+    return lax.broadcasted_iota(jnp.int32, shape, axis)
+
+
+def pack_kernel(geno_ref, panel_ref, *out_refs):
+    place = lax.axis_index("group")
+    chunk = panel_ref.shape[1] // GROUPS
+    row, lane = iota((ROWS, LANES), 0), iota((ROWS, LANES), 1)
+    tile = jnp.zeros((ROWS, LANES), jnp.int32)
+    for i in range(ROWS):
+        both = jnp.where(lane < HALF, geno_ref[0, i], geno_ref[1, i])
+        tile = jnp.where(row == i, both, tile)
+    for d in range(GROUPS):
+        start = pl.multiple_of((place ^ d) * chunk, LANES)
+        out_refs[d][:, :chunk] = panel_ref[:, pl.ds(start, chunk)]
+        out_refs[d][:, chunk:] = tile
+
+
+def window_kernel(step, rate_ref, *refs):
+    pieces, (t_ref, em_ref, panel, genos, wide, left) = refs[:GROUPS], refs[GROUPS:]
+    place = lax.axis_index("group")
+    columns = panel.shape[1]
+    markers = ROWS * GROUPS
+    for d in range(GROUPS):
+        rows = pl.ds(pl.multiple_of((place ^ d) * ROWS, ROWS), ROWS)
+        panel[rows, :] = pieces[d][:, :columns]
+        genos[rows, :] = pieces[d][:, columns:]
+
+    r, j = iota((4 * markers, 2 * markers), 0), iota((4 * markers, 2 * markers), 1)
+    same = r // (2 * markers) == j // markers
+    prefix, marker = (r // markers) % 2 == 0, r % markers
+    at = j % markers
+    sums = jnp.where(prefix, jnp.where(at <= marker, 1.0, 0.0), jnp.where(at < marker, -1.0, 0.0))
+    sums = jnp.where(same, sums, 0.0).astype(BF16)
+
+    def fill(c, carry):
+        here = pl.ds(pl.multiple_of(c * step, LANES), step)
+        signs = []
+        for h in range(2):
+            for b in range(GROUPS):
+                rows = slice(b * ROWS, (b + 1) * ROWS)
+                seen = genos[rows, h * HALF : h * HALF + 1]
+                agrees = jnp.where(panel[rows, here] == seen, 1.0, -1.0)
+                signs.append(jnp.where(seen == MISSING, 0.0, agrees))
+        signs = jnp.concatenate(signs, axis=0).astype(BF16)
+        power = jnp.dot(sums, signs, preferred_element_type=F32)
+        value = jnp.exp(power * HALF_STEP)
+        upper = value.astype(BF16).astype(F32)
+        lower = value - upper
+        blocks = {}
+        for h in range(2):
+            for kind in range(2):
+                for b in range(GROUPS):
+                    at = h * 2 * markers + kind * markers + b * ROWS
+                    both = jnp.concatenate([upper[at : at + ROWS], lower[at : at + ROWS]], axis=0).astype(BF16)
+                    blocks[kind, h, b] = both
+                    wide[kind, (h * GROUPS + b) * 2 * ROWS : (h * GROUPS + b + 1) * 2 * ROWS, here] = both
+        slot = 0
+        for half, h, t, b in LEFT:
+            carries = jnp.broadcast_to(panel[t : t + 1, here], (2 * ROWS, step)).astype(F32).astype(BF16)
+            left[slot * 2 * ROWS : (slot + 1) * 2 * ROWS, here] = blocks[1 - half, h, b] * carries
+            slot += 1
+        return carry
+
+    lax.fori_loop(0, columns // step, fill, 0)
+
+    def product(a, b):
+        return lax.dot_general(a, b, (((1,), (1,)), ((), ())), preferred_element_type=F32)
+
+    middle = len(LEFT) * ROWS
+    sums_t = [product(left[:middle, :], wide[0]), product(left[middle:, :], wide[1])]
+    sums_e = [product(wide[1], wide[0]), product(wide[0], wide[1])]
+    lane = iota((ROWS, LANES), 1)
+    first = lane % (2 * ROWS) < ROWS
+
+    def rows_of(acc, slot):
+        return acc[slot * 2 * ROWS : slot * 2 * ROWS + ROWS] + acc[slot * 2 * ROWS + ROWS : (slot + 1) * 2 * ROWS]
+
+    def fold(a, b):
+        a = a + pltpu.roll(a, LANES - ROWS, 1)
+        b = 0.0 if b is None else b + pltpu.roll(b, ROWS, 1)
+        return jnp.where(first, a, b)
+
+    def both_targets(acc, slots):
+        return jnp.where(lane < HALF, rows_of(acc, slots[0]), rows_of(acc, slots[1]))
+
+    for t in range(markers):
+        half = t // (markers // 2)
+        tiles = [both_targets(sums_t[half], [LEFT_AT[half, h, t, b] for h in range(2)]) for b in left_blocks(t)]
+        tiles = tiles + [None] * (2 - len(tiles))
+        t_ref[t // ROWS, (t % ROWS) * ROWS : (t % ROWS + 1) * ROWS, :] = fold(*tiles)
+    for kind in range(2):
+        tiles = [both_targets(sums_e[kind], [b, GROUPS + b]) for b in range(GROUPS)]
+        for q in range(GROUPS // 2):
+            at = (kind * GROUPS // 2 + q) * ROWS
+            em_ref[at : at + ROWS, :] = fold(tiles[2 * q], tiles[2 * q + 1])
+    row = iota((ROWS, LANES), 0)
+    rates = jnp.zeros((ROWS, LANES), F32)
+    for i in range(ROWS):
+        rates = jnp.where(row == i, rate_ref[i], rates)
+    own = pl.ds(pl.multiple_of(place * ROWS, ROWS), ROWS)
+    inner = lane % (LANES // GROUPS)
+    known = jnp.where(genos[own, :] == MISSING, 0.0, 1.0)
+    known0 = jnp.broadcast_to(known[:, 0:1], (ROWS, LANES))
+    known1 = jnp.broadcast_to(known[:, HALF : HALF + 1], (ROWS, LANES))
+    misc = jnp.where(inner < 2 * ROWS, rates, jnp.where(inner < 3 * ROWS, known0, known1))
+    em_ref[GROUPS * ROWS :, :] = jnp.where(lane // (LANES // GROUPS) == place, misc, 0.0)
+
+
+def left_blocks(t):
+    b = t // ROWS
+    return list(range(b + 1)) if b < GROUPS // 2 else list(range(GROUPS - 1, b - 1, -1))
+
+
+LEFT = [
+    (half, h, t, b)
+    for half in range(2)
+    for t in range(half * ROWS * GROUPS // 2, (half + 1) * ROWS * GROUPS // 2)
+    for b in left_blocks(t)
+    for h in range(2)
+]
+LEFT_AT = {entry: slot % (len(LEFT) // 2) for slot, entry in enumerate(LEFT)}
+
+
+def finish_kernel(panel_size, copies, t_ref, em_ref, dose_ref, log_ref):
+    place = lax.axis_index("group")
+    markers = ROWS * GROUPS
+    row, lane = iota((ROWS, LANES), 0), iota((ROWS, LANES), 1)
+    target = lane // HALF
+    folded = (lane % (2 * ROWS)) // ROWS
+    misc = em_ref[GROUPS * ROWS :, :] * (1.0 / copies)
+    wide = LANES // GROUPS
+
+    def spread(tile, at):
+        return jnp.broadcast_to(tile[:, at : at + 1], (ROWS, LANES))
+
+    rates = [spread(misc, b * wide) for b in range(GROUPS)]
+    odds = [rate / (1.0 - rate) for rate in rates]
+    inverse = 1.0 / panel_size
+    ahead = []
+    for b in range(GROUPS):
+        following = odds[b + 1][0:1, :] if b + 1 < GROUPS else jnp.ones((1, LANES), F32)
+        ahead.append(jnp.concatenate([odds[b][1:, :], following], axis=0) * inverse)
+    behind = [odd * inverse for odd in odds]
+
+    def scaled(base, factors):
+        tiles = []
+        for q in range(GROUPS // 2):
+            tile = em_ref[base + q * ROWS : base + (q + 1) * ROWS, :]
+            tiles.append(tile * jnp.where(folded == 0, factors[2 * q], factors[2 * q + 1]))
+        return tiles
+
+    lead_tiles = scaled(GROUPS // 2 * ROWS, ahead)
+    trail_tiles = scaled(0, behind)
+
+    def column(tiles, t, b):
+        at = 2 * ROWS * (t // ROWS) + t % ROWS + ROWS * (b % 2)
+        tile = tiles[b // 2]
+        return jnp.where(target == 0, spread(tile, at), spread(tile, HALF + at))
+
+    lead = [jnp.zeros((ROWS, LANES), F32)] * GROUPS
+    trail = [jnp.zeros((ROWS, LANES), F32)] * GROUPS
+    starts = [jnp.zeros((ROWS, LANES), F32)] * GROUPS
+    ends = [jnp.zeros((ROWS, LANES), F32)] * GROUPS
+    v = jnp.ones((ROWS, LANES), F32)
+    z = jnp.ones((ROWS, LANES), F32)
+    for step in range(markers):
+        t, u = step, markers - 1 - step
+        bt, bu = t // ROWS, u // ROWS
+        starts[bt] = jnp.where(row == t % ROWS, v, starts[bt])
+        ends[bu] = jnp.where(row == u % ROWS, z, ends[bu])
+        for b in range(bt, GROUPS):
+            lead[b] = lead[b] + v * column(lead_tiles, t, b)
+        for b in range(bu + 1):
+            trail[b] = trail[b] + z * column(trail_tiles, u, b)
+        v = jnp.broadcast_to(lead[bt][t % ROWS : t % ROWS + 1, :], (ROWS, LANES))
+        z = jnp.broadcast_to(trail[bu][u % ROWS : u % ROWS + 1, :], (ROWS, LANES))
+    total = v
+
+    low = place < GROUPS // 2
+    inner = lane % HALF
+    outer = [jnp.where(low, starts[b], ends[GROUPS - 1 - b]) for b in range(2)]
+    outer = jnp.where(folded == 0, outer[0], outer[1])
+    across = [jnp.where(low, ends[b], starts[b]) for b in range(GROUPS)]
+    picked = across[GROUPS - 1]
+    for b in range(GROUPS - 1):
+        picked = jnp.where(inner // (2 * ROWS) == b, across[b], picked)
+    picked = jnp.where(row == lane % ROWS, picked, 0.0)
+    across = jnp.sum(picked, axis=0, keepdims=True)
+    weight = outer * across
+    block = jnp.where(low, folded, GROUPS - 1 - folded)
+    side = jnp.where(low, 1, -1)
+    near = block * ROWS + row
+    far = ROWS * (inner // (2 * ROWS)) + lane % ROWS
+    parts = []
+    for i in range(ROWS):
+        t = place * ROWS + i
+        inside = ((near - t) * side <= 0) & ((far - t) * side >= 0)
+        tile = jnp.where(inside, t_ref[i * ROWS : (i + 1) * ROWS, :] * weight, 0.0)
+        parts.append(jnp.sum(tile, axis=0, keepdims=True))
+    parts = jnp.concatenate(parts, axis=0) * (inverse / total)
+    doses, logs = [], []
+    counts = jnp.sum(misc, axis=0, keepdims=True)
+    stay = [jnp.log(1.0 - rate) for rate in rates]
+    stay[0] = jnp.where(row == 0, 0.0, stay[0])
+    stay = jnp.sum(sum(stay), axis=0, keepdims=True)
+    for h in range(2):
+        dose = jnp.sum(jnp.where(target == h, parts, 0.0), axis=1, keepdims=True)
+        doses.append(jnp.sum(jnp.where(row == lane, dose, 0.0), axis=0, keepdims=True))
+        seen = sum(counts[:, b * wide + (2 + h) * ROWS : b * wide + (2 + h) * ROWS + 1] for b in range(GROUPS))
+        whole = jnp.log(total[0:1, h * HALF : h * HALF + 1]) + stay[:, 0:1] + seen * math.log(SCALE)
+        logs.append(whole * (1.0 / markers))
+    dose_ref[...] = jnp.concatenate(doses, axis=0)[:, :ROWS]
+    log_ref[...] = jnp.concatenate(logs, axis=0)
+
+
+def exchange(x, axis, by):
+    peers = lax.axis_size(axis)
+    return lax.ppermute(x, axis, [(i, i ^ by) for i in range(peers)])
+
+
+def on_device_windows(panel_alleles, recomb_rates, genotypes):
+    width = panel_alleles.shape[1]
+    copies = lax.axis_size("batch")
+    chunk = width // GROUPS
+    markers = ROWS * GROUPS
+    cut = jax.ShapeDtypeStruct((ROWS, chunk + LANES), jnp.int32)
+    pieces = pl.pallas_call(
+        pack_kernel, out_shape=[cut] * GROUPS, in_specs=[SMEM, VMEM], out_specs=[VMEM] * GROUPS, name="pack"
+    )(genotypes, panel_alleles)
+    pieces = [pieces[0]] + [exchange(pieces[d], "group", d) for d in range(1, GROUPS)]
+    extra = (GROUPS + 1) * ROWS
+    sums_t, sums_e = pl.pallas_call(
+        functools.partial(window_kernel, min(512, chunk)),
+        out_shape=[
+            jax.ShapeDtypeStruct((GROUPS, ROWS * ROWS, LANES), F32),
+            jax.ShapeDtypeStruct((extra, LANES), F32),
+        ],
+        in_specs=[SMEM] + [VMEM] * GROUPS,
+        out_specs=[VMEM] * 2,
+        scratch_shapes=[
+            pltpu.VMEM((markers, chunk), jnp.int32),
+            pltpu.VMEM((markers, LANES), jnp.int32),
+            pltpu.VMEM((2, 4 * markers, chunk), BF16),
+            pltpu.VMEM((len(LEFT) * 2 * ROWS, chunk), BF16),
+        ],
+        compiler_params=pltpu.CompilerParams(vmem_limit_bytes=48 * 1024 * 1024),
+        name="windows",
+    )(recomb_rates, *pieces)
+    place = lax.axis_index("group")
+    tall = ROWS * ROWS
+
+    def block(index):
+        return lax.dynamic_index_in_dim(sums_t, index, 0, False)
+
+    kept = jnp.concatenate([block(place), sums_e, block(place ^ 2)], axis=0)
+    sent = jnp.concatenate([block(place ^ 1), sums_e, block(place ^ 3)], axis=0)
+    kept = kept + exchange(sent, "group", 1)
+    got = exchange(kept[tall:], "group", 2)
+    kept = kept[: tall + extra] + jnp.concatenate([got[extra:], got[:extra]], axis=0)
+    by = 1
+    while by < copies:
+        kept = kept + exchange(kept, "batch", by)
+        by *= 2
+    dosage, logs = pl.pallas_call(
+        functools.partial(finish_kernel, float(width * copies), float(copies)),
+        out_shape=[jax.ShapeDtypeStruct((2, ROWS), F32), jax.ShapeDtypeStruct((2, 1), F32)],
+        in_specs=[VMEM] * 2,
+        out_specs=[VMEM] * 2,
+        name="finish",
+    )(kept[:tall], kept[tall:])
+    return dosage, logs.reshape(2)
+
+
+def fits_windows(panel_alleles, genotypes, groups, copies):
+    markers, width = panel_alleles.shape
+    return (
+        groups == GROUPS
+        and copies & (copies - 1) == 0
+        and markers == ROWS
+        and genotypes.shape[0] == 2
+        and width % (GROUPS * LANES * 4) == 0
+    )
+
+
+def on_device(panel_alleles, recomb_rates, genotypes):
+    groups, copies = lax.axis_size("group"), lax.axis_size("batch")
+    if fits_windows(panel_alleles, genotypes, groups, copies):
+        return on_device_windows(panel_alleles, recomb_rates, genotypes)
+    return on_device_chain(panel_alleles, recomb_rates, genotypes)
+
+
 def solution(mesh):
     placed = (P("group", "batch"), P("group"), P(None, "group"))
     return jax.shard_map(

time: 586 us -> 46.8 us (0.08)
  other arithmetic: 170 us -> 0.68 us
  blocking collectives: 162 us -> 0 us
  local copies, waits for them, and re-layouts: 131 us -> 2.84 us
  starting transfers between devices: 84.7 us -> 11.3 us
  matrix products: 13.5 us -> 0 us
  Pallas kernels: 0 us -> 13 us
    psum x6 -> x0, blocking collectives: 162 us -> none  [the longest x4 140 us: moment_step(): lax.psum((lead_forward, couple_forward, lead_backward, couple_backward),...]
    another operation x148 -> x0, other arithmetic: 94.5 us -> none
    ppermute x8, starting transfers between devices: 84.7 us -> 11.3 us  [exchange(): return lax.ppermute(x, axis, [(i, i ^ by) for i in range(peers)])]
    mul x76 -> x0, other arithmetic: 49.5 us -> none  [the longest x64 45.9 us: advance_single(): current = pieces[0] * current + pieces[1] * pieces[2]]
    dynamic_slice x78 -> x0, local copies, waits for them, and re-layouts: 40 us -> none  [the longest x64 39.4 us: advance(): lax.scan(advance_single, entering, (retain, inject, sigmas[:retain.shape[...]
    another operation x236 -> x0, local copies, waits for them, and re-layouts: 31 us -> none
    dynamic_update_slice x44 -> x0, local copies, waits for them, and re-layouts: 28.5 us -> none  [the longest x32 15.8 us: advance(): lax.scan(advance_single, entering, (retain, inject, sigmas[:retain.shape[...]
    rev x14 -> x0, local copies, waits for them, and re-layouts: 16 us -> none  [the longest x6 11.5 us: backward_terms(): emitted = emission(panel_rows, geno_col)[::-1]]
  transfers between devices with their start and end apart: 8 -> 8, of which waited for: 1 -> 7; matrix products, arithmetic and copies ran while one was open for 3% -> 0% of each run, Pallas kernels for 0% -> 0%
where the time goes in v1:
time: 46.8 us; the launch traced here: 46.5 us
  waiting for transfers between devices  18 us (38%)
  Pallas kernels  13 us (28%)
  starting transfers between devices  11.3 us (24%)
  local copies, waits for them, and re-layouts  2.84 us (6%)
  other arithmetic  0.68 us (1%)
  between operations  0.68 us (1%)
    ppermute x8, waiting for transfers between devices, exchange(): return lax.ppermute(x, axis, [(i, i ^ by) for i in range(peers)])  18 us
    ppermute x8, starting transfers between devices, exchange(): return lax.ppermute(x, axis, [(i, i ^ by) for i in range(peers)])  11.3 us
    pallas_call x1, Pallas kernels, on_device_windows(): pl.pallas_call(functools.partial(window_kernel, min(512, chunk)), out_sha...  8.94 us
    pallas_call x1, Pallas kernels, on_device_windows(): pl.pallas_call(functools.partial(finish_kernel, float(width * copies), fl...  2.18 us
    pallas_call x1, Pallas kernels, on_device_windows(): pl.pallas_call(pack_kernel, out_shape=[cut] * GROUPS, in_specs=[SMEM, VME...  1.88 us
    unnamed x6, local copies, waits for them, and re-layouts  1.58 us
  transfers between devices with their start and end apart: 8, of which 7 were waited for; matrix products, arithmetic and copies ran while one was open for 0% of the time, Pallas kernels for 0%

profile of v1, /device:TPU:0, one launch (start us, length us, event | category | flops | bytes accessed | tf_op | source)
XLA Modules:
  0.0 46.5 jit_solution(17718508701113311218)
XLA Ops:
  0.6 1.9 %pack.1 = (s32[8,4224]{1,0:T(8,128)}, s32[8,4224]{1,0:T(8,128)}, s32[8,4224]{1,0:T(8,128)}, s32[8,4224]{1,0:T(8,128)}) custom-call(s32[2,8]{1,0:T(2,128)} %geno_ref.1, s32[8,16384]{1,0:T(8,128)} %panel_ref.1), custom_call_target="tpu_custom_call" | custom-call | tf_op jit(solution)/shard_map/pack/pallas_call | solution.py:463
  2.5 0.5 collective-permute-start
  3.0 2.5 %collective-permute-start.1 = (s32[8,4224]{1,0:T(8,128)}, s32[8,4224]{1,0:T(8,128)S(1)}, u32[]{:S(2)}, u32[]{:S(2)}) collective-permute-start(s32[8,4224]{1,0:T(8,128)} %get-tuple-element.12), channel_id=1, source_target_pairs={{0,16},{8,24},{16,0},{24,8},{1,17},{9,25},{17,1},{25,9},{2,18},{10... | collective-permute-start | bytes 405512 | tf_op jit(solution)/shard_map/ppermute | solution.py:454
  5.5 0.1 collective-permute-start.2
  5.6 0.0 copy-start.1
  5.6 0.0 collective-permute-done.refs_1_
  5.6 4.5 %collective-permute-done.1.refs_2_ = s32[8,4224]{1,0:T(8,128)S(1)} collective-permute-done((s32[8,4224]{1,0:T(8,128)}, s32[8,4224]{1,0:T(8,128)S(1)}, u32[]{:S(2)}, u32[]{:S(2)}) %collective-permute-start.1) | collective-permute-done | bytes 135200 | tf_op jit(solution)/shard_map/ppermute | solution.py:454
  10.1 2.5 %collective-permute-done.2.refs_3_ = s32[8,4224]{1,0:T(8,128)S(1)} collective-permute-done((s32[8,4224]{1,0:T(8,128)}, s32[8,4224]{1,0:T(8,128)S(1)}, u32[]{:S(2)}, u32[]{:S(2)}) %collective-permute-start.2) | collective-permute-done | bytes 135200 | tf_op jit(solution)/shard_map/ppermute | solution.py:454
  12.6 0.0 copy-done.1
  12.6 0.0 copy-start
  12.6 0.9 %copy-done = s32[8,4224]{1,0:T(8,128)S(1)} copy-done((s32[8,4224]{1,0:T(8,128)S(1)}, s32[8,4224]{1,0:T(8,128)}, u32[]{:S(2)}) %copy-start) | copy-done | bytes 135192
  13.5 8.9 %windows.1 = (f32[4,64,128]{2,1,0:T(8,128)S(1)}, f32[40,128]{1,0:T(8,128)S(1)}) custom-call(f32[8]{0:T(128)S(1)} %copy-done.1, s32[8,4224]{1,0:T(8,128)S(1)} %copy-done, s32[8,4224]{1,0:T(8,128)S(1)} %collective-permute-done.refs_1_, s32[8,4224]{1,0:T(8,128)S(1)} %collective-permute-done.1.refs_2_, s32[8,4224]{1,0:T(8,128)S(1)} %collective-permute-done.2.refs_3_), custom_call_target="tpu_custom_call" | custom-call | tf_op jit(solution)/shard_map/windows/pallas_call | solution.py:468
  22.5 0.2 collective-permute-start.3
  22.7 1.2 %collective-permute-done.3 = f32[168,128]{1,0:T(8,128)S(1)} collective-permute-done((f32[168,128]{1,0:T(8,128)S(1)}, f32[168,128]{1,0:T(8,128)S(1)}, u32[]{:S(2)}, u32[]{:S(2)}) %collective-permute-start.3) | collective-permute-done | bytes 86048 | tf_op jit(solution)/shard_map/ppermute | solution.py:454
  23.9 1.6 %collective-permute-start.4 = (f32[104,128]{1,0:T(8,128)S(1)}, f32[104,128]{1,0:T(8,128)S(1)}, u32[]{:S(2)}, u32[]{:S(2)}) collective-permute-start(f32[104,128]{1,0:T(8,128)S(1)} %slice.25), channel_id=1, source_target_pairs={{0,16},{8,24},{16,0},{24,8},{1,17},{9,25},{17,1},{25,9},{2,18},{10... | collective-permute-start | bytes 159752 | tf_op jit(solution)/shard_map/ppermute | solution.py:454
  25.5 2.6 %collective-permute-done.4 = f32[104,128]{1,0:T(8,128)S(1)} collective-permute-done((f32[104,128]{1,0:T(8,128)S(1)}, f32[104,128]{1,0:T(8,128)S(1)}, u32[]{:S(2)}, u32[]{:S(2)}) %collective-permute-start.4) | collective-permute-done | bytes 53280 | tf_op jit(solution)/shard_map/ppermute | solution.py:454
  28.1 1.6 %collective-permute-start.5 = (f32[104,128]{1,0:T(8,128)S(1)}, f32[104,128]{1,0:T(8,128)S(1)}, u32[]{:S(2)}, u32[]{:S(2)}) collective-permute-start(f32[104,128]{1,0:T(8,128)S(1)} %slice_add_fusion), channel_id=1, source_target_pairs={{0,1},{1,0},{2,3},{3,2},{4,5},{5,4},{6,7},{7,6},{8,9},{9,8},{10,11... | collective-permute-start | bytes 159752 | tf_op jit(solution)/shard_map/ppermute | solution.py:454
  29.8 2.6 %collective-permute-done.5 = f32[104,128]{1,0:T(8,128)S(1)} collective-permute-done((f32[104,128]{1,0:T(8,128)S(1)}, f32[104,128]{1,0:T(8,128)S(1)}, u32[]{:S(2)}, u32[]{:S(2)}) %collective-permute-start.5) | collective-permute-done | bytes 53280 | tf_op jit(solution)/shard_map/ppermute | solution.py:454
  32.3 1.7 %collective-permute-start.6 = (f32[104,128]{1,0:T(8,128)S(1)}, f32[104,128]{1,0:T(8,128)S(1)}, u32[]{:S(2)}, u32[]{:S(2)}) collective-permute-start(f32[104,128]{1,0:T(8,128)S(1)} %add.34), channel_id=1, source_target_pairs={{0,2},{1,3},{2,0},{3,1},{4,6},{5,7},{6,4},{7,5},{8,10},{9,11},{10,... | collective-permute-start | bytes 159752 | tf_op jit(solution)/shard_map/ppermute | solution.py:454
  34.0 2.5 %collective-permute-done.6 = f32[104,128]{1,0:T(8,128)S(1)} collective-permute-done((f32[104,128]{1,0:T(8,128)S(1)}, f32[104,128]{1,0:T(8,128)S(1)}, u32[]{:S(2)}, u32[]{:S(2)}) %collective-permute-start.6) | collective-permute-done | bytes 53280 | tf_op jit(solution)/shard_map/ppermute | solution.py:454
  36.5 3.2 %collective-permute-start.7 = (f32[104,128]{1,0:T(8,128)S(1)}, f32[104,128]{1,0:T(8,128)S(1)}, u32[]{:S(2)}, u32[]{:S(2)}) collective-permute-start(f32[104,128]{1,0:T(8,128)S(1)} %add.35), channel_id=1, source_target_pairs={{0,4},{1,5},{2,6},{3,7},{4,0},{5,1},{6,2},{7,3},{8,12},{9,13},{10,... | collective-permute-start | bytes 159752 | tf_op jit(solution)/shard_map/ppermute | solution.py:454
  39.7 2.1 %collective-permute-done.7 = f32[104,128]{1,0:T(8,128)S(1)} collective-permute-done((f32[104,128]{1,0:T(8,128)S(1)}, f32[104,128]{1,0:T(8,128)S(1)}, u32[]{:S(2)}, u32[]{:S(2)}) %collective-permute-start.7) | collective-permute-done | bytes 53280 | tf_op jit(solution)/shard_map/ppermute | solution.py:454
  41.8 0.6 %slice.28.t_ref = f32[64,128]{1,0:T(8,128)} slice(f32[104,128]{1,0:T(8,128)S(1)} %add.36), slice={[0:64], [0:128]} | slice | bytes 65536 | tf_op jit(solution)/shard_map/slice | solution.py:506
  42.4 0.6 %slice.29.em_ref = f32[40,128]{1,0:T(8,128)} slice(f32[104,128]{1,0:T(8,128)S(1)} %add.36), slice={[64:104], [0:128]} | slice | bytes 40960 | tf_op jit(solution)/shard_map/slice | solution.py:506
  43.1 2.2 %finish.1 = (f32[2,8]{1,0:T(2,128)}, f32[2,1]{1,0:T(2,128)}) custom-call(f32[64,128]{1,0:T(8,128)} %slice.28.t_ref, f32[40,128]{1,0:T(8,128)} %slice.29.em_ref), custom_call_target="tpu_custom_call" | custom-call | tf_op jit(solution)/shard_map/finish/pallas_call | solution.py:500
  45.2 0.0 copy-start.2
  45.2 0.7 %copy-done.2 = f32[2,1]{1,0:T(2,128)S(1)} copy-done((f32[2,1]{1,0:T(2,128)S(1)}, f32[2,1]{1,0:T(2,128)}, u32[]{:S(2)}) %copy-start.2) | copy-done | bytes 32
  45.9 0.6 %reduce = f32[2]{0:T(128)} reduce(f32[2,1]{1,0:T(2,128)S(1)} %copy-done.2, f32[]{:T(128)} %constant.23), dimensions={1}, to_apply=%get-tuple-element.17.reduce_sub_computation | reduce | bytes 20 | tf_op jit(solution)/shard_map/finish/pallas_call | solution.py:500
  (10 shorter events, 0.1 us)
Async XLA Ops:
  2.5 3.1 %collective-permute-start = (s32[8,4224]{1,0:T(8,128)}, s32[8,4224]{1,0:T(8,128)S(1)}, u32[]{:S(2)}, u32[]{:S(2)}) collective-permute-start(s32[8,4224]{1,0:T(8,128)} %get-tuple-element.11), channel_id=1, source_target_pairs={{0,8},{8,0},{16,24},{24,16},{1,9},{9,1},{17,25},{25,17},{2,10},{10... | collective-permute-start | bytes 405512 | tf_op jit(solution)/shard_map/ppermute | solution.py:454
  3.0 7.1 %collective-permute-start.1 = (s32[8,4224]{1,0:T(8,128)}, s32[8,4224]{1,0:T(8,128)S(1)}, u32[]{:S(2)}, u32[]{:S(2)}) collective-permute-start(s32[8,4224]{1,0:T(8,128)} %get-tuple-element.12), channel_id=1, source_target_pairs={{0,16},{8,24},{16,0},{24,8},{1,17},{9,25},{17,1},{25,9},{2,18},{10... | collective-permute-start | bytes 405512 | tf_op jit(solution)/shard_map/ppermute | solution.py:454
  5.5 7.2 %collective-permute-start.2 = (s32[8,4224]{1,0:T(8,128)}, s32[8,4224]{1,0:T(8,128)S(1)}, u32[]{:S(2)}, u32[]{:S(2)}) collective-permute-start(s32[8,4224]{1,0:T(8,128)} %get-tuple-element.13), channel_id=1, source_target_pairs={{0,24},{8,16},{16,8},{24,0},{1,25},{9,17},{17,9},{25,1},{2,26},{10... | collective-permute-start | bytes 405512 | tf_op jit(solution)/shard_map/ppermute | solution.py:454
  5.6 7.0 %copy-start.1 = (f32[8]{0:T(128)S(1)}, f32[8]{0:T(128)}, u32[]{:S(2)}) copy-start(f32[8]{0:T(128)} %rate_ref.1) | copy-start | bytes 100
  12.6 0.9 %copy-start = (s32[8,4224]{1,0:T(8,128)S(1)}, s32[8,4224]{1,0:T(8,128)}, u32[]{:S(2)}) copy-start(s32[8,4224]{1,0:T(8,128)} %get-tuple-element.10.refs_0_) | copy-start | bytes 405508
  22.5 1.3 %collective-permute-start.3 = (f32[168,128]{1,0:T(8,128)S(1)}, f32[168,128]{1,0:T(8,128)S(1)}, u32[]{:S(2)}, u32[]{:S(2)}) collective-permute-start(f32[168,128]{1,0:T(8,128)S(1)} %fusion.2), channel_id=1, source_target_pairs={{0,8},{8,0},{16,24},{24,16},{1,9},{9,1},{17,25},{25,17},{2,10},{10... | collective-permute-start | bytes 258056 | tf_op jit(solution)/shard_map/ppermute | solution.py:454
  23.9 4.2 %collective-permute-start.4 = (f32[104,128]{1,0:T(8,128)S(1)}, f32[104,128]{1,0:T(8,128)S(1)}, u32[]{:S(2)}, u32[]{:S(2)}) collective-permute-start(f32[104,128]{1,0:T(8,128)S(1)} %slice.25), channel_id=1, source_target_pairs={{0,16},{8,24},{16,0},{24,8},{1,17},{9,25},{17,1},{25,9},{2,18},{10... | collective-permute-start | bytes 159752 | tf_op jit(solution)/shard_map/ppermute | solution.py:454
  28.1 4.2 %collective-permute-start.5 = (f32[104,128]{1,0:T(8,128)S(1)}, f32[104,128]{1,0:T(8,128)S(1)}, u32[]{:S(2)}, u32[]{:S(2)}) collective-permute-start(f32[104,128]{1,0:T(8,128)S(1)} %slice_add_fusion), channel_id=1, source_target_pairs={{0,1},{1,0},{2,3},{3,2},{4,5},{5,4},{6,7},{7,6},{8,9},{9,8},{10,11... | collective-permute-start | bytes 159752 | tf_op jit(solution)/shard_map/ppermute | solution.py:454
  32.3 4.2 %collective-permute-start.6 = (f32[104,128]{1,0:T(8,128)S(1)}, f32[104,128]{1,0:T(8,128)S(1)}, u32[]{:S(2)}, u32[]{:S(2)}) collective-permute-start(f32[104,128]{1,0:T(8,128)S(1)} %add.34), channel_id=1, source_target_pairs={{0,2},{1,3},{2,0},{3,1},{4,6},{5,7},{6,4},{7,5},{8,10},{9,11},{10,... | collective-permute-start | bytes 159752 | tf_op jit(solution)/shard_map/ppermute | solution.py:454
  36.5 5.3 %collective-permute-start.7 = (f32[104,128]{1,0:T(8,128)S(1)}, f32[104,128]{1,0:T(8,128)S(1)}, u32[]{:S(2)}, u32[]{:S(2)}) collective-permute-start(f32[104,128]{1,0:T(8,128)S(1)} %add.35), channel_id=1, source_target_pairs={{0,4},{1,5},{2,6},{3,7},{4,0},{5,1},{6,2},{7,3},{8,12},{9,13},{10,... | collective-permute-start | bytes 159752 | tf_op jit(solution)/shard_map/ppermute | solution.py:454
  45.2 0.7 %copy-start.2 = (f32[2,1]{1,0:T(2,128)S(1)}, f32[2,1]{1,0:T(2,128)}, u32[]{:S(2)}) copy-start(f32[2,1]{1,0:T(2,128)} %get-tuple-element.17) | copy-start | bytes 28

commit v2 on v1

--- a/solution.py
+++ b/solution.py
@@ -237,39 +237,42 @@
     return lax.broadcasted_iota(jnp.int32, shape, axis)
 
 
-def pack_kernel(geno_ref, panel_ref, *out_refs):
-    place = lax.axis_index("group")
-    chunk = panel_ref.shape[1] // GROUPS
-    row, lane = iota((ROWS, LANES), 0), iota((ROWS, LANES), 1)
-    tile = jnp.zeros((ROWS, LANES), jnp.int32)
-    for i in range(ROWS):
-        both = jnp.where(lane < HALF, geno_ref[0, i], geno_ref[1, i])
-        tile = jnp.where(row == i, both, tile)
-    for d in range(GROUPS):
-        start = pl.multiple_of((place ^ d) * chunk, LANES)
-        out_refs[d][:, :chunk] = panel_ref[:, pl.ds(start, chunk)]
-        out_refs[d][:, chunk:] = tile
+def left_blocks(t):
+    b = t // ROWS
+    return list(range(b + 1)) if b < GROUPS // 2 else list(range(GROUPS - 1, b - 1, -1))
+
+
+MARKERS = ROWS * GROUPS
+HALF_T = MARKERS // 2
+LEFT = [
+    [(h, t, b) for t in range(half * HALF_T, (half + 1) * HALF_T) for b in left_blocks(t) for h in range(2)]
+    for half in range(2)
+]
+LEFT_AT = [{entry: slot for slot, entry in enumerate(LEFT[half])} for half in range(2)]
+TALL = len(LEFT[0]) // 4 * ROWS
+SHORT_TALL = ROWS // 2 * ROWS
+EXTRA = (GROUPS // 2 + 1) * ROWS
 
 
 def window_kernel(step, rate_ref, *refs):
-    pieces, (t_ref, em_ref, panel, genos, wide, left) = refs[:GROUPS], refs[GROUPS:]
+    pieces, geno_refs = refs[:GROUPS], refs[GROUPS : 2 * GROUPS]
+    t_ref, em_ref, panel, genos, wide, left = refs[2 * GROUPS :]
     place = lax.axis_index("group")
     columns = panel.shape[1]
-    markers = ROWS * GROUPS
     for d in range(GROUPS):
         rows = pl.ds(pl.multiple_of((place ^ d) * ROWS, ROWS), ROWS)
-        panel[rows, :] = pieces[d][:, :columns]
-        genos[rows, :] = pieces[d][:, columns:]
-
-    r, j = iota((4 * markers, 2 * markers), 0), iota((4 * markers, 2 * markers), 1)
-    same = r // (2 * markers) == j // markers
-    prefix, marker = (r // markers) % 2 == 0, r % markers
-    at = j % markers
+        panel[rows, :] = pieces[d][...]
+        genos[rows, :] = geno_refs[d][...]
+
+    r, j = iota((4 * MARKERS, 2 * MARKERS), 0), iota((4 * MARKERS, 2 * MARKERS), 1)
+    same = r // (2 * MARKERS) == j // MARKERS
+    prefix, marker = (r // MARKERS) % 2 == 0, r % MARKERS
+    at = j % MARKERS
     sums = jnp.where(prefix, jnp.where(at <= marker, 1.0, 0.0), jnp.where(at < marker, -1.0, 0.0))
     sums = jnp.where(same, sums, 0.0).astype(BF16)
 
-    def fill(c, carry):
-        here = pl.ds(pl.multiple_of(c * step, LANES), step)
+    for start in range(0, columns, step):
+        here = slice(start, start + step)
         signs = []
         for h in range(2):
             for b in range(GROUPS):
@@ -286,25 +289,18 @@
         for h in range(2):
             for kind in range(2):
                 for b in range(GROUPS):
-                    at = h * 2 * markers + kind * markers + b * ROWS
+                    at = h * 2 * MARKERS + kind * MARKERS + b * ROWS
                     both = jnp.concatenate([upper[at : at + ROWS], lower[at : at + ROWS]], axis=0).astype(BF16)
                     blocks[kind, h, b] = both
                     wide[kind, (h * GROUPS + b) * 2 * ROWS : (h * GROUPS + b + 1) * 2 * ROWS, here] = both
-        slot = 0
-        for half, h, t, b in LEFT:
-            carries = jnp.broadcast_to(panel[t : t + 1, here], (2 * ROWS, step)).astype(F32).astype(BF16)
-            left[slot * 2 * ROWS : (slot + 1) * 2 * ROWS, here] = blocks[1 - half, h, b] * carries
-            slot += 1
-        return carry
-
-    lax.fori_loop(0, columns // step, fill, 0)
+        for half in range(2):
+            for slot, (h, t, b) in enumerate(LEFT[half]):
+                carries = jnp.broadcast_to(panel[t : t + 1, here], (2 * ROWS, step)).astype(F32).astype(BF16)
+                left[half, slot * 2 * ROWS : (slot + 1) * 2 * ROWS, here] = blocks[1 - half, h, b] * carries
 
     def product(a, b):
         return lax.dot_general(a, b, (((1,), (1,)), ((), ())), preferred_element_type=F32)
 
-    middle = len(LEFT) * ROWS
-    sums_t = [product(left[:middle, :], wide[0]), product(left[middle:, :], wide[1])]
-    sums_e = [product(wide[1], wide[0]), product(wide[0], wide[1])]
     lane = iota((ROWS, LANES), 1)
     first = lane % (2 * ROWS) < ROWS
 
@@ -312,23 +308,26 @@
         return acc[slot * 2 * ROWS : slot * 2 * ROWS + ROWS] + acc[slot * 2 * ROWS + ROWS : (slot + 1) * 2 * ROWS]
 
     def fold(a, b):
-        a = a + pltpu.roll(a, LANES - ROWS, 1)
-        b = 0.0 if b is None else b + pltpu.roll(b, ROWS, 1)
-        return jnp.where(first, a, b)
+        return jnp.where(first, a + pltpu.roll(a, LANES - ROWS, 1), b + pltpu.roll(b, ROWS, 1))
 
     def both_targets(acc, slots):
         return jnp.where(lane < HALF, rows_of(acc, slots[0]), rows_of(acc, slots[1]))
 
-    for t in range(markers):
-        half = t // (markers // 2)
-        tiles = [both_targets(sums_t[half], [LEFT_AT[half, h, t, b] for h in range(2)]) for b in left_blocks(t)]
-        tiles = tiles + [None] * (2 - len(tiles))
-        t_ref[t // ROWS, (t % ROWS) * ROWS : (t % ROWS + 1) * ROWS, :] = fold(*tiles)
-    for kind in range(2):
-        tiles = [both_targets(sums_e[kind], [b, GROUPS + b]) for b in range(GROUPS)]
-        for q in range(GROUPS // 2):
-            at = (kind * GROUPS // 2 + q) * ROWS
-            em_ref[at : at + ROWS, :] = fold(tiles[2 * q], tiles[2 * q + 1])
+    for half in range(2):
+        sums_t = product(left[half], wide[half])
+        tiles = {
+            (t, b): both_targets(sums_t, [LEFT_AT[half][h, t, b] for h in range(2)]) for h, t, b in LEFT[half] if h == 0
+        }
+        short, long = near_markers(half)
+        pairs = [((short[2 * q], 0), (short[2 * q + 1], 0)) for q in range(ROWS // 2)]
+        pairs += [((t, 0), (t, 1)) for t in long]
+        for q, pair in enumerate(pairs):
+            a, b = (tiles[t, left_blocks(t)[depth]] for t, depth in pair)
+            t_ref[half, q * ROWS : (q + 1) * ROWS, :] = fold(a, b)
+    sums_e = product(wide[1], wide[0])
+    tiles = [both_targets(sums_e, [b, GROUPS + b]) for b in range(GROUPS)]
+    for q in range(GROUPS // 2):
+        em_ref[q * ROWS : (q + 1) * ROWS, :] = fold(tiles[2 * q], tiles[2 * q + 1])
     row = iota((ROWS, LANES), 0)
     rates = jnp.zeros((ROWS, LANES), F32)
     for i in range(ROWS):
@@ -339,31 +338,20 @@
     known0 = jnp.broadcast_to(known[:, 0:1], (ROWS, LANES))
     known1 = jnp.broadcast_to(known[:, HALF : HALF + 1], (ROWS, LANES))
     misc = jnp.where(inner < 2 * ROWS, rates, jnp.where(inner < 3 * ROWS, known0, known1))
-    em_ref[GROUPS * ROWS :, :] = jnp.where(lane // (LANES // GROUPS) == place, misc, 0.0)
-
-
-def left_blocks(t):
-    b = t // ROWS
-    return list(range(b + 1)) if b < GROUPS // 2 else list(range(GROUPS - 1, b - 1, -1))
-
-
-LEFT = [
-    (half, h, t, b)
-    for half in range(2)
-    for t in range(half * ROWS * GROUPS // 2, (half + 1) * ROWS * GROUPS // 2)
-    for b in left_blocks(t)
-    for h in range(2)
-]
-LEFT_AT = {entry: slot % (len(LEFT) // 2) for slot, entry in enumerate(LEFT)}
-
-
-def finish_kernel(panel_size, copies, t_ref, em_ref, dose_ref, log_ref):
+    em_ref[GROUPS // 2 * ROWS :, :] = jnp.where(lane // (LANES // GROUPS) == place, misc, 0.0)
+
+
+def near_markers(half):
+    outer, inner = (0, 1) if half == 0 else (GROUPS - 1, GROUPS - 2)
+    return [outer * ROWS + i for i in range(ROWS)], [inner * ROWS + i for i in range(ROWS)]
+
+
+def finish_kernel(panel_size, copies, sum_ref, dose_ref, log_ref):
     place = lax.axis_index("group")
-    markers = ROWS * GROUPS
     row, lane = iota((ROWS, LANES), 0), iota((ROWS, LANES), 1)
     target = lane // HALF
     folded = (lane % (2 * ROWS)) // ROWS
-    misc = em_ref[GROUPS * ROWS :, :] * (1.0 / copies)
+    misc = sum_ref[TALL + GROUPS // 2 * ROWS :, :] * (1.0 / copies)
     wide = LANES // GROUPS
 
     def spread(tile, at):
@@ -378,132 +366,165 @@
         ahead.append(jnp.concatenate([odds[b][1:, :], following], axis=0) * inverse)
     behind = [odd * inverse for odd in odds]
 
-    def scaled(base, factors):
-        tiles = []
-        for q in range(GROUPS // 2):
-            tile = em_ref[base + q * ROWS : base + (q + 1) * ROWS, :]
-            tiles.append(tile * jnp.where(folded == 0, factors[2 * q], factors[2 * q + 1]))
-        return tiles
-
-    lead_tiles = scaled(GROUPS // 2 * ROWS, ahead)
-    trail_tiles = scaled(0, behind)
-
-    def column(tiles, t, b):
+    pair = sum_ref[TALL : TALL + GROUPS // 2 * ROWS, :]
+    trail_tiles = []
+    for q in range(GROUPS // 2):
+        factor = jnp.where(folded == 0, behind[2 * q], behind[2 * q + 1])
+        trail_tiles.append(pair[q * ROWS : (q + 1) * ROWS] * factor)
+    square = jnp.concatenate([pair, jnp.zeros((LANES - pair.shape[0], LANES), F32)], axis=0)
+    turned = jnp.transpose(square)
+
+    def turned_tile(h, b, f):
+        at = h * HALF + b * 2 * ROWS + f * ROWS
+        return turned[at : at + ROWS] * ahead[b]
+
+    lead_tiles = {(h, b, f): turned_tile(h, b, f) for h in range(2) for b in range(GROUPS) for f in range(2)}
+
+    def lead_column(t, b):
+        s, at = t // ROWS, (t // ROWS // 2) * ROWS + t % ROWS
+        return jnp.where(target == 0, spread(lead_tiles[0, b, s % 2], at), spread(lead_tiles[1, b, s % 2], at))
+
+    def trail_column(t, b):
         at = 2 * ROWS * (t // ROWS) + t % ROWS + ROWS * (b % 2)
-        tile = tiles[b // 2]
+        tile = trail_tiles[b // 2]
         return jnp.where(target == 0, spread(tile, at), spread(tile, HALF + at))
 
-    lead = [jnp.zeros((ROWS, LANES), F32)] * GROUPS
-    trail = [jnp.zeros((ROWS, LANES), F32)] * GROUPS
-    starts = [jnp.zeros((ROWS, LANES), F32)] * GROUPS
-    ends = [jnp.zeros((ROWS, LANES), F32)] * GROUPS
+    zero = jnp.zeros((ROWS, LANES), F32)
+    lead, trail, starts, ends = [zero] * GROUPS, [zero] * GROUPS, [zero] * GROUPS, [zero] * GROUPS
     v = jnp.ones((ROWS, LANES), F32)
     z = jnp.ones((ROWS, LANES), F32)
-    for step in range(markers):
-        t, u = step, markers - 1 - step
+    for t in range(MARKERS):
+        u = MARKERS - 1 - t
         bt, bu = t // ROWS, u // ROWS
         starts[bt] = jnp.where(row == t % ROWS, v, starts[bt])
         ends[bu] = jnp.where(row == u % ROWS, z, ends[bu])
         for b in range(bt, GROUPS):
-            lead[b] = lead[b] + v * column(lead_tiles, t, b)
+            lead[b] = lead[b] + v * lead_column(t, b)
         for b in range(bu + 1):
-            trail[b] = trail[b] + z * column(trail_tiles, u, b)
+            trail[b] = trail[b] + z * trail_column(u, b)
         v = jnp.broadcast_to(lead[bt][t % ROWS : t % ROWS + 1, :], (ROWS, LANES))
         z = jnp.broadcast_to(trail[bu][u % ROWS : u % ROWS + 1, :], (ROWS, LANES))
     total = v
 
     low = place < GROUPS // 2
+    side = jnp.where(low, 1, -1)
     inner = lane % HALF
-    outer = [jnp.where(low, starts[b], ends[GROUPS - 1 - b]) for b in range(2)]
-    outer = jnp.where(folded == 0, outer[0], outer[1])
+    near = [jnp.where(low, starts[b], ends[GROUPS - 1 - b]) for b in range(2)]
     across = [jnp.where(low, ends[b], starts[b]) for b in range(GROUPS)]
     picked = across[GROUPS - 1]
     for b in range(GROUPS - 1):
         picked = jnp.where(inner // (2 * ROWS) == b, across[b], picked)
     picked = jnp.where(row == lane % ROWS, picked, 0.0)
     across = jnp.sum(picked, axis=0, keepdims=True)
-    weight = outer * across
-    block = jnp.where(low, folded, GROUPS - 1 - folded)
-    side = jnp.where(low, 1, -1)
-    near = block * ROWS + row
-    far = ROWS * (inner // (2 * ROWS)) + lane % ROWS
-    parts = []
-    for i in range(ROWS):
-        t = place * ROWS + i
-        inside = ((near - t) * side <= 0) & ((far - t) * side >= 0)
-        tile = jnp.where(inside, t_ref[i * ROWS : (i + 1) * ROWS, :] * weight, 0.0)
-        parts.append(jnp.sum(tile, axis=0, keepdims=True))
-    parts = jnp.concatenate(parts, axis=0) * (inverse / total)
-    doses, logs = [], []
+    far_end = ROWS * (inner // (2 * ROWS)) + lane % ROWS
+    scale = inverse / total[0:1, :]
+
+    def inside(t, near_end):
+        return ((near_end - t) * side <= 0) & ((far_end - t) * side >= 0)
+
+    def put(rows_of_t):
+        doses = []
+        for h in range(2):
+            dose = jnp.sum(jnp.where(target == h, rows_of_t * scale, 0.0), axis=1, keepdims=True)
+            doses.append(jnp.sum(jnp.where(row == lane, dose, 0.0), axis=0, keepdims=True))
+        dose_ref[...] = jnp.concatenate(doses, axis=0)[:, :ROWS]
+
+    outermost = (place == 0) | (place == GROUPS - 1)
+
+    @pl.when(outermost)
+    def _():
+        weight = near[0] * across
+        near_end = place * ROWS + row
+        merged = zero
+        for q in range(ROWS // 2):
+            t = place * ROWS + 2 * q + folded
+            tile = jnp.where(inside(t, near_end), sum_ref[q * ROWS : (q + 1) * ROWS, :] * weight, 0.0)
+            tile = jnp.sum(tile, axis=0, keepdims=True)
+            merged = jnp.where(row // 2 == q, jnp.where(folded == row % 2, tile, 0.0), merged)
+        put(merged)
+
+    @pl.when(jnp.logical_not(outermost))
+    def _():
+        weight = jnp.where(folded == 0, near[0], near[1]) * across
+        near_end = jnp.where(low, folded, GROUPS - 1 - folded) * ROWS + row
+        merged = zero
+        for q in range(ROWS):
+            at = SHORT_TALL + q * ROWS
+            tile = jnp.where(inside(place * ROWS + q, near_end), sum_ref[at : at + ROWS, :] * weight, 0.0)
+            merged = jnp.where(row == q, jnp.sum(tile, axis=0, keepdims=True), merged)
+        put(merged)
+
     counts = jnp.sum(misc, axis=0, keepdims=True)
     stay = [jnp.log(1.0 - rate) for rate in rates]
     stay[0] = jnp.where(row == 0, 0.0, stay[0])
     stay = jnp.sum(sum(stay), axis=0, keepdims=True)
+    logs = []
     for h in range(2):
-        dose = jnp.sum(jnp.where(target == h, parts, 0.0), axis=1, keepdims=True)
-        doses.append(jnp.sum(jnp.where(row == lane, dose, 0.0), axis=0, keepdims=True))
         seen = sum(counts[:, b * wide + (2 + h) * ROWS : b * wide + (2 + h) * ROWS + 1] for b in range(GROUPS))
         whole = jnp.log(total[0:1, h * HALF : h * HALF + 1]) + stay[:, 0:1] + seen * math.log(SCALE)
-        logs.append(whole * (1.0 / markers))
-    dose_ref[...] = jnp.concatenate(doses, axis=0)[:, :ROWS]
-    log_ref[...] = jnp.concatenate(logs, axis=0)
+        logs.append(whole * (1.0 / MARKERS))
+    log_ref[...] = jnp.concatenate(logs, axis=1)
 
 
 def exchange(x, axis, by):
     peers = lax.axis_size(axis)
     return lax.ppermute(x, axis, [(i, i ^ by) for i in range(peers)])
+
+
+def exchange_crossed(x, by):
+    copies = lax.axis_size("batch")
+    peers = lax.axis_size("group") * copies
+    return lax.ppermute(x, ("group", "batch"), [(i, i ^ (copies + by)) for i in range(peers)])
 
 
 def on_device_windows(panel_alleles, recomb_rates, genotypes):
     width = panel_alleles.shape[1]
     copies = lax.axis_size("batch")
     chunk = width // GROUPS
-    markers = ROWS * GROUPS
-    cut = jax.ShapeDtypeStruct((ROWS, chunk + LANES), jnp.int32)
-    pieces = pl.pallas_call(
-        pack_kernel, out_shape=[cut] * GROUPS, in_specs=[SMEM, VMEM], out_specs=[VMEM] * GROUPS, name="pack"
-    )(genotypes, panel_alleles)
-    pieces = [pieces[0]] + [exchange(pieces[d], "group", d) for d in range(1, GROUPS)]
-    extra = (GROUPS + 1) * ROWS
+    place = lax.axis_index("group")
+    own_genos = jnp.broadcast_to(genotypes.T[:, :, None], (ROWS, 2, HALF)).reshape(ROWS, LANES)
+    cuts = panel_alleles.reshape(ROWS, GROUPS, chunk)
+    cuts = [lax.dynamic_index_in_dim(cuts, place ^ d, 1, False) for d in range(GROUPS)]
+    pieces, tags = [cuts[0]], [own_genos]
+    for d in range(1, GROUPS):
+        got = exchange(jnp.concatenate([cuts[d], own_genos], axis=1), "group", d)
+        pieces.append(got[:, :chunk])
+        tags.append(got[:, chunk:])
     sums_t, sums_e = pl.pallas_call(
         functools.partial(window_kernel, min(512, chunk)),
         out_shape=[
-            jax.ShapeDtypeStruct((GROUPS, ROWS * ROWS, LANES), F32),
-            jax.ShapeDtypeStruct((extra, LANES), F32),
+            jax.ShapeDtypeStruct((2, TALL, LANES), F32),
+            jax.ShapeDtypeStruct((EXTRA, LANES), F32),
         ],
-        in_specs=[SMEM] + [VMEM] * GROUPS,
+        in_specs=[SMEM] + [VMEM] * (2 * GROUPS),
         out_specs=[VMEM] * 2,
         scratch_shapes=[
-            pltpu.VMEM((markers, chunk), jnp.int32),
-            pltpu.VMEM((markers, LANES), jnp.int32),
-            pltpu.VMEM((2, 4 * markers, chunk), BF16),
-            pltpu.VMEM((len(LEFT) * 2 * ROWS, chunk), BF16),
+            pltpu.VMEM((MARKERS, chunk), jnp.int32),
+            pltpu.VMEM((MARKERS, LANES), jnp.int32),
+            pltpu.VMEM((2, 4 * MARKERS, chunk), BF16),
+            pltpu.VMEM((2, len(LEFT[0]) * 2 * ROWS, chunk), BF16),
         ],
-        compiler_params=pltpu.CompilerParams(vmem_limit_bytes=48 * 1024 * 1024),
+        compiler_params=pltpu.CompilerParams(vmem_limit_bytes=40 * 1024 * 1024),
         name="windows",
-    )(recomb_rates, *pieces)
-    place = lax.axis_index("group")
-    tall = ROWS * ROWS
-
-    def block(index):
-        return lax.dynamic_index_in_dim(sums_t, index, 0, False)
-
-    kept = jnp.concatenate([block(place), sums_e, block(place ^ 2)], axis=0)
-    sent = jnp.concatenate([block(place ^ 1), sums_e, block(place ^ 3)], axis=0)
-    kept = kept + exchange(sent, "group", 1)
-    got = exchange(kept[tall:], "group", 2)
-    kept = kept[: tall + extra] + jnp.concatenate([got[extra:], got[:extra]], axis=0)
+    )(recomb_rates, *pieces, *tags)
+
+    sent = jnp.concatenate([sums_t[0], sums_e, sums_t[1]], axis=0)
+    both = sent + exchange(sent, "group", 1)
+    low = place < GROUPS // 2
+    upper, lower = both[: TALL + EXTRA], both[TALL:]
+    lower = jnp.concatenate([lower[EXTRA:], lower[:EXTRA]], axis=0)
+    kept = jnp.where(low, upper, lower) + exchange(jnp.where(low, lower, upper), "group", 3)
     by = 1
     while by < copies:
-        kept = kept + exchange(kept, "batch", by)
+        kept = kept + exchange_crossed(kept, by)
         by *= 2
     dosage, logs = pl.pallas_call(
         functools.partial(finish_kernel, float(width * copies), float(copies)),
-        out_shape=[jax.ShapeDtypeStruct((2, ROWS), F32), jax.ShapeDtypeStruct((2, 1), F32)],
-        in_specs=[VMEM] * 2,
+        out_shape=[jax.ShapeDtypeStruct((2, ROWS), F32), jax.ShapeDtypeStruct((1, 2), F32)],
+        in_specs=[VMEM],
         out_specs=[VMEM] * 2,
         name="finish",
-    )(kept[:tall], kept[tall:])
+    )(kept)
     return dosage, logs.reshape(2)
 
 

time: 46.8 us -> 40.5 us (0.87)
  the two profiles are of different devices: /device:TPU:0 before, /device:TPU:25 now
where the time goes in v2:
time: 40.5 us; the launch traced here: 40.3 us
  waiting for transfers between devices  22.3 us (55%)
  Pallas kernels  6.98 us (17%)
  starting transfers between devices  6.72 us (17%)
  local copies, waits for them, and re-layouts  2.74 us (7%)
  between operations  0.77 us (2%)
  other arithmetic  0.72 us (2%)
    ppermute x3, waiting for transfers between devices, exchange_crossed(): lax.ppermute(x, ('group', 'batch'), [(i, i ^ copies + by) for i in range(...  12.1 us
    ppermute x5, waiting for transfers between devices, exchange(): return lax.ppermute(x, axis, [(i, i ^ by) for i in range(peers)])  10.2 us
    pallas_call x1, Pallas kernels, on_device_windows(): pl.pallas_call(functools.partial(window_kernel, min(512, chunk)), out_sha...  4.66 us
    ppermute x5, starting transfers between devices, exchange(): return lax.ppermute(x, axis, [(i, i ^ by) for i in range(peers)])  4.34 us
    ppermute x3, starting transfers between devices, exchange_crossed(): lax.ppermute(x, ('group', 'batch'), [(i, i ^ copies + by) for i in range(...  2.38 us
    pallas_call x1, Pallas kernels, on_device_windows(): pl.pallas_call(functools.partial(finish_kernel, float(width * copies), fl...  2.32 us
    unnamed x4, local copies, waits for them, and re-layouts  1.32 us
    squeeze x1, local copies, waits for them, and re-layouts, on_device_windows(): lax.dynamic_index_in_dim(cuts, place ^ d, 1, False)  1.13 us
  transfers between devices with their start and end apart: 8, of which 7 were waited for; matrix products, arithmetic and copies ran while one was open for 0% of the time, Pallas kernels for 0%

profile of v2, /device:TPU:25, one launch (start us, length us, event | category | flops | bytes accessed | tf_op | source)
XLA Modules:
  0.0 40.3 jit_solution(16374306486879404119)
XLA Ops:
  0.6 0.0 copy-start.1
  0.7 0.7 %copy-done.1 = s32[2,8]{1,0:T(2,128)S(1)} copy-done((s32[2,8]{1,0:T(2,128)S(1)}, s32[2,8]{1,0:T(2,128)}, u32[]{:S(2)}) %copy-start.1) | copy-done | bytes 88
  1.3 0.1 copy.5
  1.4 0.1 broadcast_in_dim.2
  1.5 0.1 reshape.15.refs_4_
  1.6 1.1 %dynamic-slice_bitcast_fusion = (s32[8,4096]{1,0:T(8,128)S(1)}, s32[8,4096]{1,0:T(8,128)S(1)}, s32[8,4096]{1,0:T(8,128)S(1)}, s32[8,4096]{1,0:T(8,128)S(1)}) fusion(s32[8,4,4096]{2,0,1:T(8,128)} %bitcast.15, s32[]{:T(128)S(6)} %select_n.29, s32[]{:T(128)S(6)} %select_n.28, s32[]{:T(128)S(6)} %select_n.27, s32[]{:T(128)S(6)} %select_n.26), kind=kLoop, calls=%fused_computation.3 | loop fusion | bytes 1048592 | tf_op jit(solution)/shard_map/jit(dynamic_index_in_dim)/squeeze | solution.py:487
  2.7 1.8 %collective-permute-start.2 = (s32[8,4224]{1,0:T(8,128)S(1)}, s32[8,4224]{1,0:T(8,128)S(1)}, u32[]{:S(2)}, u32[]{:S(2)}) collective-permute-start(s32[8,4224]{1,0:T(8,128)S(1)} %get-tuple-element.16), channel_id=1, source_target_pairs={{0,24},{8,16},{16,8},{24,0},{1,25},{9,17},{17,9},{25,1},{2,26},{10... | collective-permute-start | bytes 405512 | tf_op jit(solution)/shard_map/ppermute | solution.py:471
  4.6 0.3 collective-permute-start.1
  4.8 0.2 collective-permute-start
  5.0 3.9 %collective-permute-done.2 = s32[8,4224]{1,0:T(8,128)S(1)} collective-permute-done((s32[8,4224]{1,0:T(8,128)S(1)}, s32[8,4224]{1,0:T(8,128)S(1)}, u32[]{:S(2)}, u32[]{:S(2)}) %collective-permute-start.2) | collective-permute-done | bytes 135200 | tf_op jit(solution)/shard_map/ppermute | solution.py:471
  8.9 2.9 %collective-permute-done.1 = s32[8,4224]{1,0:T(8,128)S(1)} collective-permute-done((s32[8,4224]{1,0:T(8,128)S(1)}, s32[8,4224]{1,0:T(8,128)S(1)}, u32[]{:S(2)}, u32[]{:S(2)}) %collective-permute-start.1) | collective-permute-done | bytes 135200 | tf_op jit(solution)/shard_map/ppermute | solution.py:471
  11.8 0.0 collective-permute-done
  11.9 0.0 copy-start
  11.9 0.6 %copy-done = f32[8]{0:T(128)S(1)} copy-done((f32[8]{0:T(128)S(1)}, f32[8]{0:T(128)}, u32[]{:S(2)}) %copy-start) | copy-done | bytes 56
  12.5 4.7 %windows.1 = (f32[2,96,128]{2,1,0:T(8,128)S(1)}, f32[24,128]{1,0:T(8,128)S(1)}) custom-call(f32[8]{0:T(128)S(1)} %copy-done, s32[8,4096]{1,0:T(8,128)S(1)} %get-tuple-element.13.refs_0_, s32[8,4096]{1,0:T(8,128)S(1)} %slice.47.refs_1_, s32[8,4096]{1,0:T(8,128)S(1)} %slice.48.refs_2_, s32[8,4096]{1,0:T(8,128)S(1)} %slice.49.refs_3_, ...), custom_call_target="tpu_custom_call" | custom-call | tf_op jit(solution)/shard_map/windows/pallas_call | solution.py:493
  17.2 0.5 %collective-permute-start.3 = (f32[216,128]{1,0:T(8,128)S(1)}, f32[216,128]{1,0:T(8,128)S(1)}, u32[]{:S(2)}, u32[]{:S(2)}) collective-permute-start(f32[216,128]{1,0:T(8,128)S(1)} %pad_maximum_fusion), channel_id=1, source_target_pairs={{0,8},{8,0},{16,24},{24,16},{1,9},{9,1},{17,25},{25,17},{2,10},{10... | collective-permute-start | bytes 331784 | tf_op jit(solution)/shard_map/ppermute | solution.py:471
  17.7 1.0 %collective-permute-done.3 = f32[216,128]{1,0:T(8,128)S(1)} collective-permute-done((f32[216,128]{1,0:T(8,128)S(1)}, f32[216,128]{1,0:T(8,128)S(1)}, u32[]{:S(2)}, u32[]{:S(2)}) %collective-permute-start.3) | collective-permute-done | bytes 110624 | tf_op jit(solution)/shard_map/ppermute | solution.py:471
  18.8 1.5 %collective-permute-start.4 = (f32[120,128]{1,0:T(8,128)S(1)}, f32[120,128]{1,0:T(8,128)S(1)}, u32[]{:S(2)}, u32[]{:S(2)}) collective-permute-start(f32[120,128]{1,0:T(8,128)S(1)} %slice_select_fusion), channel_id=1, source_target_pairs={{0,24},{8,16},{16,8},{24,0},{1,25},{9,17},{17,9},{25,1},{2,26},{10... | collective-permute-start | bytes 184328 | tf_op jit(solution)/shard_map/ppermute | solution.py:471
  20.3 2.5 %collective-permute-done.4 = f32[120,128]{1,0:T(8,128)S(1)} collective-permute-done((f32[120,128]{1,0:T(8,128)S(1)}, f32[120,128]{1,0:T(8,128)S(1)}, u32[]{:S(2)}, u32[]{:S(2)}) %collective-permute-start.4) | collective-permute-done | bytes 61472 | tf_op jit(solution)/shard_map/ppermute | solution.py:471
  22.8 1.6 %collective-permute-start.5 = (f32[120,128]{1,0:T(8,128)S(1)}, f32[120,128]{1,0:T(8,128)S(1)}, u32[]{:S(2)}, u32[]{:S(2)}) collective-permute-start(f32[120,128]{1,0:T(8,128)S(1)} %select_add_fusion), channel_id=1, source_target_pairs={{0,9},{1,8},{2,11},{3,10},{4,13},{5,12},{6,15},{7,14},{8,1},{9,0},... | collective-permute-start | bytes 184328 | tf_op jit(solution)/shard_map/ppermute | solution.py:477
  24.4 2.5 %collective-permute-done.5 = f32[120,128]{1,0:T(8,128)S(1)} collective-permute-done((f32[120,128]{1,0:T(8,128)S(1)}, f32[120,128]{1,0:T(8,128)S(1)}, u32[]{:S(2)}, u32[]{:S(2)}) %collective-permute-start.5) | collective-permute-done | bytes 61472 | tf_op jit(solution)/shard_map/ppermute | solution.py:477
  26.9 0.5 %collective-permute-start.6 = (f32[120,128]{1,0:T(8,128)S(1)}, f32[120,128]{1,0:T(8,128)S(1)}, u32[]{:S(2)}, u32[]{:S(2)}) collective-permute-start(f32[120,128]{1,0:T(8,128)S(1)} %add.34), channel_id=1, source_target_pairs={{0,10},{1,11},{2,8},{3,9},{4,14},{5,15},{6,12},{7,13},{8,2},{9,3},... | collective-permute-start | bytes 184328 | tf_op jit(solution)/shard_map/ppermute | solution.py:477
  27.3 3.6 %collective-permute-done.6 = f32[120,128]{1,0:T(8,128)S(1)} collective-permute-done((f32[120,128]{1,0:T(8,128)S(1)}, f32[120,128]{1,0:T(8,128)S(1)}, u32[]{:S(2)}, u32[]{:S(2)}) %collective-permute-start.6) | collective-permute-done | bytes 61472 | tf_op jit(solution)/shard_map/ppermute | solution.py:477
  30.9 0.4 collective-permute-start.7
  31.3 6.0 %collective-permute-done.7 = f32[120,128]{1,0:T(8,128)S(1)} collective-permute-done((f32[120,128]{1,0:T(8,128)S(1)}, f32[120,128]{1,0:T(8,128)S(1)}, u32[]{:S(2)}, u32[]{:S(2)}) %collective-permute-start.7) | collective-permute-done | bytes 61472 | tf_op jit(solution)/shard_map/ppermute | solution.py:477
  37.3 0.6 %add.36.sum_ref = f32[120,128]{1,0:T(8,128)} add(f32[120,128]{1,0:T(8,128)S(1)} %add.35, f32[120,128]{1,0:T(8,128)S(1)} %collective-permute-done.7) | non-fusion elementwise | flops 15360 | bytes 184320 | tf_op jit(solution)/shard_map/add | solution.py:519
  37.9 2.3 %finish.1 = (f32[2,8]{1,0:T(2,128)}, f32[1,2]{1,0:T(1,128)}) custom-call(f32[120,128]{1,0:T(8,128)} %add.36.sum_ref), custom_call_target="tpu_custom_call" | custom-call | tf_op jit(solution)/shard_map/finish/pallas_call | solution.py:521
  (16 shorter events, 0.1 us)
Async XLA Ops:
  0.6 0.7 %copy-start.1 = (s32[2,8]{1,0:T(2,128)S(1)}, s32[2,8]{1,0:T(2,128)}, u32[]{:S(2)}) copy-start(s32[2,8]{1,0:T(2,128)} %param.5) | copy-start | bytes 196
  2.7 6.2 %collective-permute-start.2 = (s32[8,4224]{1,0:T(8,128)S(1)}, s32[8,4224]{1,0:T(8,128)S(1)}, u32[]{:S(2)}, u32[]{:S(2)}) collective-permute-start(s32[8,4224]{1,0:T(8,128)S(1)} %get-tuple-element.16), channel_id=1, source_target_pairs={{0,24},{8,16},{16,8},{24,0},{1,25},{9,17},{17,9},{25,1},{2,26},{10... | collective-permute-start | bytes 405512 | tf_op jit(solution)/shard_map/ppermute | solution.py:471
  4.6 7.2 %collective-permute-start.1 = (s32[8,4224]{1,0:T(8,128)S(1)}, s32[8,4224]{1,0:T(8,128)S(1)}, u32[]{:S(2)}, u32[]{:S(2)}) collective-permute-start(s32[8,4224]{1,0:T(8,128)S(1)} %get-tuple-element.17), channel_id=1, source_target_pairs={{0,16},{8,24},{16,0},{24,8},{1,17},{9,25},{17,1},{25,9},{2,18},{10... | collective-permute-start | bytes 405512 | tf_op jit(solution)/shard_map/ppermute | solution.py:471
  4.8 7.0 %collective-permute-start = (s32[8,4224]{1,0:T(8,128)S(1)}, s32[8,4224]{1,0:T(8,128)S(1)}, u32[]{:S(2)}, u32[]{:S(2)}) collective-permute-start(s32[8,4224]{1,0:T(8,128)S(1)} %get-tuple-element.18), channel_id=1, source_target_pairs={{0,8},{8,0},{16,24},{24,16},{1,9},{9,1},{17,25},{25,17},{2,10},{10... | collective-permute-start | bytes 405512 | tf_op jit(solution)/shard_map/ppermute | solution.py:471
  11.9 0.7 %copy-start = (f32[8]{0:T(128)S(1)}, f32[8]{0:T(128)}, u32[]{:S(2)}) copy-start(f32[8]{0:T(128)} %rate_ref.1) | copy-start | bytes 100
  17.2 1.5 %collective-permute-start.3 = (f32[216,128]{1,0:T(8,128)S(1)}, f32[216,128]{1,0:T(8,128)S(1)}, u32[]{:S(2)}, u32[]{:S(2)}) collective-permute-start(f32[216,128]{1,0:T(8,128)S(1)} %pad_maximum_fusion), channel_id=1, source_target_pairs={{0,8},{8,0},{16,24},{24,16},{1,9},{9,1},{17,25},{25,17},{2,10},{10... | collective-permute-start | bytes 331784 | tf_op jit(solution)/shard_map/ppermute | solution.py:471
  18.8 4.0 %collective-permute-start.4 = (f32[120,128]{1,0:T(8,128)S(1)}, f32[120,128]{1,0:T(8,128)S(1)}, u32[]{:S(2)}, u32[]{:S(2)}) collective-permute-start(f32[120,128]{1,0:T(8,128)S(1)} %slice_select_fusion), channel_id=1, source_target_pairs={{0,24},{8,16},{16,8},{24,0},{1,25},{9,17},{17,9},{25,1},{2,26},{10... | collective-permute-start | bytes 184328 | tf_op jit(solution)/shard_map/ppermute | solution.py:471
  22.8 4.0 %collective-permute-start.5 = (f32[120,128]{1,0:T(8,128)S(1)}, f32[120,128]{1,0:T(8,128)S(1)}, u32[]{:S(2)}, u32[]{:S(2)}) collective-permute-start(f32[120,128]{1,0:T(8,128)S(1)} %select_add_fusion), channel_id=1, source_target_pairs={{0,9},{1,8},{2,11},{3,10},{4,13},{5,12},{6,15},{7,14},{8,1},{9,0},... | collective-permute-start | bytes 184328 | tf_op jit(solution)/shard_map/ppermute | solution.py:477
  26.9 4.0 %collective-permute-start.6 = (f32[120,128]{1,0:T(8,128)S(1)}, f32[120,128]{1,0:T(8,128)S(1)}, u32[]{:S(2)}, u32[]{:S(2)}) collective-permute-start(f32[120,128]{1,0:T(8,128)S(1)} %add.34), channel_id=1, source_target_pairs={{0,10},{1,11},{2,8},{3,9},{4,14},{5,15},{6,12},{7,13},{8,2},{9,3},... | collective-permute-start | bytes 184328 | tf_op jit(solution)/shard_map/ppermute | solution.py:477
  30.9 6.4 %collective-permute-start.7 = (f32[120,128]{1,0:T(8,128)S(1)}, f32[120,128]{1,0:T(8,128)S(1)}, u32[]{:S(2)}, u32[]{:S(2)}) collective-permute-start(f32[120,128]{1,0:T(8,128)S(1)} %add.35), channel_id=1, source_target_pairs={{0,12},{1,13},{2,14},{3,15},{4,8},{5,9},{6,10},{7,11},{8,4},{9,5},... | collective-permute-start | bytes 184328 | tf_op jit(solution)/shard_map/ppermute | solution.py:477

commit v3 on v2

--- a/solution.py
+++ b/solution.py
@@ -225,6 +225,7 @@
 ROWS, LANES = 8, 128
 HALF = LANES // 2
 GROUPS = 4
+PARTS = 2
 MISSING = 2
 SCALE = math.sqrt(MISMATCH * (1.0 - MISMATCH))
 HALF_STEP = 0.5 * math.log((1.0 - MISMATCH) / MISMATCH)
@@ -251,10 +252,48 @@
 LEFT_AT = [{entry: slot for slot, entry in enumerate(LEFT[half])} for half in range(2)]
 TALL = len(LEFT[0]) // 4 * ROWS
 SHORT_TALL = ROWS // 2 * ROWS
-EXTRA = (GROUPS // 2 + 1) * ROWS
-
-
-def window_kernel(step, rate_ref, *refs):
+PAIRS = GROUPS // 2 * ROWS
+EXTRA = PAIRS + ROWS
+
+
+def pack_kernel(parts, geno_ref, rate_ref, panel_ref, *refs):
+    outs, (misc_ref, genos, rates_in, sems) = refs[:-4], refs[-4:]
+    place = lax.axis_index("group")
+    chunk = panel_ref.shape[1] // GROUPS
+    part = chunk // parts
+    copies = []
+    for n, ref in enumerate(outs):
+        d, p = n % GROUPS, n // GROUPS
+        start = pl.multiple_of((place ^ d) * chunk + p * part, LANES)
+        copies.append(
+            pltpu.make_async_copy(panel_ref.at[:, pl.ds(start, part)], ref.at[:, pl.ds(0, part)], sems.at[n])
+        )
+    small = [
+        pltpu.make_async_copy(geno_ref, genos, sems.at[len(outs)]),
+        pltpu.make_async_copy(rate_ref, rates_in, sems.at[len(outs) + 1]),
+    ]
+    for copy in small + copies:
+        copy.start()
+    for copy in small:
+        copy.wait()
+    row, lane = iota((ROWS, LANES), 0), iota((ROWS, LANES), 1)
+    tile = jnp.zeros((ROWS, LANES), jnp.int32)
+    rates = jnp.zeros((ROWS, LANES), F32)
+    for i in range(ROWS):
+        tile = jnp.where(row == i, jnp.where(lane < HALF, genos[0, i], genos[1, i]), tile)
+        rates = jnp.where(row == i, rates_in[i], rates)
+    for ref in outs[:GROUPS]:
+        ref[:, part:] = tile
+    inner = lane % (LANES // GROUPS)
+    known = jnp.where(tile == MISSING, 0.0, 1.0)
+    known = [jnp.broadcast_to(known[:, h * HALF : h * HALF + 1], (ROWS, LANES)) for h in range(2)]
+    misc = jnp.where(inner < 2 * ROWS, rates, jnp.where(inner < 3 * ROWS, known[0], known[1]))
+    misc_ref[...] = jnp.where(lane // (LANES // GROUPS) == place, misc, 0.0)
+    for copy in copies:
+        copy.wait()
+
+
+def window_kernel(step, *refs):
     pieces, geno_refs = refs[:GROUPS], refs[GROUPS : 2 * GROUPS]
     t_ref, em_ref, panel, genos, wide, left = refs[2 * GROUPS :]
     place = lax.axis_index("group")
@@ -328,17 +367,6 @@
     tiles = [both_targets(sums_e, [b, GROUPS + b]) for b in range(GROUPS)]
     for q in range(GROUPS // 2):
         em_ref[q * ROWS : (q + 1) * ROWS, :] = fold(tiles[2 * q], tiles[2 * q + 1])
-    row = iota((ROWS, LANES), 0)
-    rates = jnp.zeros((ROWS, LANES), F32)
-    for i in range(ROWS):
-        rates = jnp.where(row == i, rate_ref[i], rates)
-    own = pl.ds(pl.multiple_of(place * ROWS, ROWS), ROWS)
-    inner = lane % (LANES // GROUPS)
-    known = jnp.where(genos[own, :] == MISSING, 0.0, 1.0)
-    known0 = jnp.broadcast_to(known[:, 0:1], (ROWS, LANES))
-    known1 = jnp.broadcast_to(known[:, HALF : HALF + 1], (ROWS, LANES))
-    misc = jnp.where(inner < 2 * ROWS, rates, jnp.where(inner < 3 * ROWS, known0, known1))
-    em_ref[GROUPS // 2 * ROWS :, :] = jnp.where(lane // (LANES // GROUPS) == place, misc, 0.0)
 
 
 def near_markers(half):
@@ -482,33 +510,51 @@
     copies = lax.axis_size("batch")
     chunk = width // GROUPS
     place = lax.axis_index("group")
-    own_genos = jnp.broadcast_to(genotypes.T[:, :, None], (ROWS, 2, HALF)).reshape(ROWS, LANES)
-    cuts = panel_alleles.reshape(ROWS, GROUPS, chunk)
-    cuts = [lax.dynamic_index_in_dim(cuts, place ^ d, 1, False) for d in range(GROUPS)]
-    pieces, tags = [cuts[0]], [own_genos]
-    for d in range(1, GROUPS):
-        got = exchange(jnp.concatenate([cuts[d], own_genos], axis=1), "group", d)
-        pieces.append(got[:, :chunk])
-        tags.append(got[:, chunk:])
-    sums_t, sums_e = pl.pallas_call(
-        functools.partial(window_kernel, min(512, chunk)),
-        out_shape=[
-            jax.ShapeDtypeStruct((2, TALL, LANES), F32),
-            jax.ShapeDtypeStruct((EXTRA, LANES), F32),
+    part = chunk // PARTS
+    tagged = jax.ShapeDtypeStruct((ROWS, part + LANES), jnp.int32)
+    plain = jax.ShapeDtypeStruct((ROWS, part), jnp.int32)
+    shapes = [tagged if p == 0 else plain for p in range(PARTS) for d in range(GROUPS)]
+    *cuts, misc = pl.pallas_call(
+        functools.partial(pack_kernel, PARTS),
+        out_shape=shapes + [jax.ShapeDtypeStruct((ROWS, LANES), F32)],
+        in_specs=[pl.BlockSpec(memory_space=pltpu.HBM)] * 3,
+        out_specs=[VMEM] * (len(shapes) + 1),
+        scratch_shapes=[
+            pltpu.SMEM(genotypes.shape, jnp.int32),
+            pltpu.SMEM(recomb_rates.shape, F32),
+            pltpu.SemaphoreType.DMA((len(shapes) + 2,)),
         ],
-        in_specs=[SMEM] + [VMEM] * (2 * GROUPS),
-        out_specs=[VMEM] * 2,
-        scratch_shapes=[
-            pltpu.VMEM((MARKERS, chunk), jnp.int32),
-            pltpu.VMEM((MARKERS, LANES), jnp.int32),
-            pltpu.VMEM((2, 4 * MARKERS, chunk), BF16),
-            pltpu.VMEM((2, len(LEFT[0]) * 2 * ROWS, chunk), BF16),
-        ],
-        compiler_params=pltpu.CompilerParams(vmem_limit_bytes=40 * 1024 * 1024),
-        name="windows",
-    )(recomb_rates, *pieces, *tags)
-
-    sent = jnp.concatenate([sums_t[0], sums_e, sums_t[1]], axis=0)
+        compiler_params=pltpu.CompilerParams(vmem_limit_bytes=4 * 1024 * 1024),
+        name="pack",
+    )(*(pltpu.with_memory_space_constraint(x, pltpu.HBM) for x in (genotypes, recomb_rates, panel_alleles)))
+    cuts = [cut if n % GROUPS == 0 else exchange(cut, "group", n % GROUPS) for n, cut in enumerate(cuts)]
+    tags = [cut[:, part:] for cut in cuts[:GROUPS]]
+    sums = []
+    for p in range(PARTS):
+        pieces = [cut[:, :part] for cut in cuts[p * GROUPS : (p + 1) * GROUPS]]
+        sums.append(
+            pl.pallas_call(
+                functools.partial(window_kernel, min(512, part)),
+                out_shape=[
+                    jax.ShapeDtypeStruct((2, TALL, LANES), F32),
+                    jax.ShapeDtypeStruct((PAIRS, LANES), F32),
+                ],
+                in_specs=[VMEM] * (2 * GROUPS),
+                out_specs=[VMEM] * 2,
+                scratch_shapes=[
+                    pltpu.VMEM((MARKERS, part), jnp.int32),
+                    pltpu.VMEM((MARKERS, LANES), jnp.int32),
+                    pltpu.VMEM((2, 4 * MARKERS, part), BF16),
+                    pltpu.VMEM((2, len(LEFT[0]) * 2 * ROWS, part), BF16),
+                ],
+                compiler_params=pltpu.CompilerParams(vmem_limit_bytes=40 * 1024 * 1024),
+                cost_estimate=pl.CostEstimate(flops=part * 900000, bytes_accessed=0, transcendentals=0),
+                name="windows",
+            )(*pieces, *tags)
+        )
+    sums_t, sums_e = (sum(each) for each in zip(*sums))
+
+    sent = jnp.concatenate([sums_t[0], sums_e, misc, sums_t[1]], axis=0)
     both = sent + exchange(sent, "group", 1)
     low = place < GROUPS // 2
     upper, lower = both[: TALL + EXTRA], both[TALL:]
@@ -523,6 +569,7 @@
         out_shape=[jax.ShapeDtypeStruct((2, ROWS), F32), jax.ShapeDtypeStruct((1, 2), F32)],
         in_specs=[VMEM],
         out_specs=[VMEM] * 2,
+        compiler_params=pltpu.CompilerParams(vmem_limit_bytes=4 * 1024 * 1024),
         name="finish",
     )(kept)
     return dosage, logs.reshape(2)

time: 40.5 us -> 35.5 us (0.88)
  the two profiles are of different devices: /device:TPU:25 before, /device:TPU:1 now
where the time goes in v3:
time: 35.5 us; the launch traced here: 35.3 us
  waiting for transfers between devices  14.4 us (41%)
  starting transfers between devices  12.9 us (36%)
  Pallas kernels  7.21 us (20%)
  between operations  0.74 us (2%)
    ppermute x3, waiting for transfers between devices, exchange_crossed(): lax.ppermute(x, ('group', 'batch'), [(i, i ^ copies + by) for i in range(...  8.48 us
    ppermute x8, starting transfers between devices, exchange(): return lax.ppermute(x, axis, [(i, i ^ by) for i in range(peers)])  6.91 us
    ppermute x3, starting transfers between devices, exchange_crossed(): lax.ppermute(x, ('group', 'batch'), [(i, i ^ copies + by) for i in range(...  5.95 us
    ppermute x8, waiting for transfers between devices, exchange(): return lax.ppermute(x, axis, [(i, i ^ by) for i in range(peers)])  5.9 us
    pallas_call x2, Pallas kernels, on_device_windows(): pl.pallas_call(functools.partial(window_kernel, min(512, part)), out_shap...  4.55 us
    pallas_call x1, Pallas kernels, on_device_windows(): pl.pallas_call(functools.partial(finish_kernel, float(width * copies), fl...  1.5 us
    pallas_call x1, Pallas kernels, on_device_windows(): pl.pallas_call(functools.partial(pack_kernel, PARTS), out_shape=shapes +...  1.16 us
  transfers between devices with their start and end apart: 11, of which 8 were waited for; matrix products, arithmetic and copies ran while one was open for 0% of the time, Pallas kernels for 6%

profile of v3, /device:TPU:1, one launch (start us, length us, event | category | flops | bytes accessed | tf_op | source)
XLA Modules:
  0.0 35.3 jit_solution(6845352968304997174)
XLA Ops:
  0.6 1.2 %pack.1 = (s32[8,2176]{1,0:T(8,128)S(1)}, s32[8,2176]{1,0:T(8,128)S(1)}, s32[8,2176]{1,0:T(8,128)S(1)}, s32[8,2176]{1,0:T(8,128)S(1)}, s32[8,2048]{1,0:T(8,128)S...) custom-call(s32[2,8]{1,0:T(2,128)} %geno_ref.1, ...), custom_call_target="tpu_custom_call" | custom-call | tf_op jit(solution)/shard_map/pack/pallas_call | solution.py:517
  1.8 0.1 collective-permute-start
  1.9 2.7 %collective-permute-start.1 = (s32[8,2176]{1,0:T(8,128)S(1)}, s32[8,2176]{1,0:T(8,128)S(1)}, u32[]{:S(2)}, u32[]{:S(2)}) collective-permute-start(s32[8,2176]{1,0:T(8,128)S(1)} %get-tuple-element.19), channel_id=1, source_target_pairs={{0,16},{8,24},{16,0},{24,8},{1,17},{9,25},{17,1},{25,9},{2,18},{10... | collective-permute-start | bytes 208904 | tf_op jit(solution)/shard_map/ppermute | solution.py:499
  4.6 0.0 collective-permute-start.2
  4.6 0.4 %collective-permute-start.3 = (s32[8,2048]{1,0:T(8,128)S(1)}, s32[8,2048]{1,0:T(8,128)S(1)}, u32[]{:S(2)}, u32[]{:S(2)}) collective-permute-start(s32[8,2048]{1,0:T(8,128)S(1)} %get-tuple-element.23), channel_id=1, source_target_pairs={{0,8},{8,0},{16,24},{24,16},{1,9},{9,1},{17,25},{25,17},{2,10},{10... | collective-permute-start | bytes 196616 | tf_op jit(solution)/shard_map/ppermute | solution.py:499
  5.0 1.4 %collective-permute-start.4 = (s32[8,2048]{1,0:T(8,128)S(1)}, s32[8,2048]{1,0:T(8,128)S(1)}, u32[]{:S(2)}, u32[]{:S(2)}) collective-permute-start(s32[8,2048]{1,0:T(8,128)S(1)} %get-tuple-element.24), channel_id=1, source_target_pairs={{0,16},{8,24},{16,0},{24,8},{1,17},{9,25},{17,1},{25,9},{2,18},{10... | collective-permute-start | bytes 196616 | tf_op jit(solution)/shard_map/ppermute | solution.py:499
  6.5 0.0 collective-permute-done
  6.5 0.4 %collective-permute-start.5 = (s32[8,2048]{1,0:T(8,128)S(1)}, s32[8,2048]{1,0:T(8,128)S(1)}, u32[]{:S(2)}, u32[]{:S(2)}) collective-permute-start(s32[8,2048]{1,0:T(8,128)S(1)} %get-tuple-element.25), channel_id=1, source_target_pairs={{0,24},{8,16},{16,8},{24,0},{1,25},{9,17},{17,9},{25,1},{2,26},{10... | collective-permute-start | bytes 196616 | tf_op jit(solution)/shard_map/ppermute | solution.py:499
  6.9 0.2 collective-permute-done.1
  7.1 2.0 %collective-permute-done.2 = s32[8,2176]{1,0:T(8,128)S(1)} collective-permute-done((s32[8,2176]{1,0:T(8,128)S(1)}, s32[8,2176]{1,0:T(8,128)S(1)}, u32[]{:S(2)}, u32[]{:S(2)}) %collective-permute-start.2) | collective-permute-done | bytes 69664 | tf_op jit(solution)/shard_map/ppermute | solution.py:499
  9.1 2.3 %windows.2 = (f32[2,96,128]{2,1,0:T(8,128)S(1)}, f32[16,128]{1,0:T(8,128)S(1)}) custom-call(s32[8,2048]{1,0:T(8,128)S(1)} %slice.42.refs_0_, s32[8,2048]{1,0:T(8,128)S(1)} %slice.55.refs_1_, s32[8,2048]{1,0:T(8,128)S(1)} %slice.56.refs_2_, s32[8,2048]{1,0:T(8,128)S(1)} %slice.57.refs_3_, s32[8,128]{1,0:T(8,128)S(1)} %slice.46.refs_4_, ...), custom_call_target="tpu_custom_call" | custom-call | flops 1843200000 | tf_op jit(solution)/shard_map/windows/pallas_call | solution.py:536
  11.4 0.0 collective-permute-done.3.refs_1_
  11.4 0.0 collective-permute-done.4.refs_2_
  11.4 0.2 collective-permute-done.5.refs_3_
  11.5 2.3 %windows.3 = (f32[2,96,128]{2,1,0:T(8,128)S(1)}, f32[16,128]{1,0:T(8,128)S(1)}) custom-call(s32[8,2048]{1,0:T(8,128)S(1)} %get-tuple-element.22.refs_0_, s32[8,2048]{1,0:T(8,128)S(1)} %collective-permute-done.3.refs_1_, s32[8,2048]{1,0:T(8,128)S(1)} %collective-permute-done.4.refs_2_, s32[8,2048]{1,0:T(8,128)S(1)} %collective-permute-done.5.refs_3_, ...), custom_call_target="tpu_custom_call" | custom-call | flops 1843200000 | tf_op jit(solution)/shard_map/windows/pallas_call | solution.py:536
  13.9 0.4 %collective-permute-start.6 = (f32[216,128]{1,0:T(8,128)S(1)}, f32[216,128]{1,0:T(8,128)S(1)}, u32[]{:S(2)}, u32[]{:S(2)}) collective-permute-start(f32[216,128]{1,0:T(8,128)S(1)} %pad_maximum_fusion), channel_id=1, source_target_pairs={{0,8},{8,0},{16,24},{24,16},{1,9},{9,1},{17,25},{25,17},{2,10},{10... | collective-permute-start | bytes 331784 | tf_op jit(solution)/shard_map/ppermute | solution.py:499
  14.3 1.0 %collective-permute-done.6 = f32[216,128]{1,0:T(8,128)S(1)} collective-permute-done((f32[216,128]{1,0:T(8,128)S(1)}, f32[216,128]{1,0:T(8,128)S(1)}, u32[]{:S(2)}, u32[]{:S(2)}) %collective-permute-start.6) | collective-permute-done | bytes 110624 | tf_op jit(solution)/shard_map/ppermute | solution.py:499
  15.3 1.4 %collective-permute-start.7 = (f32[120,128]{1,0:T(8,128)S(1)}, f32[120,128]{1,0:T(8,128)S(1)}, u32[]{:S(2)}, u32[]{:S(2)}) collective-permute-start(f32[120,128]{1,0:T(8,128)S(1)} %slice_select_fusion), channel_id=1, source_target_pairs={{0,24},{8,16},{16,8},{24,0},{1,25},{9,17},{17,9},{25,1},{2,26},{10... | collective-permute-start | bytes 184328 | tf_op jit(solution)/shard_map/ppermute | solution.py:499
  16.8 2.6 %collective-permute-done.7 = f32[120,128]{1,0:T(8,128)S(1)} collective-permute-done((f32[120,128]{1,0:T(8,128)S(1)}, f32[120,128]{1,0:T(8,128)S(1)}, u32[]{:S(2)}, u32[]{:S(2)}) %collective-permute-start.7) | collective-permute-done | bytes 61472 | tf_op jit(solution)/shard_map/ppermute | solution.py:499
  19.4 1.6 %collective-permute-start.8 = (f32[120,128]{1,0:T(8,128)S(1)}, f32[120,128]{1,0:T(8,128)S(1)}, u32[]{:S(2)}, u32[]{:S(2)}) collective-permute-start(f32[120,128]{1,0:T(8,128)S(1)} %select_add_fusion), channel_id=1, source_target_pairs={{0,9},{1,8},{2,11},{3,10},{4,13},{5,12},{6,15},{7,14},{8,1},{9,0},... | collective-permute-start | bytes 184328 | tf_op jit(solution)/shard_map/ppermute | solution.py:505
  21.0 2.4 %collective-permute-done.8 = f32[120,128]{1,0:T(8,128)S(1)} collective-permute-done((f32[120,128]{1,0:T(8,128)S(1)}, f32[120,128]{1,0:T(8,128)S(1)}, u32[]{:S(2)}, u32[]{:S(2)}) %collective-permute-start.8) | collective-permute-done | bytes 61472 | tf_op jit(solution)/shard_map/ppermute | solution.py:505
  23.4 1.7 %collective-permute-start.9 = (f32[120,128]{1,0:T(8,128)S(1)}, f32[120,128]{1,0:T(8,128)S(1)}, u32[]{:S(2)}, u32[]{:S(2)}) collective-permute-start(f32[120,128]{1,0:T(8,128)S(1)} %add.25), channel_id=1, source_target_pairs={{0,10},{1,11},{2,8},{3,9},{4,14},{5,15},{6,12},{7,13},{8,2},{9,3},... | collective-permute-start | bytes 184328 | tf_op jit(solution)/shard_map/ppermute | solution.py:505
  25.1 2.4 %collective-permute-done.9 = f32[120,128]{1,0:T(8,128)S(1)} collective-permute-done((f32[120,128]{1,0:T(8,128)S(1)}, f32[120,128]{1,0:T(8,128)S(1)}, u32[]{:S(2)}, u32[]{:S(2)}) %collective-permute-start.9) | collective-permute-done | bytes 61472 | tf_op jit(solution)/shard_map/ppermute | solution.py:505
  27.5 2.6 %collective-permute-start.10 = (f32[120,128]{1,0:T(8,128)S(1)}, f32[120,128]{1,0:T(8,128)S(1)}, u32[]{:S(2)}, u32[]{:S(2)}) collective-permute-start(f32[120,128]{1,0:T(8,128)S(1)} %add.26), channel_id=1, source_target_pairs={{0,12},{1,13},{2,14},{3,15},{4,8},{5,9},{6,10},{7,11},{8,4},{9,5},... | collective-permute-start | bytes 184328 | tf_op jit(solution)/shard_map/ppermute | solution.py:505
  30.2 3.7 %collective-permute-done.10 = f32[120,128]{1,0:T(8,128)S(1)} collective-permute-done((f32[120,128]{1,0:T(8,128)S(1)}, f32[120,128]{1,0:T(8,128)S(1)}, u32[]{:S(2)}, u32[]{:S(2)}) %collective-permute-start.10) | collective-permute-done | bytes 61472 | tf_op jit(solution)/shard_map/ppermute | solution.py:505
  33.8 1.5 %finish.1 = (f32[2,8]{1,0:T(2,128)}, f32[1,2]{1,0:T(1,128)}) custom-call(f32[120,128]{1,0:T(8,128)S(1)} %add.27.sum_ref), custom_call_target="tpu_custom_call" | custom-call | tf_op jit(solution)/shard_map/finish/pallas_call | solution.py:567
  (20 shorter events, 0.1 us)
Async XLA Ops:
  1.8 4.7 %collective-permute-start = (s32[8,2176]{1,0:T(8,128)S(1)}, s32[8,2176]{1,0:T(8,128)S(1)}, u32[]{:S(2)}, u32[]{:S(2)}) collective-permute-start(s32[8,2176]{1,0:T(8,128)S(1)} %get-tuple-element.18), channel_id=1, source_target_pairs={{0,8},{8,0},{16,24},{24,16},{1,9},{9,1},{17,25},{25,17},{2,10},{10... | collective-permute-start | bytes 208904 | tf_op jit(solution)/shard_map/ppermute | solution.py:499
  1.9 5.1 %collective-permute-start.1 = (s32[8,2176]{1,0:T(8,128)S(1)}, s32[8,2176]{1,0:T(8,128)S(1)}, u32[]{:S(2)}, u32[]{:S(2)}) collective-permute-start(s32[8,2176]{1,0:T(8,128)S(1)} %get-tuple-element.19), channel_id=1, source_target_pairs={{0,16},{8,24},{16,0},{24,8},{1,17},{9,25},{17,1},{25,9},{2,18},{10... | collective-permute-start | bytes 208904 | tf_op jit(solution)/shard_map/ppermute | solution.py:499
  4.6 4.5 %collective-permute-start.2 = (s32[8,2176]{1,0:T(8,128)S(1)}, s32[8,2176]{1,0:T(8,128)S(1)}, u32[]{:S(2)}, u32[]{:S(2)}) collective-permute-start(s32[8,2176]{1,0:T(8,128)S(1)} %get-tuple-element.20), channel_id=1, source_target_pairs={{0,24},{8,16},{16,8},{24,0},{1,25},{9,17},{17,9},{25,1},{2,26},{10... | collective-permute-start | bytes 208904 | tf_op jit(solution)/shard_map/ppermute | solution.py:499
  4.6 6.7 %collective-permute-start.3 = (s32[8,2048]{1,0:T(8,128)S(1)}, s32[8,2048]{1,0:T(8,128)S(1)}, u32[]{:S(2)}, u32[]{:S(2)}) collective-permute-start(s32[8,2048]{1,0:T(8,128)S(1)} %get-tuple-element.23), channel_id=1, source_target_pairs={{0,8},{8,0},{16,24},{24,16},{1,9},{9,1},{17,25},{25,17},{2,10},{10... | collective-permute-start | bytes 196616 | tf_op jit(solution)/shard_map/ppermute | solution.py:499
  5.0 6.4 %collective-permute-start.4 = (s32[8,2048]{1,0:T(8,128)S(1)}, s32[8,2048]{1,0:T(8,128)S(1)}, u32[]{:S(2)}, u32[]{:S(2)}) collective-permute-start(s32[8,2048]{1,0:T(8,128)S(1)} %get-tuple-element.24), channel_id=1, source_target_pairs={{0,16},{8,24},{16,0},{24,8},{1,17},{9,25},{17,1},{25,9},{2,18},{10... | collective-permute-start | bytes 196616 | tf_op jit(solution)/shard_map/ppermute | solution.py:499
  6.5 5.1 %collective-permute-start.5 = (s32[8,2048]{1,0:T(8,128)S(1)}, s32[8,2048]{1,0:T(8,128)S(1)}, u32[]{:S(2)}, u32[]{:S(2)}) collective-permute-start(s32[8,2048]{1,0:T(8,128)S(1)} %get-tuple-element.25), channel_id=1, source_target_pairs={{0,24},{8,16},{16,8},{24,0},{1,25},{9,17},{17,9},{25,1},{2,26},{10... | collective-permute-start | bytes 196616 | tf_op jit(solution)/shard_map/ppermute | solution.py:499
  13.9 1.4 %collective-permute-start.6 = (f32[216,128]{1,0:T(8,128)S(1)}, f32[216,128]{1,0:T(8,128)S(1)}, u32[]{:S(2)}, u32[]{:S(2)}) collective-permute-start(f32[216,128]{1,0:T(8,128)S(1)} %pad_maximum_fusion), channel_id=1, source_target_pairs={{0,8},{8,0},{16,24},{24,16},{1,9},{9,1},{17,25},{25,17},{2,10},{10... | collective-permute-start | bytes 331784 | tf_op jit(solution)/shard_map/ppermute | solution.py:499
  15.3 4.0 %collective-permute-start.7 = (f32[120,128]{1,0:T(8,128)S(1)}, f32[120,128]{1,0:T(8,128)S(1)}, u32[]{:S(2)}, u32[]{:S(2)}) collective-permute-start(f32[120,128]{1,0:T(8,128)S(1)} %slice_select_fusion), channel_id=1, source_target_pairs={{0,24},{8,16},{16,8},{24,0},{1,25},{9,17},{17,9},{25,1},{2,26},{10... | collective-permute-start | bytes 184328 | tf_op jit(solution)/shard_map/ppermute | solution.py:499
  19.4 4.1 %collective-permute-start.8 = (f32[120,128]{1,0:T(8,128)S(1)}, f32[120,128]{1,0:T(8,128)S(1)}, u32[]{:S(2)}, u32[]{:S(2)}) collective-permute-start(f32[120,128]{1,0:T(8,128)S(1)} %select_add_fusion), channel_id=1, source_target_pairs={{0,9},{1,8},{2,11},{3,10},{4,13},{5,12},{6,15},{7,14},{8,1},{9,0},... | collective-permute-start | bytes 184328 | tf_op jit(solution)/shard_map/ppermute | solution.py:505
  23.4 4.1 %collective-permute-start.9 = (f32[120,128]{1,0:T(8,128)S(1)}, f32[120,128]{1,0:T(8,128)S(1)}, u32[]{:S(2)}, u32[]{:S(2)}) collective-permute-start(f32[120,128]{1,0:T(8,128)S(1)} %add.25), channel_id=1, source_target_pairs={{0,10},{1,11},{2,8},{3,9},{4,14},{5,15},{6,12},{7,13},{8,2},{9,3},... | collective-permute-start | bytes 184328 | tf_op jit(solution)/shard_map/ppermute | solution.py:505
  27.5 6.3 %collective-permute-start.10 = (f32[120,128]{1,0:T(8,128)S(1)}, f32[120,128]{1,0:T(8,128)S(1)}, u32[]{:S(2)}, u32[]{:S(2)}) collective-permute-start(f32[120,128]{1,0:T(8,128)S(1)} %add.26), channel_id=1, source_target_pairs={{0,12},{1,13},{2,14},{3,15},{4,8},{5,9},{6,10},{7,11},{8,4},{9,5},... | collective-permute-start | bytes 184328 | tf_op jit(solution)/shard_map/ppermute | solution.py:505

commit v4 on v3

--- a/solution.py
+++ b/solution.py
@@ -250,10 +250,11 @@
     for half in range(2)
 ]
 LEFT_AT = [{entry: slot for slot, entry in enumerate(LEFT[half])} for half in range(2)]
-TALL = len(LEFT[0]) // 4 * ROWS
-SHORT_TALL = ROWS // 2 * ROWS
 PAIRS = GROUPS // 2 * ROWS
-EXTRA = PAIRS + ROWS
+SUBSET = 5 * ROWS
+TALL = 2 * SUBSET
+TRIANGLES = [(0, 1), (2, 3), (7, -1)]
+MISC = ROWS
 
 
 def pack_kernel(parts, geno_ref, rate_ref, panel_ref, *refs):
@@ -284,11 +285,10 @@
         rates = jnp.where(row == i, rates_in[i], rates)
     for ref in outs[:GROUPS]:
         ref[:, part:] = tile
-    inner = lane % (LANES // GROUPS)
     known = jnp.where(tile == MISSING, 0.0, 1.0)
-    known = [jnp.broadcast_to(known[:, h * HALF : h * HALF + 1], (ROWS, LANES)) for h in range(2)]
-    misc = jnp.where(inner < 2 * ROWS, rates, jnp.where(inner < 3 * ROWS, known[0], known[1]))
-    misc_ref[...] = jnp.where(lane // (LANES // GROUPS) == place, misc, 0.0)
+    misc = jnp.where(lane == MISC + place, rates, 0.0)
+    misc = jnp.where((lane == MISC + GROUPS + place) | (lane == HALF + MISC + place), known, misc)
+    misc_ref[...] = misc
     for copy in copies:
         copy.wait()
 
@@ -352,40 +352,50 @@
     def both_targets(acc, slots):
         return jnp.where(lane < HALF, rows_of(acc, slots[0]), rows_of(acc, slots[1]))
 
+    row = iota((ROWS, LANES), 0)
     for half in range(2):
         sums_t = product(left[half], wide[half])
-        tiles = {
-            (t, b): both_targets(sums_t, [LEFT_AT[half][h, t, b] for h in range(2)]) for h, t, b in LEFT[half] if h == 0
-        }
-        short, long = near_markers(half)
-        pairs = [((short[2 * q], 0), (short[2 * q + 1], 0)) for q in range(ROWS // 2)]
-        pairs += [((t, 0), (t, 1)) for t in long]
-        for q, pair in enumerate(pairs):
-            a, b = (tiles[t, left_blocks(t)[depth]] for t, depth in pair)
-            t_ref[half, q * ROWS : (q + 1) * ROWS, :] = fold(a, b)
+
+        def tile(block, j, depth):
+            t = block * ROWS + (j if half == 0 else ROWS - 1 - j)
+            b = left_blocks(t)[depth]
+            return both_targets(sums_t, [LEFT_AT[half][h, t, b] for h in range(2)])
+
+        def triangle(block, depth, a):
+            if a < 0:
+                return jnp.zeros((ROWS, LANES), F32)
+            one = tile(block, a, depth)
+            if a > 2:
+                return one
+            other = tile(block, ROWS - 2 - a, depth)
+            if half == 0:
+                return jnp.where(row <= a, one, pltpu.roll(other, a + 1, 0))
+            return jnp.where(row >= ROWS - 1 - a, one, pltpu.roll(other, ROWS - 1 - a, 0))
+
+        blocks = [0, 1] if half == 0 else [GROUPS - 1, GROUPS - 2]
+        for subset in range(2):
+            rows = [fold(*(triangle(blocks[subset], subset, a) for a in pair)) for pair in TRIANGLES]
+            squares = [tile(blocks[1], subset * ROWS // 2 + j, 0) for j in range(ROWS // 2)]
+            rows += [fold(squares[0], squares[1]), fold(squares[2], squares[3])]
+            for q, value in enumerate(rows):
+                at = subset * SUBSET + q * ROWS
+                t_ref[half, at : at + ROWS, :] = value
     sums_e = product(wide[1], wide[0])
     tiles = [both_targets(sums_e, [b, GROUPS + b]) for b in range(GROUPS)]
     for q in range(GROUPS // 2):
         em_ref[q * ROWS : (q + 1) * ROWS, :] = fold(tiles[2 * q], tiles[2 * q + 1])
 
 
-def near_markers(half):
-    outer, inner = (0, 1) if half == 0 else (GROUPS - 1, GROUPS - 2)
-    return [outer * ROWS + i for i in range(ROWS)], [inner * ROWS + i for i in range(ROWS)]
-
-
-def finish_kernel(panel_size, copies, sum_ref, dose_ref, log_ref):
-    place = lax.axis_index("group")
+def solve_kernel(panel_size, copies, sum_ref, ends_ref, log_ref):
     row, lane = iota((ROWS, LANES), 0), iota((ROWS, LANES), 1)
     target = lane // HALF
     folded = (lane % (2 * ROWS)) // ROWS
-    misc = sum_ref[TALL + GROUPS // 2 * ROWS :, :] * (1.0 / copies)
-    wide = LANES // GROUPS
+    misc = sum_ref[:ROWS, :] * (1.0 / copies)
 
     def spread(tile, at):
         return jnp.broadcast_to(tile[:, at : at + 1], (ROWS, LANES))
 
-    rates = [spread(misc, b * wide) for b in range(GROUPS)]
+    rates = [spread(misc, MISC + b) for b in range(GROUPS)]
     odds = [rate / (1.0 - rate) for rate in rates]
     inverse = 1.0 / panel_size
     ahead = []
@@ -394,7 +404,7 @@
         ahead.append(jnp.concatenate([odds[b][1:, :], following], axis=0) * inverse)
     behind = [odd * inverse for odd in odds]
 
-    pair = sum_ref[TALL : TALL + GROUPS // 2 * ROWS, :]
+    pair = sum_ref[...]
     trail_tiles = []
     for q in range(GROUPS // 2):
         factor = jnp.where(folded == 0, behind[2 * q], behind[2 * q + 1])
@@ -432,66 +442,82 @@
             trail[b] = trail[b] + z * trail_column(u, b)
         v = jnp.broadcast_to(lead[bt][t % ROWS : t % ROWS + 1, :], (ROWS, LANES))
         z = jnp.broadcast_to(trail[bu][u % ROWS : u % ROWS + 1, :], (ROWS, LANES))
-    total = v
-
-    low = place < GROUPS // 2
-    side = jnp.where(low, 1, -1)
-    inner = lane % HALF
-    near = [jnp.where(low, starts[b], ends[GROUPS - 1 - b]) for b in range(2)]
-    across = [jnp.where(low, ends[b], starts[b]) for b in range(GROUPS)]
-    picked = across[GROUPS - 1]
-    for b in range(GROUPS - 1):
-        picked = jnp.where(inner // (2 * ROWS) == b, across[b], picked)
-    picked = jnp.where(row == lane % ROWS, picked, 0.0)
-    across = jnp.sum(picked, axis=0, keepdims=True)
-    far_end = ROWS * (inner // (2 * ROWS)) + lane % ROWS
-    scale = inverse / total[0:1, :]
-
-    def inside(t, near_end):
-        return ((near_end - t) * side <= 0) & ((far_end - t) * side >= 0)
-
-    def put(rows_of_t):
-        doses = []
-        for h in range(2):
-            dose = jnp.sum(jnp.where(target == h, rows_of_t * scale, 0.0), axis=1, keepdims=True)
-            doses.append(jnp.sum(jnp.where(row == lane, dose, 0.0), axis=0, keepdims=True))
-        dose_ref[...] = jnp.concatenate(doses, axis=0)[:, :ROWS]
-
-    outermost = (place == 0) | (place == GROUPS - 1)
-
-    @pl.when(outermost)
-    def _():
-        weight = near[0] * across
-        near_end = place * ROWS + row
-        merged = zero
-        for q in range(ROWS // 2):
-            t = place * ROWS + 2 * q + folded
-            tile = jnp.where(inside(t, near_end), sum_ref[q * ROWS : (q + 1) * ROWS, :] * weight, 0.0)
-            tile = jnp.sum(tile, axis=0, keepdims=True)
-            merged = jnp.where(row // 2 == q, jnp.where(folded == row % 2, tile, 0.0), merged)
-        put(merged)
-
-    @pl.when(jnp.logical_not(outermost))
-    def _():
-        weight = jnp.where(folded == 0, near[0], near[1]) * across
-        near_end = jnp.where(low, folded, GROUPS - 1 - folded) * ROWS + row
-        merged = zero
-        for q in range(ROWS):
-            at = SHORT_TALL + q * ROWS
-            tile = jnp.where(inside(place * ROWS + q, near_end), sum_ref[at : at + ROWS, :] * weight, 0.0)
-            merged = jnp.where(row == q, jnp.sum(tile, axis=0, keepdims=True), merged)
-        put(merged)
-
-    counts = jnp.sum(misc, axis=0, keepdims=True)
+    for b in range(GROUPS):
+        ends_ref[b * ROWS : (b + 1) * ROWS, :] = starts[b]
+        ends_ref[MARKERS + b * ROWS : MARKERS + (b + 1) * ROWS, :] = ends[b]
+    ends_ref[2 * MARKERS :, :] = inverse / v
+
     stay = [jnp.log(1.0 - rate) for rate in rates]
     stay[0] = jnp.where(row == 0, 0.0, stay[0])
     stay = jnp.sum(sum(stay), axis=0, keepdims=True)
+    counts = jnp.sum(misc, axis=0, keepdims=True)
     logs = []
-    for h in range(2):
-        seen = sum(counts[:, b * wide + (2 + h) * ROWS : b * wide + (2 + h) * ROWS + 1] for b in range(GROUPS))
-        whole = jnp.log(total[0:1, h * HALF : h * HALF + 1]) + stay[:, 0:1] + seen * math.log(SCALE)
+    for h, at in enumerate((MISC + GROUPS, HALF + MISC)):
+        seen = sum(counts[:, at + b : at + b + 1] for b in range(GROUPS))
+        whole = jnp.log(v[0:1, h * HALF : h * HALF + 1]) + stay[:, 0:1] + seen * math.log(SCALE)
         logs.append(whole * (1.0 / MARKERS))
     log_ref[...] = jnp.concatenate(logs, axis=1)
+
+
+def contract_kernel(weight_ref, t_ref, dose_ref):
+    place = lax.axis_index("group")
+    low = place < GROUPS // 2
+    inward = (place == 1) | (place == GROUPS - 2)
+    row, lane = iota((ROWS, LANES), 0), iota((ROWS, LANES), 1)
+    folded = (lane % (2 * ROWS)) // ROWS
+    side = jnp.where(low, 1, -1)
+    turn = jnp.where(low, 0, ROWS - 1)
+    order = turn + side * row
+
+    def weights(is_start, block):
+        at = jnp.where(is_start, 0, MARKERS) + block * ROWS
+        return weight_ref[pl.ds(pl.multiple_of(at, ROWS), ROWS), :]
+
+    picked = weights(jnp.logical_not(low), GROUPS - 1)
+    column = (lane % HALF) // (2 * ROWS)
+    for b in range(GROUPS - 1):
+        picked = jnp.where(column == b, weights(jnp.logical_not(low), b), picked)
+    picked = jnp.where(row == lane % ROWS, picked, 0.0)
+    across = jnp.sum(picked, axis=0, keepdims=True) * weight_ref[2 * MARKERS : 2 * MARKERS + 1, :]
+    far_end = ROWS * column + lane % ROWS
+
+    def reaches(j):
+        t = place * ROWS + turn + side * j
+        return (far_end - t) * side >= 0
+
+    near = weights(low, place)
+    base = jnp.where(inward, SUBSET, 0)
+    total = jnp.zeros((ROWS, LANES), F32)
+    for q, (a0, a1) in enumerate(TRIANGLES):
+        a = jnp.where(folded == 0, a0, a1)
+        own = order <= a
+        paired = (a >= 0) & (a < 3)
+        moved = []
+        for each in (a0, a1):
+            if 0 <= each < 3:
+                moved.append(jnp.where(low, pltpu.roll(near, each + 1, 0), pltpu.roll(near, ROWS - 1 - each, 0)))
+            else:
+                moved.append(near)
+        weight = jnp.where(own, near, jnp.where(folded == 0, moved[0], moved[1])) * across
+        data = t_ref[pl.ds(pl.multiple_of(base + q * ROWS, ROWS), ROWS), :]
+        valid = (own | paired) & reaches(jnp.where(own, a, ROWS - 2 - a))
+        terms = jnp.where(valid, data * weight, 0.0)
+        one = jnp.sum(jnp.where(own, terms, 0.0), axis=0, keepdims=True)
+        other = jnp.sum(jnp.where(own, 0.0, terms), axis=0, keepdims=True)
+        total = total + jnp.where(row == a, one, 0.0)
+        total = total + jnp.where(paired & (row == ROWS - 2 - a), other, 0.0)
+    outermost = weights(low, jnp.where(low, 0, GROUPS - 1)) * jnp.where(inward, 1.0, 0.0) * across
+    for subset in range(2):
+        for q in range(ROWS // 4):
+            j = subset * ROWS // 2 + 2 * q + folded
+            at = subset * SUBSET + (len(TRIANGLES) + q) * ROWS
+            terms = jnp.where(reaches(j), t_ref[at : at + ROWS, :] * outermost, 0.0)
+            total = total + jnp.where(row == j, jnp.sum(terms, axis=0, keepdims=True), 0.0)
+    doses = []
+    for h in range(2):
+        dose = jnp.sum(jnp.where(lane // HALF == h, total, 0.0), axis=1, keepdims=True)
+        doses.append(jnp.sum(jnp.where(order == lane, dose, 0.0), axis=0, keepdims=True))
+    dose_ref[...] = jnp.concatenate(doses, axis=0)[:, :ROWS]
 
 
 def exchange(x, axis, by):
@@ -499,10 +525,16 @@
     return lax.ppermute(x, axis, [(i, i ^ by) for i in range(peers)])
 
 
-def exchange_crossed(x, by):
-    copies = lax.axis_size("batch")
-    peers = lax.axis_size("group") * copies
-    return lax.ppermute(x, ("group", "batch"), [(i, i ^ (copies + by)) for i in range(peers)])
+def exchange_flat(x, by):
+    peers = lax.axis_size("group") * lax.axis_size("batch")
+    return lax.ppermute(x, ("group", "batch"), [(i, i ^ by) for i in range(peers)])
+
+
+def is_odd(bits):
+    odd = bits
+    for shift in (16, 8, 4, 2, 1):
+        odd = odd ^ (odd >> shift)
+    return odd & 1
 
 
 def on_device_windows(panel_alleles, recomb_rates, genotypes):
@@ -554,24 +586,47 @@
         )
     sums_t, sums_e = (sum(each) for each in zip(*sums))
 
-    sent = jnp.concatenate([sums_t[0], sums_e, misc, sums_t[1]], axis=0)
+    lane, row = iota(sums_e.shape, 1), iota(sums_e.shape, 0)
+    unused = (row < ROWS) & (lane % HALF >= MISC) & (lane % HALF < 2 * ROWS)
+    sums_e = jnp.where(unused, jnp.concatenate([misc, jnp.zeros_like(misc)], axis=0), sums_e)
+    sent = jnp.concatenate([sums_t.reshape(2 * TALL, LANES), sums_e], axis=0)
     both = sent + exchange(sent, "group", 1)
-    low = place < GROUPS // 2
-    upper, lower = both[: TALL + EXTRA], both[TALL:]
-    lower = jnp.concatenate([lower[EXTRA:], lower[:EXTRA]], axis=0)
-    kept = jnp.where(low, upper, lower) + exchange(jnp.where(low, lower, upper), "group", 3)
+    half = place // (GROUPS // 2)
+    carried = is_odd(place ^ lax.axis_index("batch"))
+
+    def part_of(which):
+        start = (2 * which + carried) * SUBSET
+        return jnp.concatenate([lax.dynamic_slice_in_dim(both, start, SUBSET), both[2 * TALL :]], axis=0)
+
+    core = copies
+    kept = part_of(half) + exchange_flat(part_of(1 - half), 2 * core + core)
     by = 1
     while by < copies:
-        kept = kept + exchange_crossed(kept, by)
+        kept = kept + exchange_flat(kept, by + core)
         by *= 2
-    dosage, logs = pl.pallas_call(
-        functools.partial(finish_kernel, float(width * copies), float(copies)),
-        out_shape=[jax.ShapeDtypeStruct((2, ROWS), F32), jax.ShapeDtypeStruct((1, 2), F32)],
+    mine = kept[:SUBSET]
+    theirs = exchange(mine, "group", 1)
+    weights, logs = pl.pallas_call(
+        functools.partial(solve_kernel, float(width * copies), float(copies)),
+        out_shape=[
+            jax.ShapeDtypeStruct((2 * MARKERS + ROWS, LANES), F32),
+            jax.ShapeDtypeStruct((1, 2), F32),
+        ],
         in_specs=[VMEM],
         out_specs=[VMEM] * 2,
         compiler_params=pltpu.CompilerParams(vmem_limit_bytes=4 * 1024 * 1024),
-        name="finish",
-    )(kept)
+        cost_estimate=pl.CostEstimate(flops=1000000, bytes_accessed=0, transcendentals=0),
+        name="solve",
+    )(kept[SUBSET:])
+    whole = jnp.where(carried == 0, jnp.concatenate([mine, theirs], axis=0), jnp.concatenate([theirs, mine], axis=0))
+    dosage = pl.pallas_call(
+        contract_kernel,
+        out_shape=jax.ShapeDtypeStruct((2, ROWS), F32),
+        in_specs=[VMEM] * 2,
+        out_specs=VMEM,
+        compiler_params=pltpu.CompilerParams(vmem_limit_bytes=4 * 1024 * 1024),
+        name="contract",
+    )(weights, whole)
     return dosage, logs.reshape(2)
 
 

time: 35.5 us -> 32.1 us (0.904)
  the two profiles are of different devices: /device:TPU:1 before, /device:TPU:0 now
where the time goes in v4:
time: 32.1 us; the launch traced here: 32 us
  starting transfers between devices  12.4 us (39%)
  waiting for transfers between devices  11 us (34%)
  Pallas kernels  7.64 us (24%)
  between operations  0.76 us (2%)
    ppermute x4, waiting for transfers between devices, exchange_flat(): lax.ppermute(x, ('group', 'batch'), [(i, i ^ by) for i in range(peers)])  7.5 us
    ppermute x4, starting transfers between devices, exchange_flat(): lax.ppermute(x, ('group', 'batch'), [(i, i ^ by) for i in range(peers)])  6.64 us
    ppermute x8, starting transfers between devices, exchange(): return lax.ppermute(x, axis, [(i, i ^ by) for i in range(peers)])  5.75 us
    pallas_call x2, Pallas kernels, on_device_windows(): pl.pallas_call(functools.partial(window_kernel, min(512, part)), out_shap...  4.55 us
    ppermute x8, waiting for transfers between devices, exchange(): return lax.ppermute(x, axis, [(i, i ^ by) for i in range(peers)])  3.47 us
    pallas_call x1, Pallas kernels, on_device_windows(): pl.pallas_call(functools.partial(solve_kernel, float(width * copies), flo...  1.23 us
    pallas_call x1, Pallas kernels, on_device_windows(): pl.pallas_call(functools.partial(pack_kernel, PARTS), out_shape=shapes +...  1.16 us
    pallas_call x1, Pallas kernels, on_device_windows(): pl.pallas_call(contract_kernel, out_shape=jax.ShapeDtypeStruct((2, ROWS),...  0.69 us
  transfers between devices with their start and end apart: 12, of which 8 were waited for; matrix products, arithmetic and copies ran while one was open for 0% of the time, Pallas kernels for 11%

profile of v4, /device:TPU:0, one launch (start us, length us, event | category | flops | bytes accessed | tf_op | source)
XLA Modules:
  0.0 32.0 jit_solution(2913245500135197133)
XLA Ops:
  0.6 1.2 %pack.1 = (s32[8,2176]{1,0:T(8,128)S(1)}, s32[8,2176]{1,0:T(8,128)S(1)}, s32[8,2176]{1,0:T(8,128)S(1)}, s32[8,2176]{1,0:T(8,128)S(1)}, s32[8,2048]{1,0:T(8,128)S...) custom-call(s32[2,8]{1,0:T(2,128)} %geno_ref.1, ...), custom_call_target="tpu_custom_call" | custom-call | tf_op jit(solution)/shard_map/pack/pallas_call | solution.py:549
  1.8 0.5 %collective-permute-start = (s32[8,2176]{1,0:T(8,128)S(1)}, s32[8,2176]{1,0:T(8,128)S(1)}, u32[]{:S(2)}, u32[]{:S(2)}) collective-permute-start(s32[8,2176]{1,0:T(8,128)S(1)} %get-tuple-element.18), channel_id=1, source_target_pairs={{0,8},{8,0},{16,24},{24,16},{1,9},{9,1},{17,25},{25,17},{2,10},{10... | collective-permute-start | bytes 208904 | tf_op jit(solution)/shard_map/ppermute | solution.py:525
  2.3 2.6 %collective-permute-start.1 = (s32[8,2176]{1,0:T(8,128)S(1)}, s32[8,2176]{1,0:T(8,128)S(1)}, u32[]{:S(2)}, u32[]{:S(2)}) collective-permute-start(s32[8,2176]{1,0:T(8,128)S(1)} %get-tuple-element.19), channel_id=1, source_target_pairs={{0,16},{8,24},{16,0},{24,8},{1,17},{9,25},{17,1},{25,9},{2,18},{10... | collective-permute-start | bytes 208904 | tf_op jit(solution)/shard_map/ppermute | solution.py:525
  4.9 0.1 collective-permute-start.2
  5.0 0.1 collective-permute-start.3
  5.1 1.9 %collective-permute-start.4 = (s32[8,2048]{1,0:T(8,128)S(1)}, s32[8,2048]{1,0:T(8,128)S(1)}, u32[]{:S(2)}, u32[]{:S(2)}) collective-permute-start(s32[8,2048]{1,0:T(8,128)S(1)} %get-tuple-element.24), channel_id=1, source_target_pairs={{0,16},{8,24},{16,0},{24,8},{1,17},{9,25},{17,1},{25,9},{2,18},{10... | collective-permute-start | bytes 196616 | tf_op jit(solution)/shard_map/ppermute | solution.py:525
  7.1 0.0 collective-permute-done
  7.1 0.1 collective-permute-start.5
  7.2 0.5 %collective-permute-done.1 = s32[8,2176]{1,0:T(8,128)S(1)} collective-permute-done((s32[8,2176]{1,0:T(8,128)S(1)}, s32[8,2176]{1,0:T(8,128)S(1)}, u32[]{:S(2)}, u32[]{:S(2)}) %collective-permute-start.1) | collective-permute-done | bytes 69664 | tf_op jit(solution)/shard_map/ppermute | solution.py:525
  7.7 1.4 %collective-permute-done.2 = s32[8,2176]{1,0:T(8,128)S(1)} collective-permute-done((s32[8,2176]{1,0:T(8,128)S(1)}, s32[8,2176]{1,0:T(8,128)S(1)}, u32[]{:S(2)}, u32[]{:S(2)}) %collective-permute-start.2) | collective-permute-done | bytes 69664 | tf_op jit(solution)/shard_map/ppermute | solution.py:525
  9.0 2.3 %windows.2 = (f32[2,80,128]{2,1,0:T(8,128)S(1)}, f32[16,128]{1,0:T(8,128)S(1)}) custom-call(s32[8,2048]{1,0:T(8,128)S(1)} %slice.34.refs_0_, s32[8,2048]{1,0:T(8,128)S(1)} %slice.45.refs_1_, s32[8,2048]{1,0:T(8,128)S(1)} %slice.46.refs_2_, s32[8,2048]{1,0:T(8,128)S(1)} %slice.47.refs_3_, s32[8,128]{1,0:T(8,128)S(1)} %slice.38.refs_4_, ...), custom_call_target="tpu_custom_call" | custom-call | flops 1843200000 | tf_op jit(solution)/shard_map/windows/pallas_call | solution.py:568
  11.3 0.0 collective-permute-done.3.refs_1_
  11.3 0.0 collective-permute-done.4.refs_2_
  11.3 0.5 %collective-permute-done.5.refs_3_ = s32[8,2048]{1,0:T(8,128)S(1)} collective-permute-done((s32[8,2048]{1,0:T(8,128)S(1)}, s32[8,2048]{1,0:T(8,128)S(1)}, u32[]{:S(2)}, u32[]{:S(2)}) %collective-permute-start.5) | collective-permute-done | bytes 65568 | tf_op jit(solution)/shard_map/ppermute | solution.py:525
  11.8 2.3 %windows.3 = (f32[2,80,128]{2,1,0:T(8,128)S(1)}, f32[16,128]{1,0:T(8,128)S(1)}) custom-call(s32[8,2048]{1,0:T(8,128)S(1)} %get-tuple-element.22.refs_0_, s32[8,2048]{1,0:T(8,128)S(1)} %collective-permute-done.3.refs_1_, s32[8,2048]{1,0:T(8,128)S(1)} %collective-permute-done.4.refs_2_, s32[8,2048]{1,0:T(8,128)S(1)} %collective-permute-done.5.refs_3_, ...), custom_call_target="tpu_custom_call" | custom-call | flops 1843200000 | tf_op jit(solution)/shard_map/windows/pallas_call | solution.py:568
  14.1 0.1 add_select_fusion
  14.2 0.2 collective-permute-start.6
  14.4 1.1 %collective-permute-done.6 = f32[176,128]{1,0:T(8,128)S(1)} collective-permute-done((f32[176,128]{1,0:T(8,128)S(1)}, f32[176,128]{1,0:T(8,128)S(1)}, u32[]{:S(2)}, u32[]{:S(2)}) %collective-permute-start.6) | collective-permute-done | bytes 90144 | tf_op jit(solution)/shard_map/ppermute | solution.py:525
  15.6 1.4 %collective-permute-start.7 = (f32[56,128]{1,0:T(8,128)S(1)}, f32[56,128]{1,0:T(8,128)S(1)}, u32[]{:S(2)}, u32[]{:S(2)}) collective-permute-start(f32[56,128]{1,0:T(8,128)S(1)} %pad_maximum_fusion.1), channel_id=1, source_target_pairs={{0,24},{1,25},{2,26},{3,27},{4,28},{5,29},{6,30},{7,31},{8,16},{9,... | collective-permute-start | bytes 86024 | tf_op jit(solution)/shard_map/ppermute | solution.py:530
  17.0 2.0 %collective-permute-done.7 = f32[56,128]{1,0:T(8,128)S(1)} collective-permute-done((f32[56,128]{1,0:T(8,128)S(1)}, f32[56,128]{1,0:T(8,128)S(1)}, u32[]{:S(2)}, u32[]{:S(2)}) %collective-permute-start.7) | collective-permute-done | bytes 28704 | tf_op jit(solution)/shard_map/ppermute | solution.py:530
  19.0 1.4 %collective-permute-start.8 = (f32[56,128]{1,0:T(8,128)S(1)}, f32[56,128]{1,0:T(8,128)S(1)}, u32[]{:S(2)}, u32[]{:S(2)}) collective-permute-start(f32[56,128]{1,0:T(8,128)S(1)} %fusion), channel_id=1, source_target_pairs={{0,9},{1,8},{2,11},{3,10},{4,13},{5,12},{6,15},{7,14},{8,1},{9,0},... | collective-permute-start | bytes 86024 | tf_op jit(solution)/shard_map/ppermute | solution.py:530
  20.4 1.9 %collective-permute-done.8 = f32[56,128]{1,0:T(8,128)S(1)} collective-permute-done((f32[56,128]{1,0:T(8,128)S(1)}, f32[56,128]{1,0:T(8,128)S(1)}, u32[]{:S(2)}, u32[]{:S(2)}) %collective-permute-start.8) | collective-permute-done | bytes 28704 | tf_op jit(solution)/shard_map/ppermute | solution.py:530
  22.3 1.4 %collective-permute-start.9 = (f32[56,128]{1,0:T(8,128)S(1)}, f32[56,128]{1,0:T(8,128)S(1)}, u32[]{:S(2)}, u32[]{:S(2)}) collective-permute-start(f32[56,128]{1,0:T(8,128)S(1)} %add.54), channel_id=1, source_target_pairs={{0,10},{1,11},{2,8},{3,9},{4,14},{5,15},{6,12},{7,13},{8,2},{9,3},... | collective-permute-start | bytes 86024 | tf_op jit(solution)/shard_map/ppermute | solution.py:530
  23.7 1.9 %collective-permute-done.9 = f32[56,128]{1,0:T(8,128)S(1)} collective-permute-done((f32[56,128]{1,0:T(8,128)S(1)}, f32[56,128]{1,0:T(8,128)S(1)}, u32[]{:S(2)}, u32[]{:S(2)}) %collective-permute-start.9) | collective-permute-done | bytes 28704 | tf_op jit(solution)/shard_map/ppermute | solution.py:530
  25.6 2.4 %collective-permute-start.10 = (f32[56,128]{1,0:T(8,128)S(1)}, f32[56,128]{1,0:T(8,128)S(1)}, u32[]{:S(2)}, u32[]{:S(2)}) collective-permute-start(f32[56,128]{1,0:T(8,128)S(1)} %add.55), channel_id=1, source_target_pairs={{0,12},{1,13},{2,14},{3,15},{4,8},{5,9},{6,10},{7,11},{8,4},{9,5},... | collective-permute-start | bytes 86024 | tf_op jit(solution)/shard_map/ppermute | solution.py:530
  28.0 1.7 %collective-permute-done.10 = f32[56,128]{1,0:T(8,128)S(1)} collective-permute-done((f32[56,128]{1,0:T(8,128)S(1)}, f32[56,128]{1,0:T(8,128)S(1)}, u32[]{:S(2)}, u32[]{:S(2)}) %collective-permute-start.10) | collective-permute-done | bytes 28704 | tf_op jit(solution)/shard_map/ppermute | solution.py:530
  29.8 0.2 collective-permute-start.11
  30.0 1.2 %solve.1 = (f32[72,128]{1,0:T(8,128)S(1)}, f32[1,2]{1,0:T(1,128)}) custom-call(f32[16,128]{1,0:T(8,128)S(1)} %slice.52.sum_ref), custom_call_target="tpu_custom_call" | custom-call | flops 1000000 | tf_op jit(solution)/shard_map/solve/pallas_call | solution.py:609
  31.3 0.0 collective-permute-done.11
  31.3 0.7 %contract.1 = f32[2,8]{1,0:T(2,128)} custom-call(f32[72,128]{1,0:T(8,128)S(1)} %get-tuple-element.30.weight_ref, f32[80,128]{1,0:T(8,128)S(1)} %maximum_select_fusion.t_ref), custom_call_target="tpu_custom_call" | custom-call | tf_op jit(solution)/shard_map/contract/pallas_call | solution.py:622
  (24 shorter events, 0.1 us)
Async XLA Ops:
  1.8 5.3 %collective-permute-start = (s32[8,2176]{1,0:T(8,128)S(1)}, s32[8,2176]{1,0:T(8,128)S(1)}, u32[]{:S(2)}, u32[]{:S(2)}) collective-permute-start(s32[8,2176]{1,0:T(8,128)S(1)} %get-tuple-element.18), channel_id=1, source_target_pairs={{0,8},{8,0},{16,24},{24,16},{1,9},{9,1},{17,25},{25,17},{2,10},{10... | collective-permute-start | bytes 208904 | tf_op jit(solution)/shard_map/ppermute | solution.py:525
  2.3 5.3 %collective-permute-start.1 = (s32[8,2176]{1,0:T(8,128)S(1)}, s32[8,2176]{1,0:T(8,128)S(1)}, u32[]{:S(2)}, u32[]{:S(2)}) collective-permute-start(s32[8,2176]{1,0:T(8,128)S(1)} %get-tuple-element.19), channel_id=1, source_target_pairs={{0,16},{8,24},{16,0},{24,8},{1,17},{9,25},{17,1},{25,9},{2,18},{10... | collective-permute-start | bytes 208904 | tf_op jit(solution)/shard_map/ppermute | solution.py:525
  4.9 4.1 %collective-permute-start.2 = (s32[8,2176]{1,0:T(8,128)S(1)}, s32[8,2176]{1,0:T(8,128)S(1)}, u32[]{:S(2)}, u32[]{:S(2)}) collective-permute-start(s32[8,2176]{1,0:T(8,128)S(1)} %get-tuple-element.20), channel_id=1, source_target_pairs={{0,24},{8,16},{16,8},{24,0},{1,25},{9,17},{17,9},{25,1},{2,26},{10... | collective-permute-start | bytes 208904 | tf_op jit(solution)/shard_map/ppermute | solution.py:525
  5.0 6.4 %collective-permute-start.3 = (s32[8,2048]{1,0:T(8,128)S(1)}, s32[8,2048]{1,0:T(8,128)S(1)}, u32[]{:S(2)}, u32[]{:S(2)}) collective-permute-start(s32[8,2048]{1,0:T(8,128)S(1)} %get-tuple-element.23), channel_id=1, source_target_pairs={{0,8},{8,0},{16,24},{24,16},{1,9},{9,1},{17,25},{25,17},{2,10},{10... | collective-permute-start | bytes 196616 | tf_op jit(solution)/shard_map/ppermute | solution.py:525
  5.1 6.2 %collective-permute-start.4 = (s32[8,2048]{1,0:T(8,128)S(1)}, s32[8,2048]{1,0:T(8,128)S(1)}, u32[]{:S(2)}, u32[]{:S(2)}) collective-permute-start(s32[8,2048]{1,0:T(8,128)S(1)} %get-tuple-element.24), channel_id=1, source_target_pairs={{0,16},{8,24},{16,0},{24,8},{1,17},{9,25},{17,1},{25,9},{2,18},{10... | collective-permute-start | bytes 196616 | tf_op jit(solution)/shard_map/ppermute | solution.py:525
  7.1 4.8 %collective-permute-start.5 = (s32[8,2048]{1,0:T(8,128)S(1)}, s32[8,2048]{1,0:T(8,128)S(1)}, u32[]{:S(2)}, u32[]{:S(2)}) collective-permute-start(s32[8,2048]{1,0:T(8,128)S(1)} %get-tuple-element.25), channel_id=1, source_target_pairs={{0,24},{8,16},{16,8},{24,0},{1,25},{9,17},{17,9},{25,1},{2,26},{10... | collective-permute-start | bytes 196616 | tf_op jit(solution)/shard_map/ppermute | solution.py:525
  14.2 1.4 %collective-permute-start.6 = (f32[176,128]{1,0:T(8,128)S(1)}, f32[176,128]{1,0:T(8,128)S(1)}, u32[]{:S(2)}, u32[]{:S(2)}) collective-permute-start(f32[176,128]{1,0:T(8,128)S(1)} %pad_maximum_fusion), channel_id=1, source_target_pairs={{0,8},{8,0},{16,24},{24,16},{1,9},{9,1},{17,25},{25,17},{2,10},{10... | collective-permute-start | bytes 270344 | tf_op jit(solution)/shard_map/ppermute | solution.py:525
  15.6 3.4 %collective-permute-start.7 = (f32[56,128]{1,0:T(8,128)S(1)}, f32[56,128]{1,0:T(8,128)S(1)}, u32[]{:S(2)}, u32[]{:S(2)}) collective-permute-start(f32[56,128]{1,0:T(8,128)S(1)} %pad_maximum_fusion.1), channel_id=1, source_target_pairs={{0,24},{1,25},{2,26},{3,27},{4,28},{5,29},{6,30},{7,31},{8,16},{9,... | collective-permute-start | bytes 86024 | tf_op jit(solution)/shard_map/ppermute | solution.py:530
  19.0 3.3 %collective-permute-start.8 = (f32[56,128]{1,0:T(8,128)S(1)}, f32[56,128]{1,0:T(8,128)S(1)}, u32[]{:S(2)}, u32[]{:S(2)}) collective-permute-start(f32[56,128]{1,0:T(8,128)S(1)} %fusion), channel_id=1, source_target_pairs={{0,9},{1,8},{2,11},{3,10},{4,13},{5,12},{6,15},{7,14},{8,1},{9,0},... | collective-permute-start | bytes 86024 | tf_op jit(solution)/shard_map/ppermute | solution.py:530
  22.3 3.3 %collective-permute-start.9 = (f32[56,128]{1,0:T(8,128)S(1)}, f32[56,128]{1,0:T(8,128)S(1)}, u32[]{:S(2)}, u32[]{:S(2)}) collective-permute-start(f32[56,128]{1,0:T(8,128)S(1)} %add.54), channel_id=1, source_target_pairs={{0,10},{1,11},{2,8},{3,9},{4,14},{5,15},{6,12},{7,13},{8,2},{9,3},... | collective-permute-start | bytes 86024 | tf_op jit(solution)/shard_map/ppermute | solution.py:530
  25.6 4.2 %collective-permute-start.10 = (f32[56,128]{1,0:T(8,128)S(1)}, f32[56,128]{1,0:T(8,128)S(1)}, u32[]{:S(2)}, u32[]{:S(2)}) collective-permute-start(f32[56,128]{1,0:T(8,128)S(1)} %add.55), channel_id=1, source_target_pairs={{0,12},{1,13},{2,14},{3,15},{4,8},{5,9},{6,10},{7,11},{8,4},{9,5},... | collective-permute-start | bytes 86024 | tf_op jit(solution)/shard_map/ppermute | solution.py:530
  29.8 1.5 %collective-permute-start.11 = (f32[40,128]{1,0:T(8,128)S(1)}, f32[40,128]{1,0:T(8,128)S(1)}, u32[]{:S(2)}, u32[]{:S(2)}) collective-permute-start(f32[40,128]{1,0:T(8,128)S(1)} %slice.53), channel_id=1, source_target_pairs={{0,8},{8,0},{16,24},{24,16},{1,9},{9,1},{17,25},{25,17},{2,10},{10... | collective-permute-start | bytes 61448 | tf_op jit(solution)/shard_map/ppermute | solution.py:525

commit v5 on v4

--- a/solution.py
+++ b/solution.py
@@ -225,7 +225,7 @@
 ROWS, LANES = 8, 128
 HALF = LANES // 2
 GROUPS = 4
-PARTS = 2
+SHARES = (9, 7)
 MISSING = 2
 SCALE = math.sqrt(MISMATCH * (1.0 - MISMATCH))
 HALF_STEP = 0.5 * math.log((1.0 - MISMATCH) / MISMATCH)
@@ -238,34 +238,27 @@
     return lax.broadcasted_iota(jnp.int32, shape, axis)
 
 
-def left_blocks(t):
-    b = t // ROWS
-    return list(range(b + 1)) if b < GROUPS // 2 else list(range(GROUPS - 1, b - 1, -1))
-
-
 MARKERS = ROWS * GROUPS
 HALF_T = MARKERS // 2
-LEFT = [
-    [(h, t, b) for t in range(half * HALF_T, (half + 1) * HALF_T) for b in left_blocks(t) for h in range(2)]
-    for half in range(2)
-]
-LEFT_AT = [{entry: slot for slot, entry in enumerate(LEFT[half])} for half in range(2)]
 PAIRS = GROUPS // 2 * ROWS
 SUBSET = 5 * ROWS
 TALL = 2 * SUBSET
 TRIANGLES = [(0, 1), (2, 3), (7, -1)]
 MISC = ROWS
-
-
-def pack_kernel(parts, geno_ref, rate_ref, panel_ref, *refs):
+TILES = [
+    ("triangle", subset, a, ROWS - 2 - a if a < 3 else -1) for subset in range(2) for pair in TRIANGLES for a in pair if a >= 0
+] + [("square", 1, j, -1) for j in range(ROWS)]
+
+
+def pack_kernel(widths, geno_ref, rate_ref, panel_ref, *refs):
     outs, (misc_ref, genos, rates_in, sems) = refs[:-4], refs[-4:]
     place = lax.axis_index("group")
     chunk = panel_ref.shape[1] // GROUPS
-    part = chunk // parts
     copies = []
     for n, ref in enumerate(outs):
         d, p = n % GROUPS, n // GROUPS
-        start = pl.multiple_of((place ^ d) * chunk + p * part, LANES)
+        part = widths[p]
+        start = pl.multiple_of((place ^ d) * chunk + sum(widths[:p]), LANES)
         copies.append(
             pltpu.make_async_copy(panel_ref.at[:, pl.ds(start, part)], ref.at[:, pl.ds(0, part)], sems.at[n])
         )
@@ -284,7 +277,7 @@
         tile = jnp.where(row == i, jnp.where(lane < HALF, genos[0, i], genos[1, i]), tile)
         rates = jnp.where(row == i, rates_in[i], rates)
     for ref in outs[:GROUPS]:
-        ref[:, part:] = tile
+        ref[:, widths[0] :] = tile
     known = jnp.where(tile == MISSING, 0.0, 1.0)
     misc = jnp.where(lane == MISC + place, rates, 0.0)
     misc = jnp.where((lane == MISC + GROUPS + place) | (lane == HALF + MISC + place), known, misc)
@@ -332,10 +325,30 @@
                     both = jnp.concatenate([upper[at : at + ROWS], lower[at : at + ROWS]], axis=0).astype(BF16)
                     blocks[kind, h, b] = both
                     wide[kind, (h * GROUPS + b) * 2 * ROWS : (h * GROUPS + b + 1) * 2 * ROWS, here] = both
+        row = iota((ROWS, step), 0)
         for half in range(2):
-            for slot, (h, t, b) in enumerate(LEFT[half]):
-                carries = jnp.broadcast_to(panel[t : t + 1, here], (2 * ROWS, step)).astype(F32).astype(BF16)
-                left[half, slot * 2 * ROWS : (slot + 1) * 2 * ROWS, here] = blocks[1 - half, h, b] * carries
+            for slot, (shape, subset, j, paired) in enumerate(TILES):
+                outer = 0 if half == 0 else GROUPS - 1
+                own = abs(outer - subset)
+                near = own if shape == "triangle" else outer
+                first = row <= j if half == 0 else row >= ROWS - 1 - j
+
+                def carries(j):
+                    t = own * ROWS + (j if half == 0 else ROWS - 1 - j)
+                    return jnp.broadcast_to(panel[t : t + 1, here], (ROWS, step)).astype(F32)
+
+                mask = carries(j) if paired < 0 else jnp.where(first, carries(j), carries(paired))
+                mask = jnp.concatenate([mask, mask], axis=0).astype(BF16)
+                for h in range(2):
+                    base = blocks[1 - half, h, near]
+                    if paired >= 0:
+                        at = h * 2 * MARKERS + (1 - half) * MARKERS + near * ROWS
+                        shift = j + 1 if half == 0 else ROWS - 1 - j
+                        both = [x[at : at + ROWS] for x in (upper, lower)]
+                        both = [jnp.where(first, x, pltpu.roll(x, shift, 0)) for x in both]
+                        base = jnp.concatenate(both, axis=0).astype(BF16)
+                    at = (slot * 2 + h) * 2 * ROWS
+                    left[half, at : at + 2 * ROWS, here] = base * mask
 
     def product(a, b):
         return lax.dot_general(a, b, (((1,), (1,)), ((), ())), preferred_element_type=F32)
@@ -352,34 +365,19 @@
     def both_targets(acc, slots):
         return jnp.where(lane < HALF, rows_of(acc, slots[0]), rows_of(acc, slots[1]))
 
-    row = iota((ROWS, LANES), 0)
+    zero = jnp.zeros((ROWS, LANES), F32)
     for half in range(2):
         sums_t = product(left[half], wide[half])
-
-        def tile(block, j, depth):
-            t = block * ROWS + (j if half == 0 else ROWS - 1 - j)
-            b = left_blocks(t)[depth]
-            return both_targets(sums_t, [LEFT_AT[half][h, t, b] for h in range(2)])
-
-        def triangle(block, depth, a):
-            if a < 0:
-                return jnp.zeros((ROWS, LANES), F32)
-            one = tile(block, a, depth)
-            if a > 2:
-                return one
-            other = tile(block, ROWS - 2 - a, depth)
-            if half == 0:
-                return jnp.where(row <= a, one, pltpu.roll(other, a + 1, 0))
-            return jnp.where(row >= ROWS - 1 - a, one, pltpu.roll(other, ROWS - 1 - a, 0))
-
-        blocks = [0, 1] if half == 0 else [GROUPS - 1, GROUPS - 2]
+        tiles = {
+            (shape, subset, j): both_targets(sums_t, [2 * slot, 2 * slot + 1])
+            for slot, (shape, subset, j, paired) in enumerate(TILES)
+        }
         for subset in range(2):
-            rows = [fold(*(triangle(blocks[subset], subset, a) for a in pair)) for pair in TRIANGLES]
-            squares = [tile(blocks[1], subset * ROWS // 2 + j, 0) for j in range(ROWS // 2)]
-            rows += [fold(squares[0], squares[1]), fold(squares[2], squares[3])]
-            for q, value in enumerate(rows):
+            rows = [[tiles.get(("triangle", subset, j), zero) for j in pair] for pair in TRIANGLES]
+            rows += [[tiles["square", 1, subset * ROWS // 2 + 2 * q + f] for f in range(2)] for q in range(ROWS // 4)]
+            for q, pair in enumerate(rows):
                 at = subset * SUBSET + q * ROWS
-                t_ref[half, at : at + ROWS, :] = value
+                t_ref[half, at : at + ROWS, :] = fold(*pair)
     sums_e = product(wide[1], wide[0])
     tiles = [both_targets(sums_e, [b, GROUPS + b]) for b in range(GROUPS)]
     for q in range(GROUPS // 2):
@@ -542,12 +540,14 @@
     copies = lax.axis_size("batch")
     chunk = width // GROUPS
     place = lax.axis_index("group")
-    part = chunk // PARTS
-    tagged = jax.ShapeDtypeStruct((ROWS, part + LANES), jnp.int32)
-    plain = jax.ShapeDtypeStruct((ROWS, part), jnp.int32)
-    shapes = [tagged if p == 0 else plain for p in range(PARTS) for d in range(GROUPS)]
+    widths = [chunk * share // sum(SHARES) for share in SHARES]
+    shapes = [
+        jax.ShapeDtypeStruct((ROWS, part + (LANES if p == 0 else 0)), jnp.int32)
+        for p, part in enumerate(widths)
+        for d in range(GROUPS)
+    ]
     *cuts, misc = pl.pallas_call(
-        functools.partial(pack_kernel, PARTS),
+        functools.partial(pack_kernel, widths),
         out_shape=shapes + [jax.ShapeDtypeStruct((ROWS, LANES), F32)],
         in_specs=[pl.BlockSpec(memory_space=pltpu.HBM)] * 3,
         out_specs=[VMEM] * (len(shapes) + 1),
@@ -559,14 +559,22 @@
         compiler_params=pltpu.CompilerParams(vmem_limit_bytes=4 * 1024 * 1024),
         name="pack",
     )(*(pltpu.with_memory_space_constraint(x, pltpu.HBM) for x in (genotypes, recomb_rates, panel_alleles)))
-    cuts = [cut if n % GROUPS == 0 else exchange(cut, "group", n % GROUPS) for n, cut in enumerate(cuts)]
-    tags = [cut[:, part:] for cut in cuts[:GROUPS]]
+    arrived = None
+    for p in range(len(widths)):
+        part = cuts[p * GROUPS : (p + 1) * GROUPS]
+        if arrived is not None:
+            part[1:], arrived = lax.optimization_barrier((part[1:], arrived))
+            cuts[(p - 1) * GROUPS + 1] = arrived
+        part = [cut if d == 0 else exchange(cut, "group", d) for d, cut in enumerate(part)]
+        cuts[p * GROUPS : (p + 1) * GROUPS] = part
+        arrived = part[1]
+    tags = [cut[:, widths[0] :] for cut in cuts[:GROUPS]]
     sums = []
-    for p in range(PARTS):
+    for p, part in enumerate(widths):
         pieces = [cut[:, :part] for cut in cuts[p * GROUPS : (p + 1) * GROUPS]]
         sums.append(
             pl.pallas_call(
-                functools.partial(window_kernel, min(512, part)),
+                functools.partial(window_kernel, min(256, part)),
                 out_shape=[
                     jax.ShapeDtypeStruct((2, TALL, LANES), F32),
                     jax.ShapeDtypeStruct((PAIRS, LANES), F32),
@@ -577,7 +585,7 @@
                     pltpu.VMEM((MARKERS, part), jnp.int32),
                     pltpu.VMEM((MARKERS, LANES), jnp.int32),
                     pltpu.VMEM((2, 4 * MARKERS, part), BF16),
-                    pltpu.VMEM((2, len(LEFT[0]) * 2 * ROWS, part), BF16),
+                    pltpu.VMEM((2, len(TILES) * 4 * ROWS, part), BF16),
                 ],
                 compiler_params=pltpu.CompilerParams(vmem_limit_bytes=40 * 1024 * 1024),
                 cost_estimate=pl.CostEstimate(flops=part * 900000, bytes_accessed=0, transcendentals=0),
@@ -637,7 +645,7 @@
         and copies & (copies - 1) == 0
         and markers == ROWS
         and genotypes.shape[0] == 2
-        and width % (GROUPS * LANES * 4) == 0
+        and width % (GROUPS * LANES * 32) == 0
     )
 
 

time: 32.1 us -> 31.6 us (0.984)
  starting transfers between devices: 12.4 us -> 13.5 us
  waiting for transfers between devices: 11 us -> 10.1 us
  Pallas kernels: 7.64 us -> 6.84 us
    ppermute x4, starting transfers between devices: 6.64 us -> 7.58 us  [exchange_flat(): lax.ppermute(x, ('group', 'batch'), [(i, i ^ by) for i in range(peers)])]
    ppermute x4, waiting for transfers between devices: 7.5 us -> 6.6 us  [exchange_flat(): lax.ppermute(x, ('group', 'batch'), [(i, i ^ by) for i in range(peers)])]
    pallas_call x3, Pallas kernels: 5.72 us -> 4.92 us  [the longest x2 3.77 us: on_device_windows(): pl.pallas_call(functools.partial(window_kernel, min(256, part)), out_shap...]
  transfers between devices with their start and end apart: 12 -> 12, of which waited for: 8 -> 8; matrix products, arithmetic and copies ran while one was open for 0% -> 0% of each run, Pallas kernels for 11% -> 10%
where the time goes in v5:
time: 31.6 us; the launch traced here: 31.4 us
  starting transfers between devices  13.5 us (43%)
  waiting for transfers between devices  10.1 us (32%)
  Pallas kernels  6.84 us (22%)
  between operations  0.75 us (2%)
    ppermute x4, starting transfers between devices, exchange_flat(): lax.ppermute(x, ('group', 'batch'), [(i, i ^ by) for i in range(peers)])  7.58 us
    ppermute x4, waiting for transfers between devices, exchange_flat(): lax.ppermute(x, ('group', 'batch'), [(i, i ^ by) for i in range(peers)])  6.6 us
    ppermute x8, starting transfers between devices, exchange(): return lax.ppermute(x, axis, [(i, i ^ by) for i in range(peers)])  5.94 us
    pallas_call x2, Pallas kernels, on_device_windows(): pl.pallas_call(functools.partial(window_kernel, min(256, part)), out_shap...  3.77 us
    ppermute x8, waiting for transfers between devices, exchange(): return lax.ppermute(x, axis, [(i, i ^ by) for i in range(peers)])  3.52 us
    pallas_call x1, Pallas kernels, on_device_windows(): pl.pallas_call(functools.partial(solve_kernel, float(width * copies), flo...  1.23 us
    pallas_call x1, Pallas kernels, on_device_windows(): pl.pallas_call(functools.partial(pack_kernel, widths), out_shape=shapes +...  1.15 us
    pallas_call x1, Pallas kernels, on_device_windows(): pl.pallas_call(contract_kernel, out_shape=jax.ShapeDtypeStruct((2, ROWS),...  0.69 us
  transfers between devices with their start and end apart: 12, of which 8 were waited for; matrix products, arithmetic and copies ran while one was open for 0% of the time, Pallas kernels for 10%

profile of v5, /device:TPU:0, one launch (start us, length us, event | category | flops | bytes accessed | tf_op | source)
XLA Modules:
  0.0 31.4 jit_solution(3237714828285758826)
XLA Ops:
  0.6 1.1 %pack.1 = (s32[8,2432]{1,0:T(8,128)S(1)}, s32[8,2432]{1,0:T(8,128)S(1)}, s32[8,2432]{1,0:T(8,128)S(1)}, s32[8,2432]{1,0:T(8,128)S(1)}, s32[8,1792]{1,0:T(8,128)S...) custom-call(s32[2,8]{1,0:T(2,128)} %geno_ref.1, ...), custom_call_target="tpu_custom_call" | custom-call | tf_op jit(solution)/shard_map/pack/pallas_call | solution.py:549
  1.8 0.5 %collective-permute-start = (s32[8,2432]{1,0:T(8,128)S(1)}, s32[8,2432]{1,0:T(8,128)S(1)}, u32[]{:S(2)}, u32[]{:S(2)}) collective-permute-start(s32[8,2432]{1,0:T(8,128)S(1)} %get-tuple-element.25), channel_id=1, source_target_pairs={{0,8},{8,0},{16,24},{24,16},{1,9},{9,1},{17,25},{25,17},{2,10},{10... | collective-permute-start | bytes 233480 | tf_op jit(solution)/shard_map/ppermute | solution.py:523
  2.3 2.6 %collective-permute-start.1 = (s32[8,2432]{1,0:T(8,128)S(1)}, s32[8,2432]{1,0:T(8,128)S(1)}, u32[]{:S(2)}, u32[]{:S(2)}) collective-permute-start(s32[8,2432]{1,0:T(8,128)S(1)} %get-tuple-element.27), channel_id=1, source_target_pairs={{0,16},{8,24},{16,0},{24,8},{1,17},{9,25},{17,1},{25,9},{2,18},{10... | collective-permute-start | bytes 233480 | tf_op jit(solution)/shard_map/ppermute | solution.py:523
  4.9 0.1 collective-permute-start.2
  5.0 0.0 collective-permute-done
  5.0 0.2 collective-permute-start.3
  5.2 1.9 %collective-permute-start.4 = (s32[8,1792]{1,0:T(8,128)S(1)}, s32[8,1792]{1,0:T(8,128)S(1)}, u32[]{:S(2)}, u32[]{:S(2)}) collective-permute-start(s32[8,1792]{1,0:T(8,128)S(1)} %get-tuple-element.32), channel_id=1, source_target_pairs={{0,16},{8,24},{16,0},{24,8},{1,17},{9,25},{17,1},{25,9},{2,18},{10... | collective-permute-start | bytes 172040 | tf_op jit(solution)/shard_map/ppermute | solution.py:523
  7.1 0.0 collective-permute-start.5
  7.2 0.7 %collective-permute-done.1 = s32[8,2432]{1,0:T(8,128)S(1)} collective-permute-done((s32[8,2432]{1,0:T(8,128)S(1)}, s32[8,2432]{1,0:T(8,128)S(1)}, u32[]{:S(2)}, u32[]{:S(2)}) %collective-permute-start.1) | collective-permute-done | bytes 77856 | tf_op jit(solution)/shard_map/ppermute | solution.py:523
  7.8 1.4 %collective-permute-done.2 = s32[8,2432]{1,0:T(8,128)S(1)} collective-permute-done((s32[8,2432]{1,0:T(8,128)S(1)}, s32[8,2432]{1,0:T(8,128)S(1)}, u32[]{:S(2)}, u32[]{:S(2)}) %collective-permute-start.2) | collective-permute-done | bytes 77856 | tf_op jit(solution)/shard_map/ppermute | solution.py:523
  9.2 2.1 %windows.2 = (f32[2,80,128]{2,1,0:T(8,128)S(1)}, f32[16,128]{1,0:T(8,128)S(1)}) custom-call(s32[8,2304]{1,0:T(8,128)S(1)} %slice.34.refs_0_, s32[8,2304]{1,0:T(8,128)S(1)} %slice.35.refs_1_, s32[8,2304]{1,0:T(8,128)S(1)} %slice.45.refs_2_, s32[8,2304]{1,0:T(8,128)S(1)} %slice.46.refs_3_, s32[8,128]{1,0:T(8,128)S(1)} %slice.38.refs_4_, ...), custom_call_target="tpu_custom_call" | custom-call | flops 2073600000 | tf_op jit(solution)/shard_map/windows/pallas_call | solution.py:576
  11.3 0.0 collective-permute-done.3.refs_1_
  11.3 0.0 collective-permute-done.4.refs_2_
  11.3 0.3 %collective-permute-done.5.refs_3_ = s32[8,1792]{1,0:T(8,128)S(1)} collective-permute-done((s32[8,1792]{1,0:T(8,128)S(1)}, s32[8,1792]{1,0:T(8,128)S(1)}, u32[]{:S(2)}, u32[]{:S(2)}) %collective-permute-start.5) | collective-permute-done | bytes 57376 | tf_op jit(solution)/shard_map/ppermute | solution.py:523
  11.6 1.7 %windows.3 = (f32[2,80,128]{2,1,0:T(8,128)S(1)}, f32[16,128]{1,0:T(8,128)S(1)}) custom-call(s32[8,1792]{1,0:T(8,128)S(1)} %get-tuple-element.30.refs_0_, s32[8,1792]{1,0:T(8,128)S(1)} %collective-permute-done.3.refs_1_, s32[8,1792]{1,0:T(8,128)S(1)} %collective-permute-done.4.refs_2_, s32[8,1792]{1,0:T(8,128)S(1)} %collective-permute-done.5.refs_3_, ...), custom_call_target="tpu_custom_call" | custom-call | flops 1612800000 | tf_op jit(solution)/shard_map/windows/pallas_call | solution.py:576
  13.4 0.1 add_select_fusion
  13.5 0.2 collective-permute-start.6
  13.7 1.1 %collective-permute-done.6 = f32[176,128]{1,0:T(8,128)S(1)} collective-permute-done((f32[176,128]{1,0:T(8,128)S(1)}, f32[176,128]{1,0:T(8,128)S(1)}, u32[]{:S(2)}, u32[]{:S(2)}) %collective-permute-start.6) | collective-permute-done | bytes 90144 | tf_op jit(solution)/shard_map/ppermute | solution.py:523
  14.9 1.6 %collective-permute-start.7 = (f32[56,128]{1,0:T(8,128)S(1)}, f32[56,128]{1,0:T(8,128)S(1)}, u32[]{:S(2)}, u32[]{:S(2)}) collective-permute-start(f32[56,128]{1,0:T(8,128)S(1)} %pad_maximum_fusion.1), channel_id=1, source_target_pairs={{0,24},{1,25},{2,26},{3,27},{4,28},{5,29},{6,30},{7,31},{8,16},{9,... | collective-permute-start | bytes 86024 | tf_op jit(solution)/shard_map/ppermute | solution.py:528
  16.5 1.7 %collective-permute-done.7 = f32[56,128]{1,0:T(8,128)S(1)} collective-permute-done((f32[56,128]{1,0:T(8,128)S(1)}, f32[56,128]{1,0:T(8,128)S(1)}, u32[]{:S(2)}, u32[]{:S(2)}) %collective-permute-start.7) | collective-permute-done | bytes 28704 | tf_op jit(solution)/shard_map/ppermute | solution.py:528
  18.2 1.6 %collective-permute-start.8 = (f32[56,128]{1,0:T(8,128)S(1)}, f32[56,128]{1,0:T(8,128)S(1)}, u32[]{:S(2)}, u32[]{:S(2)}) collective-permute-start(f32[56,128]{1,0:T(8,128)S(1)} %fusion), channel_id=1, source_target_pairs={{0,9},{1,8},{2,11},{3,10},{4,13},{5,12},{6,15},{7,14},{8,1},{9,0},... | collective-permute-start | bytes 86024 | tf_op jit(solution)/shard_map/ppermute | solution.py:528
  19.8 1.7 %collective-permute-done.8 = f32[56,128]{1,0:T(8,128)S(1)} collective-permute-done((f32[56,128]{1,0:T(8,128)S(1)}, f32[56,128]{1,0:T(8,128)S(1)}, u32[]{:S(2)}, u32[]{:S(2)}) %collective-permute-start.8) | collective-permute-done | bytes 28704 | tf_op jit(solution)/shard_map/ppermute | solution.py:528
  21.5 1.7 %collective-permute-start.9 = (f32[56,128]{1,0:T(8,128)S(1)}, f32[56,128]{1,0:T(8,128)S(1)}, u32[]{:S(2)}, u32[]{:S(2)}) collective-permute-start(f32[56,128]{1,0:T(8,128)S(1)} %add.54), channel_id=1, source_target_pairs={{0,10},{1,11},{2,8},{3,9},{4,14},{5,15},{6,12},{7,13},{8,2},{9,3},... | collective-permute-start | bytes 86024 | tf_op jit(solution)/shard_map/ppermute | solution.py:528
  23.2 1.6 %collective-permute-done.9 = f32[56,128]{1,0:T(8,128)S(1)} collective-permute-done((f32[56,128]{1,0:T(8,128)S(1)}, f32[56,128]{1,0:T(8,128)S(1)}, u32[]{:S(2)}, u32[]{:S(2)}) %collective-permute-start.9) | collective-permute-done | bytes 28704 | tf_op jit(solution)/shard_map/ppermute | solution.py:528
  24.8 2.7 %collective-permute-start.10 = (f32[56,128]{1,0:T(8,128)S(1)}, f32[56,128]{1,0:T(8,128)S(1)}, u32[]{:S(2)}, u32[]{:S(2)}) collective-permute-start(f32[56,128]{1,0:T(8,128)S(1)} %add.55), channel_id=1, source_target_pairs={{0,12},{1,13},{2,14},{3,15},{4,8},{5,9},{6,10},{7,11},{8,4},{9,5},... | collective-permute-start | bytes 86024 | tf_op jit(solution)/shard_map/ppermute | solution.py:528
  27.5 1.6 %collective-permute-done.10 = f32[56,128]{1,0:T(8,128)S(1)} collective-permute-done((f32[56,128]{1,0:T(8,128)S(1)}, f32[56,128]{1,0:T(8,128)S(1)}, u32[]{:S(2)}, u32[]{:S(2)}) %collective-permute-start.10) | collective-permute-done | bytes 28704 | tf_op jit(solution)/shard_map/ppermute | solution.py:528
  29.1 0.4 %collective-permute-start.11 = (f32[40,128]{1,0:T(8,128)S(1)}, f32[40,128]{1,0:T(8,128)S(1)}, u32[]{:S(2)}, u32[]{:S(2)}) collective-permute-start(f32[40,128]{1,0:T(8,128)S(1)} %slice.51), channel_id=1, source_target_pairs={{0,8},{8,0},{16,24},{24,16},{1,9},{9,1},{17,25},{25,17},{2,10},{10... | collective-permute-start | bytes 61448 | tf_op jit(solution)/shard_map/ppermute | solution.py:523
  29.5 1.2 %solve.1 = (f32[72,128]{1,0:T(8,128)S(1)}, f32[1,2]{1,0:T(1,128)}) custom-call(f32[16,128]{1,0:T(8,128)S(1)} %slice.50.sum_ref), custom_call_target="tpu_custom_call" | custom-call | flops 1000000 | tf_op jit(solution)/shard_map/solve/pallas_call | solution.py:617
  30.7 0.0 collective-permute-done.11
  30.7 0.7 %contract.1 = f32[2,8]{1,0:T(2,128)} custom-call(f32[72,128]{1,0:T(8,128)S(1)} %get-tuple-element.38.weight_ref, f32[80,128]{1,0:T(8,128)S(1)} %maximum_select_fusion.t_ref), custom_call_target="tpu_custom_call" | custom-call | tf_op jit(solution)/shard_map/contract/pallas_call | solution.py:630
  (24 shorter events, 0.1 us)
Async XLA Ops:
  1.8 3.2 %collective-permute-start = (s32[8,2432]{1,0:T(8,128)S(1)}, s32[8,2432]{1,0:T(8,128)S(1)}, u32[]{:S(2)}, u32[]{:S(2)}) collective-permute-start(s32[8,2432]{1,0:T(8,128)S(1)} %get-tuple-element.25), channel_id=1, source_target_pairs={{0,8},{8,0},{16,24},{24,16},{1,9},{9,1},{17,25},{25,17},{2,10},{10... | collective-permute-start | bytes 233480 | tf_op jit(solution)/shard_map/ppermute | solution.py:523
  2.3 5.5 %collective-permute-start.1 = (s32[8,2432]{1,0:T(8,128)S(1)}, s32[8,2432]{1,0:T(8,128)S(1)}, u32[]{:S(2)}, u32[]{:S(2)}) collective-permute-start(s32[8,2432]{1,0:T(8,128)S(1)} %get-tuple-element.27), channel_id=1, source_target_pairs={{0,16},{8,24},{16,0},{24,8},{1,17},{9,25},{17,1},{25,9},{2,18},{10... | collective-permute-start | bytes 233480 | tf_op jit(solution)/shard_map/ppermute | solution.py:523
  4.9 4.3 %collective-permute-start.2 = (s32[8,2432]{1,0:T(8,128)S(1)}, s32[8,2432]{1,0:T(8,128)S(1)}, u32[]{:S(2)}, u32[]{:S(2)}) collective-permute-start(s32[8,2432]{1,0:T(8,128)S(1)} %get-tuple-element.28), channel_id=1, source_target_pairs={{0,24},{8,16},{16,8},{24,0},{1,25},{9,17},{17,9},{25,1},{2,26},{10... | collective-permute-start | bytes 233480 | tf_op jit(solution)/shard_map/ppermute | solution.py:523
  5.0 6.3 %collective-permute-start.3 = (s32[8,1792]{1,0:T(8,128)S(1)}, s32[8,1792]{1,0:T(8,128)S(1)}, u32[]{:S(2)}, u32[]{:S(2)}) collective-permute-start(s32[8,1792]{1,0:T(8,128)S(1)} %get-tuple-element.31), channel_id=1, source_target_pairs={{0,8},{8,0},{16,24},{24,16},{1,9},{9,1},{17,25},{25,17},{2,10},{10... | collective-permute-start | bytes 172040 | tf_op jit(solution)/shard_map/ppermute | solution.py:523
  5.2 6.1 %collective-permute-start.4 = (s32[8,1792]{1,0:T(8,128)S(1)}, s32[8,1792]{1,0:T(8,128)S(1)}, u32[]{:S(2)}, u32[]{:S(2)}) collective-permute-start(s32[8,1792]{1,0:T(8,128)S(1)} %get-tuple-element.32), channel_id=1, source_target_pairs={{0,16},{8,24},{16,0},{24,8},{1,17},{9,25},{17,1},{25,9},{2,18},{10... | collective-permute-start | bytes 172040 | tf_op jit(solution)/shard_map/ppermute | solution.py:523
  7.1 4.5 %collective-permute-start.5 = (s32[8,1792]{1,0:T(8,128)S(1)}, s32[8,1792]{1,0:T(8,128)S(1)}, u32[]{:S(2)}, u32[]{:S(2)}) collective-permute-start(s32[8,1792]{1,0:T(8,128)S(1)} %get-tuple-element.33), channel_id=1, source_target_pairs={{0,24},{8,16},{16,8},{24,0},{1,25},{9,17},{17,9},{25,1},{2,26},{10... | collective-permute-start | bytes 172040 | tf_op jit(solution)/shard_map/ppermute | solution.py:523
  13.5 1.4 %collective-permute-start.6 = (f32[176,128]{1,0:T(8,128)S(1)}, f32[176,128]{1,0:T(8,128)S(1)}, u32[]{:S(2)}, u32[]{:S(2)}) collective-permute-start(f32[176,128]{1,0:T(8,128)S(1)} %pad_maximum_fusion), channel_id=1, source_target_pairs={{0,8},{8,0},{16,24},{24,16},{1,9},{9,1},{17,25},{25,17},{2,10},{10... | collective-permute-start | bytes 270344 | tf_op jit(solution)/shard_map/ppermute | solution.py:523
  14.9 3.4 %collective-permute-start.7 = (f32[56,128]{1,0:T(8,128)S(1)}, f32[56,128]{1,0:T(8,128)S(1)}, u32[]{:S(2)}, u32[]{:S(2)}) collective-permute-start(f32[56,128]{1,0:T(8,128)S(1)} %pad_maximum_fusion.1), channel_id=1, source_target_pairs={{0,24},{1,25},{2,26},{3,27},{4,28},{5,29},{6,30},{7,31},{8,16},{9,... | collective-permute-start | bytes 86024 | tf_op jit(solution)/shard_map/ppermute | solution.py:528
  18.2 3.3 %collective-permute-start.8 = (f32[56,128]{1,0:T(8,128)S(1)}, f32[56,128]{1,0:T(8,128)S(1)}, u32[]{:S(2)}, u32[]{:S(2)}) collective-permute-start(f32[56,128]{1,0:T(8,128)S(1)} %fusion), channel_id=1, source_target_pairs={{0,9},{1,8},{2,11},{3,10},{4,13},{5,12},{6,15},{7,14},{8,1},{9,0},... | collective-permute-start | bytes 86024 | tf_op jit(solution)/shard_map/ppermute | solution.py:528
  21.5 3.3 %collective-permute-start.9 = (f32[56,128]{1,0:T(8,128)S(1)}, f32[56,128]{1,0:T(8,128)S(1)}, u32[]{:S(2)}, u32[]{:S(2)}) collective-permute-start(f32[56,128]{1,0:T(8,128)S(1)} %add.54), channel_id=1, source_target_pairs={{0,10},{1,11},{2,8},{3,9},{4,14},{5,15},{6,12},{7,13},{8,2},{9,3},... | collective-permute-start | bytes 86024 | tf_op jit(solution)/shard_map/ppermute | solution.py:528
  24.8 4.2 %collective-permute-start.10 = (f32[56,128]{1,0:T(8,128)S(1)}, f32[56,128]{1,0:T(8,128)S(1)}, u32[]{:S(2)}, u32[]{:S(2)}) collective-permute-start(f32[56,128]{1,0:T(8,128)S(1)} %add.55), channel_id=1, source_target_pairs={{0,12},{1,13},{2,14},{3,15},{4,8},{5,9},{6,10},{7,11},{8,4},{9,5},... | collective-permute-start | bytes 86024 | tf_op jit(solution)/shard_map/ppermute | solution.py:528
  29.1 1.6 %collective-permute-start.11 = (f32[40,128]{1,0:T(8,128)S(1)}, f32[40,128]{1,0:T(8,128)S(1)}, u32[]{:S(2)}, u32[]{:S(2)}) collective-permute-start(f32[40,128]{1,0:T(8,128)S(1)} %slice.51), channel_id=1, source_target_pairs={{0,8},{8,0},{16,24},{24,16},{1,9},{9,1},{17,25},{25,17},{2,10},{10... | collective-permute-start | bytes 61448 | tf_op jit(solution)/shard_map/ppermute | solution.py:523

commit v6 on v5

--- a/solution.py
+++ b/solution.py
@@ -240,14 +240,23 @@
 
 MARKERS = ROWS * GROUPS
 HALF_T = MARKERS // 2
-PAIRS = GROUPS // 2 * ROWS
 SUBSET = 5 * ROWS
 TALL = 2 * SUBSET
-TRIANGLES = [(0, 1), (2, 3), (7, -1)]
-MISC = ROWS
-TILES = [
-    ("triangle", subset, a, ROWS - 2 - a if a < 3 else -1) for subset in range(2) for pair in TRIANGLES for a in pair if a >= 0
-] + [("square", 1, j, -1) for j in range(ROWS)]
+TRIANGLE, SQUARE = 0, 1
+SETS = [
+    [(TRIANGLE, 0, 0), (TRIANGLE, 0, 1), (TRIANGLE, 0, 3)]
+    + [(TRIANGLE, 1, a) for a in (0, 1, 2, 7)]
+    + [(SQUARE, 1, j) for j in (0, 1)],
+    [(TRIANGLE, 0, 2), (TRIANGLE, 0, 7), (TRIANGLE, 1, 3)] + [(SQUARE, 1, j) for j in range(2, ROWS)],
+]
+TILES = SETS[0] + SETS[1]
+TUCKED = [(1, 1), (1, 2), (1, 3), (2, 2), (2, 3), (3, 3)]
+FIRST_TUCKED = 3
+SPARE = 2
+
+
+def paired_with(shape, a):
+    return ROWS - 2 - a if shape == TRIANGLE and a < 3 else -1
 
 
 def pack_kernel(widths, geno_ref, rate_ref, panel_ref, *refs):
@@ -272,23 +281,23 @@
         copy.wait()
     row, lane = iota((ROWS, LANES), 0), iota((ROWS, LANES), 1)
     tile = jnp.zeros((ROWS, LANES), jnp.int32)
-    rates = jnp.zeros((ROWS, LANES), F32)
+    misc = jnp.zeros((ROWS, LANES), F32)
     for i in range(ROWS):
         tile = jnp.where(row == i, jnp.where(lane < HALF, genos[0, i], genos[1, i]), tile)
-        rates = jnp.where(row == i, rates_in[i], rates)
+        misc = jnp.where(lane == i, rates_in[i], misc)
+        for h in range(2):
+            known = jnp.where(genos[h, i] == MISSING, 0.0, 1.0)
+            misc = jnp.where(lane == 2 * ROWS * (h + 1) + i, known, misc)
     for ref in outs[:GROUPS]:
         ref[:, widths[0] :] = tile
-    known = jnp.where(tile == MISSING, 0.0, 1.0)
-    misc = jnp.where(lane == MISC + place, rates, 0.0)
-    misc = jnp.where((lane == MISC + GROUPS + place) | (lane == HALF + MISC + place), known, misc)
-    misc_ref[...] = misc
+    misc_ref[...] = jnp.where((row == GROUPS + place) | (row == GROUPS - 1 - place), misc, 0.0)
     for copy in copies:
         copy.wait()
 
 
 def window_kernel(step, *refs):
     pieces, geno_refs = refs[:GROUPS], refs[GROUPS : 2 * GROUPS]
-    t_ref, em_ref, panel, genos, wide, left = refs[2 * GROUPS :]
+    t_ref, panel, genos, wide, left = refs[2 * GROUPS :]
     place = lax.axis_index("group")
     columns = panel.shape[1]
     for d in range(GROUPS):
@@ -327,10 +336,11 @@
                     wide[kind, (h * GROUPS + b) * 2 * ROWS : (h * GROUPS + b + 1) * 2 * ROWS, here] = both
         row = iota((ROWS, step), 0)
         for half in range(2):
-            for slot, (shape, subset, j, paired) in enumerate(TILES):
+            for slot, (shape, block, j) in enumerate(TILES):
+                paired = paired_with(shape, j)
                 outer = 0 if half == 0 else GROUPS - 1
-                own = abs(outer - subset)
-                near = own if shape == "triangle" else outer
+                own = abs(outer - block)
+                near = own if shape == TRIANGLE else outer
                 first = row <= j if half == 0 else row >= ROWS - 1 - j
 
                 def carries(j):
@@ -365,35 +375,61 @@
     def both_targets(acc, slots):
         return jnp.where(lane < HALF, rows_of(acc, slots[0]), rows_of(acc, slots[1]))
 
-    zero = jnp.zeros((ROWS, LANES), F32)
+    def unfold(tile, column, to_column, odd):
+        shift = 2 * ROWS * (to_column - column) + ROWS * odd
+        tile = tile + pltpu.roll(tile, LANES - ROWS, 1)
+        return tile if shift == 0 else pltpu.roll(tile, shift % LANES, 1)
+
+    sums_e = product(wide[1], wide[0])
+    plain = [both_targets(sums_e, [b, GROUPS + b]) for b in range(GROUPS)]
+    column = (lane % HALF) // (2 * ROWS)
     for half in range(2):
+        outer = 0 if half == 0 else GROUPS - 1
         sums_t = product(left[half], wide[half])
-        tiles = {
-            (shape, subset, j): both_targets(sums_t, [2 * slot, 2 * slot + 1])
-            for slot, (shape, subset, j, paired) in enumerate(TILES)
-        }
+        tucked = {}
+        for n, (b, to) in enumerate(TUCKED):
+            slot = FIRST_TUCKED + n
+            moved = unfold(plain[b], to, outer, slot % 2)
+            here = (column == outer) & (first if slot % 2 == 0 else jnp.logical_not(first))
+            tucked.setdefault(slot // 2, []).append((here, moved))
         for subset in range(2):
-            rows = [[tiles.get(("triangle", subset, j), zero) for j in pair] for pair in TRIANGLES]
-            rows += [[tiles["square", 1, subset * ROWS // 2 + 2 * q + f] for f in range(2)] for q in range(ROWS // 4)]
-            for q, pair in enumerate(rows):
+            base = subset * len(SETS[0])
+            tiles = [both_targets(sums_t, [2 * n, 2 * n + 1]) for n in range(base, base + len(SETS[subset]))] + [plain[0]]
+            for q in range(SUBSET // ROWS):
+                value = fold(tiles[2 * q], tiles[2 * q + 1])
+                for here, moved in tucked.get(q, []):
+                    value = jnp.where(here, moved, value)
                 at = subset * SUBSET + q * ROWS
-                t_ref[half, at : at + ROWS, :] = fold(*pair)
-    sums_e = product(wide[1], wide[0])
-    tiles = [both_targets(sums_e, [b, GROUPS + b]) for b in range(GROUPS)]
-    for q in range(GROUPS // 2):
-        em_ref[q * ROWS : (q + 1) * ROWS, :] = fold(tiles[2 * q], tiles[2 * q + 1])
+                t_ref[half, at : at + ROWS, :] = value
 
 
 def solve_kernel(panel_size, copies, sum_ref, ends_ref, log_ref):
+    low = lax.axis_index("group") < GROUPS // 2
     row, lane = iota((ROWS, LANES), 0), iota((ROWS, LANES), 1)
     target = lane // HALF
     folded = (lane % (2 * ROWS)) // ROWS
-    misc = sum_ref[:ROWS, :] * (1.0 / copies)
+    column_of = (lane % HALF) // (2 * ROWS)
+    misc = sum_ref[SPARE // 2 * ROWS : (SPARE // 2 + 1) * ROWS, :]
 
     def spread(tile, at):
         return jnp.broadcast_to(tile[:, at : at + 1], (ROWS, LANES))
 
-    rates = [spread(misc, MISC + b) for b in range(GROUPS)]
+    def drawn(slot, to, odd):
+        tile = sum_ref[slot // 2 * ROWS : (slot // 2 + 1) * ROWS, :]
+        shifts = [2 * ROWS * (to - outer) + ROWS * (odd - slot % 2) for outer in (0, GROUPS - 1)]
+        return jnp.where(low, *(pltpu.roll(tile, shift % LANES, 1) if shift else tile for shift in shifts))
+
+    last = sum_ref[SUBSET - ROWS :, :]
+    pair = [jnp.where(folded == 0, pltpu.roll(last, LANES - ROWS, 1), 0.0), jnp.zeros((ROWS, LANES), F32)]
+    for n, (b, to) in enumerate(TUCKED):
+        here = (column_of == to) & (folded == b % 2)
+        pair[b // 2] = jnp.where(here, drawn(FIRST_TUCKED + n, to, b % 2), pair[b // 2])
+    square = jnp.concatenate(pair + [misc, jnp.zeros((LANES - 3 * ROWS, LANES), F32)], axis=0)
+    turned = jnp.transpose(square)
+
+    listed = turned[:ROWS] * (1.0 / copies)
+    spare = GROUPS * ROWS // 2
+    rates = [jnp.where(low, spread(listed, spare + GROUPS + b), spread(listed, spare + GROUPS - 1 - b)) for b in range(GROUPS)]
     odds = [rate / (1.0 - rate) for rate in rates]
     inverse = 1.0 / panel_size
     ahead = []
@@ -402,13 +438,10 @@
         ahead.append(jnp.concatenate([odds[b][1:, :], following], axis=0) * inverse)
     behind = [odd * inverse for odd in odds]
 
-    pair = sum_ref[...]
     trail_tiles = []
     for q in range(GROUPS // 2):
         factor = jnp.where(folded == 0, behind[2 * q], behind[2 * q + 1])
-        trail_tiles.append(pair[q * ROWS : (q + 1) * ROWS] * factor)
-    square = jnp.concatenate([pair, jnp.zeros((LANES - pair.shape[0], LANES), F32)], axis=0)
-    turned = jnp.transpose(square)
+        trail_tiles.append(pair[q] * factor)
 
     def turned_tile(h, b, f):
         at = h * HALF + b * 2 * ROWS + f * ROWS
@@ -448,10 +481,12 @@
     stay = [jnp.log(1.0 - rate) for rate in rates]
     stay[0] = jnp.where(row == 0, 0.0, stay[0])
     stay = jnp.sum(sum(stay), axis=0, keepdims=True)
-    counts = jnp.sum(misc, axis=0, keepdims=True)
+    marked = jnp.where(low, row, ROWS - 1 - row) >= GROUPS
     logs = []
-    for h, at in enumerate((MISC + GROUPS, HALF + MISC)):
-        seen = sum(counts[:, at + b : at + b + 1] for b in range(GROUPS))
+    for h in range(2):
+        cell = marked & (lane >= 2 * ROWS * (h + 1)) & (lane < 2 * ROWS * (h + 1) + ROWS)
+        seen = jnp.sum(jnp.where(cell, misc, 0.0), axis=0, keepdims=True)
+        seen = jnp.sum(seen, axis=1, keepdims=True) * (1.0 / copies)
         whole = jnp.log(v[0:1, h * HALF : h * HALF + 1]) + stay[:, 0:1] + seen * math.log(SCALE)
         logs.append(whole * (1.0 / MARKERS))
     log_ref[...] = jnp.concatenate(logs, axis=1)
@@ -484,33 +519,48 @@
         return (far_end - t) * side >= 0
 
     near = weights(low, place)
-    base = jnp.where(inward, SUBSET, 0)
+    outermost = weights(low, jnp.where(low, 0, GROUPS - 1))
+    inner = jnp.where(inward, 1.0, 0.0)
     total = jnp.zeros((ROWS, LANES), F32)
-    for q, (a0, a1) in enumerate(TRIANGLES):
-        a = jnp.where(folded == 0, a0, a1)
-        own = order <= a
-        paired = (a >= 0) & (a < 3)
-        moved = []
-        for each in (a0, a1):
-            if 0 <= each < 3:
-                moved.append(jnp.where(low, pltpu.roll(near, each + 1, 0), pltpu.roll(near, ROWS - 1 - each, 0)))
-            else:
-                moved.append(near)
-        weight = jnp.where(own, near, jnp.where(folded == 0, moved[0], moved[1])) * across
-        data = t_ref[pl.ds(pl.multiple_of(base + q * ROWS, ROWS), ROWS), :]
-        valid = (own | paired) & reaches(jnp.where(own, a, ROWS - 2 - a))
-        terms = jnp.where(valid, data * weight, 0.0)
-        one = jnp.sum(jnp.where(own, terms, 0.0), axis=0, keepdims=True)
-        other = jnp.sum(jnp.where(own, 0.0, terms), axis=0, keepdims=True)
-        total = total + jnp.where(row == a, one, 0.0)
-        total = total + jnp.where(paired & (row == ROWS - 2 - a), other, 0.0)
-    outermost = weights(low, jnp.where(low, 0, GROUPS - 1)) * jnp.where(inward, 1.0, 0.0) * across
+
+    def select(pair):
+        return pair[0] if pair[0] is pair[1] else jnp.where(folded == 0, *pair)
+
     for subset in range(2):
-        for q in range(ROWS // 4):
-            j = subset * ROWS // 2 + 2 * q + folded
-            at = subset * SUBSET + (len(TRIANGLES) + q) * ROWS
-            terms = jnp.where(reaches(j), t_ref[at : at + ROWS, :] * outermost, 0.0)
-            total = total + jnp.where(row == j, jnp.sum(terms, axis=0, keepdims=True), 0.0)
+        slots = SETS[subset] + [None]
+        for q in range(SUBSET // ROWS):
+            firsts, seconds, shared, moved = [], [], [], []
+            for entry in slots[2 * q : 2 * q + 2]:
+                if entry is None:
+                    firsts.append(-1)
+                    seconds.append(-1)
+                    shared.append(near)
+                    moved.append(near)
+                    continue
+                shape, block, j = entry
+                paired = paired_with(shape, j)
+                used = inner if block else 1.0 - inner
+                weight = (near if shape == TRIANGLE else outermost) * used
+                firsts.append(j)
+                seconds.append(paired)
+                shared.append(weight)
+                if paired < 0:
+                    moved.append(weight)
+                else:
+                    moved.append(jnp.where(low, pltpu.roll(weight, j + 1, 0), pltpu.roll(weight, ROWS - 1 - j, 0)))
+            is_square = [entry is not None and entry[0] == SQUARE for entry in slots[2 * q : 2 * q + 2]]
+            ends = [ROWS - 1 if square else j for square, j in zip(is_square, firsts)]
+            a, second, end = (jnp.where(folded == 0, *pair) for pair in (firsts, seconds, ends))
+            own = order <= end
+            marker = jnp.where(own, a, second)
+            weight = jnp.where(own, select(shared), select(moved)) * across
+            at = subset * SUBSET + q * ROWS
+            terms = jnp.where((marker >= 0) & reaches(marker), t_ref[at : at + ROWS, :] * weight, 0.0)
+            one = jnp.sum(jnp.where(own, terms, 0.0), axis=0, keepdims=True)
+            total = total + jnp.where(row == a, one, 0.0)
+            if max(seconds) >= 0:
+                other = jnp.sum(jnp.where(own, 0.0, terms), axis=0, keepdims=True)
+                total = total + jnp.where(row == second, other, 0.0)
     doses = []
     for h in range(2):
         dose = jnp.sum(jnp.where(lane // HALF == h, total, 0.0), axis=1, keepdims=True)
@@ -575,12 +625,9 @@
         sums.append(
             pl.pallas_call(
                 functools.partial(window_kernel, min(256, part)),
-                out_shape=[
-                    jax.ShapeDtypeStruct((2, TALL, LANES), F32),
-                    jax.ShapeDtypeStruct((PAIRS, LANES), F32),
-                ],
+                out_shape=jax.ShapeDtypeStruct((2, TALL, LANES), F32),
                 in_specs=[VMEM] * (2 * GROUPS),
-                out_specs=[VMEM] * 2,
+                out_specs=VMEM,
                 scratch_shapes=[
                     pltpu.VMEM((MARKERS, part), jnp.int32),
                     pltpu.VMEM((MARKERS, LANES), jnp.int32),
@@ -592,19 +639,20 @@
                 name="windows",
             )(*pieces, *tags)
         )
-    sums_t, sums_e = (sum(each) for each in zip(*sums))
-
-    lane, row = iota(sums_e.shape, 1), iota(sums_e.shape, 0)
-    unused = (row < ROWS) & (lane % HALF >= MISC) & (lane % HALF < 2 * ROWS)
-    sums_e = jnp.where(unused, jnp.concatenate([misc, jnp.zeros_like(misc)], axis=0), sums_e)
-    sent = jnp.concatenate([sums_t.reshape(2 * TALL, LANES), sums_e], axis=0)
+    sums = sum(sums)
+    shape = (2, 2, SUBSET, LANES)
+    rows, lane = iota(shape, 2) - SPARE // 2 * ROWS, iota(shape, 3)
+    rows = jnp.where(iota(shape, 0) == 0, rows, ROWS - 1 - rows)
+    spare = (rows >= GROUPS) & (rows < ROWS) & (lane % (2 * ROWS) < ROWS)
+    misc = jnp.pad(misc, ((SPARE // 2 * ROWS, SUBSET - (SPARE // 2 + 1) * ROWS), (0, 0)))
+    sent = jnp.where(spare, misc, sums.reshape(shape)).reshape(2 * TALL, LANES)
     both = sent + exchange(sent, "group", 1)
     half = place // (GROUPS // 2)
     carried = is_odd(place ^ lax.axis_index("batch"))
 
     def part_of(which):
         start = (2 * which + carried) * SUBSET
-        return jnp.concatenate([lax.dynamic_slice_in_dim(both, start, SUBSET), both[2 * TALL :]], axis=0)
+        return lax.dynamic_slice_in_dim(both, start, SUBSET)
 
     core = copies
     kept = part_of(half) + exchange_flat(part_of(1 - half), 2 * core + core)
@@ -612,8 +660,7 @@
     while by < copies:
         kept = kept + exchange_flat(kept, by + core)
         by *= 2
-    mine = kept[:SUBSET]
-    theirs = exchange(mine, "group", 1)
+    theirs = exchange(kept, "group", 1)
     weights, logs = pl.pallas_call(
         functools.partial(solve_kernel, float(width * copies), float(copies)),
         out_shape=[
@@ -625,8 +672,8 @@
         compiler_params=pltpu.CompilerParams(vmem_limit_bytes=4 * 1024 * 1024),
         cost_estimate=pl.CostEstimate(flops=1000000, bytes_accessed=0, transcendentals=0),
         name="solve",
-    )(kept[SUBSET:])
-    whole = jnp.where(carried == 0, jnp.concatenate([mine, theirs], axis=0), jnp.concatenate([theirs, mine], axis=0))
+    )(kept)
+    whole = jnp.where(carried == 0, jnp.concatenate([kept, theirs], axis=0), jnp.concatenate([theirs, kept], axis=0))
     dosage = pl.pallas_call(
         contract_kernel,
         out_shape=jax.ShapeDtypeStruct((2, ROWS), F32),

time: 31.6 us -> 31.4 us (level)
  starting transfers between devices: 13.5 us -> 12.7 us
  local copies, waits for them, and re-layouts: 0.05 us -> 0.38 us
    ppermute x4, starting transfers between devices: 7.58 us -> 6.97 us  [exchange_flat(): lax.ppermute(x, ('group', 'batch'), [(i, i ^ by) for i in range(peers)])]
    iota x0 -> x6, local copies, waits for them, and re-layouts: none -> 0.33 us  [iota(): return lax.broadcasted_iota(jnp.int32, shape, axis)]
  transfers between devices with their start and end apart: 12 -> 12, of which waited for: 8 -> 8; matrix products, arithmetic and copies ran while one was open for 0% -> 1% of each run, Pallas kernels for 10% -> 11%
where the time goes in v6:
time: 31.4 us; the launch traced here: 31.2 us
  starting transfers between devices  12.7 us (40%)
  waiting for transfers between devices  10.1 us (32%)
  Pallas kernels  7.03 us (22%)
  between operations  0.77 us (2%)
  local copies, waits for them, and re-layouts  0.38 us (1%)
    ppermute x4, starting transfers between devices, exchange_flat(): lax.ppermute(x, ('group', 'batch'), [(i, i ^ by) for i in range(peers)])  6.97 us
    ppermute x4, waiting for transfers between devices, exchange_flat(): lax.ppermute(x, ('group', 'batch'), [(i, i ^ by) for i in range(peers)])  6.82 us
    ppermute x8, starting transfers between devices, exchange(): return lax.ppermute(x, axis, [(i, i ^ by) for i in range(peers)])  5.69 us
    pallas_call x2, Pallas kernels, on_device_windows(): pl.pallas_call(functools.partial(window_kernel, min(256, part)), out_shap...  3.79 us
    ppermute x8, waiting for transfers between devices, exchange(): return lax.ppermute(x, axis, [(i, i ^ by) for i in range(peers)])  3.31 us
    pallas_call x1, Pallas kernels, on_device_windows(): pl.pallas_call(functools.partial(solve_kernel, float(width * copies), flo...  1.38 us
    pallas_call x1, Pallas kernels, on_device_windows(): pl.pallas_call(functools.partial(pack_kernel, widths), out_shape=shapes +...  1.15 us
    pallas_call x1, Pallas kernels, on_device_windows(): pl.pallas_call(contract_kernel, out_shape=jax.ShapeDtypeStruct((2, ROWS),...  0.71 us
  transfers between devices with their start and end apart: 12, of which 8 were waited for; matrix products, arithmetic and copies ran while one was open for 1% of the time, Pallas kernels for 11%

profile of v6, /device:TPU:0, one launch (start us, length us, event | category | flops | bytes accessed | tf_op | source)
XLA Modules:
  0.0 31.2 jit_solution(14642697151810618944)
XLA Ops:
  0.6 1.1 %pack.1 = (s32[8,2432]{1,0:T(8,128)S(1)}, s32[8,2432]{1,0:T(8,128)S(1)}, s32[8,2432]{1,0:T(8,128)S(1)}, s32[8,2432]{1,0:T(8,128)S(1)}, s32[8,1792]{1,0:T(8,128)S...) custom-call(s32[2,8]{1,0:T(2,128)} %geno_ref.1, ...), custom_call_target="tpu_custom_call" | custom-call | tf_op jit(solution)/shard_map/pack/pallas_call | solution.py:599
  1.8 0.5 %collective-permute-start = (s32[8,2432]{1,0:T(8,128)S(1)}, s32[8,2432]{1,0:T(8,128)S(1)}, u32[]{:S(2)}, u32[]{:S(2)}) collective-permute-start(s32[8,2432]{1,0:T(8,128)S(1)} %get-tuple-element.22), channel_id=1, source_target_pairs={{0,8},{8,0},{16,24},{24,16},{1,9},{9,1},{17,25},{25,17},{2,10},{10... | collective-permute-start | bytes 233480 | tf_op jit(solution)/shard_map/ppermute | solution.py:573
  2.3 2.6 %collective-permute-start.1 = (s32[8,2432]{1,0:T(8,128)S(1)}, s32[8,2432]{1,0:T(8,128)S(1)}, u32[]{:S(2)}, u32[]{:S(2)}) collective-permute-start(s32[8,2432]{1,0:T(8,128)S(1)} %get-tuple-element.24), channel_id=1, source_target_pairs={{0,16},{8,24},{16,0},{24,8},{1,17},{9,25},{17,1},{25,9},{2,18},{10... | collective-permute-start | bytes 233480 | tf_op jit(solution)/shard_map/ppermute | solution.py:573
  4.9 0.1 collective-permute-start.2
  5.0 0.1 iota.42
  5.1 0.1 iota.45
  5.2 0.1 iota.37
  5.2 0.1 iota.38
  5.3 0.0 collective-permute-done
  5.4 0.2 collective-permute-start.3
  5.6 1.9 %collective-permute-start.4 = (s32[8,1792]{1,0:T(8,128)S(1)}, s32[8,1792]{1,0:T(8,128)S(1)}, u32[]{:S(2)}, u32[]{:S(2)}) collective-permute-start(s32[8,1792]{1,0:T(8,128)S(1)} %get-tuple-element.28), channel_id=1, source_target_pairs={{0,16},{8,24},{16,0},{24,8},{1,17},{9,25},{17,1},{25,9},{2,18},{10... | collective-permute-start | bytes 172040 | tf_op jit(solution)/shard_map/ppermute | solution.py:573
  7.5 0.3 collective-permute-done.1
  7.8 1.4 %collective-permute-done.2 = s32[8,2432]{1,0:T(8,128)S(1)} collective-permute-done((s32[8,2432]{1,0:T(8,128)S(1)}, s32[8,2432]{1,0:T(8,128)S(1)}, u32[]{:S(2)}, u32[]{:S(2)}) %collective-permute-start.2) | collective-permute-done | bytes 77856 | tf_op jit(solution)/shard_map/ppermute | solution.py:573
  9.2 2.1 %windows.2 = f32[2,80,128]{2,1,0:T(8,128)S(1)} custom-call(s32[8,2304]{1,0:T(8,128)S(1)} %slice.24.refs_0_, s32[8,2304]{1,0:T(8,128)S(1)} %slice.25.refs_1_, s32[8,2304]{1,0:T(8,128)S(1)} %slice.32.refs_2_, s32[8,2304]{1,0:T(8,128)S(1)} %slice.33.refs_3_, s32[8,128]{1,0:T(8,128)S(1)} %slice.28.refs_4_, s32[8,128]{1,0:T(8,128)S(1)} %slice.29.refs_5_, ...), custom_call_target="tpu_custom_call" | custom-call | flops 2073600000 | tf_op jit(solution)/shard_map/windows/pallas_call | solution.py:626
  11.3 0.0 collective-permute-done.3.refs_1_
  11.3 0.5 %collective-permute-done.5.refs_3_ = s32[8,1792]{1,0:T(8,128)S(1)} collective-permute-done((s32[8,1792]{1,0:T(8,128)S(1)}, s32[8,1792]{1,0:T(8,128)S(1)}, u32[]{:S(2)}, u32[]{:S(2)}) %collective-permute-start.5) | collective-permute-done | bytes 57376 | tf_op jit(solution)/shard_map/ppermute | solution.py:573
  11.8 1.7 %windows.3 = f32[2,80,128]{2,1,0:T(8,128)S(1)} custom-call(s32[8,1792]{1,0:T(8,128)S(1)} %get-tuple-element.26.refs_0_, s32[8,1792]{1,0:T(8,128)S(1)} %collective-permute-done.3.refs_1_, s32[8,1792]{1,0:T(8,128)S(1)} %collective-permute-done.4.refs_2_, s32[8,1792]{1,0:T(8,128)S(1)} %collective-permute-done.5.refs_3_, s32[8,128]{1,0:T(8,128)S(1)} %slice.28.refs_4_, ...), custom_call_target="tpu_custom_call" | custom-call | flops 1612800000 | tf_op jit(solution)/shard_map/windows/pallas_call | solution.py:626
  13.5 0.1 bitcast_select_fusion
  13.7 0.2 collective-permute-start.6
  13.8 1.2 %collective-permute-done.6 = f32[160,128]{1,0:T(8,128)S(1)} collective-permute-done((f32[160,128]{1,0:T(8,128)S(1)}, f32[160,128]{1,0:T(8,128)S(1)}, u32[]{:S(2)}, u32[]{:S(2)}) %collective-permute-start.6) | collective-permute-done | bytes 81952 | tf_op jit(solution)/shard_map/ppermute | solution.py:573
  15.0 1.5 %collective-permute-start.7 = (f32[40,128]{1,0:T(8,128)S(1)}, f32[40,128]{1,0:T(8,128)S(1)}, u32[]{:S(2)}, u32[]{:S(2)}) collective-permute-start(f32[40,128]{1,0:T(8,128)S(1)} %constant_dynamic-slice_fusion), channel_id=1, source_target_pairs={{0,24},{1,25},{2,26},{3,27},{4,28},{5,29},{6,30},{7,31},{8,16},{9,... | collective-permute-start | bytes 61448 | tf_op jit(solution)/shard_map/ppermute | solution.py:578
  16.6 1.7 %collective-permute-done.7 = f32[40,128]{1,0:T(8,128)S(1)} collective-permute-done((f32[40,128]{1,0:T(8,128)S(1)}, f32[40,128]{1,0:T(8,128)S(1)}, u32[]{:S(2)}, u32[]{:S(2)}) %collective-permute-start.7) | collective-permute-done | bytes 20512 | tf_op jit(solution)/shard_map/ppermute | solution.py:578
  18.3 1.4 %collective-permute-start.8 = (f32[40,128]{1,0:T(8,128)S(1)}, f32[40,128]{1,0:T(8,128)S(1)}, u32[]{:S(2)}, u32[]{:S(2)}) collective-permute-start(f32[40,128]{1,0:T(8,128)S(1)} %dynamic-slice_add_fusion), channel_id=1, source_target_pairs={{0,9},{1,8},{2,11},{3,10},{4,13},{5,12},{6,15},{7,14},{8,1},{9,0},... | collective-permute-start | bytes 61448 | tf_op jit(solution)/shard_map/ppermute | solution.py:578
  19.8 1.8 %collective-permute-done.8 = f32[40,128]{1,0:T(8,128)S(1)} collective-permute-done((f32[40,128]{1,0:T(8,128)S(1)}, f32[40,128]{1,0:T(8,128)S(1)}, u32[]{:S(2)}, u32[]{:S(2)}) %collective-permute-start.8) | collective-permute-done | bytes 20512 | tf_op jit(solution)/shard_map/ppermute | solution.py:578
  21.5 1.5 %collective-permute-start.9 = (f32[40,128]{1,0:T(8,128)S(1)}, f32[40,128]{1,0:T(8,128)S(1)}, u32[]{:S(2)}, u32[]{:S(2)}) collective-permute-start(f32[40,128]{1,0:T(8,128)S(1)} %add.50), channel_id=1, source_target_pairs={{0,10},{1,11},{2,8},{3,9},{4,14},{5,15},{6,12},{7,13},{8,2},{9,3},... | collective-permute-start | bytes 61448 | tf_op jit(solution)/shard_map/ppermute | solution.py:578
  23.0 1.7 %collective-permute-done.9 = f32[40,128]{1,0:T(8,128)S(1)} collective-permute-done((f32[40,128]{1,0:T(8,128)S(1)}, f32[40,128]{1,0:T(8,128)S(1)}, u32[]{:S(2)}, u32[]{:S(2)}) %collective-permute-start.9) | collective-permute-done | bytes 20512 | tf_op jit(solution)/shard_map/ppermute | solution.py:578
  24.7 2.5 %collective-permute-start.10 = (f32[40,128]{1,0:T(8,128)S(1)}, f32[40,128]{1,0:T(8,128)S(1)}, u32[]{:S(2)}, u32[]{:S(2)}) collective-permute-start(f32[40,128]{1,0:T(8,128)S(1)} %add.51), channel_id=1, source_target_pairs={{0,12},{1,13},{2,14},{3,15},{4,8},{5,9},{6,10},{7,11},{8,4},{9,5},... | collective-permute-start | bytes 61448 | tf_op jit(solution)/shard_map/ppermute | solution.py:578
  27.3 1.6 %collective-permute-done.10 = f32[40,128]{1,0:T(8,128)S(1)} collective-permute-done((f32[40,128]{1,0:T(8,128)S(1)}, f32[40,128]{1,0:T(8,128)S(1)}, u32[]{:S(2)}, u32[]{:S(2)}) %collective-permute-start.10) | collective-permute-done | bytes 20512 | tf_op jit(solution)/shard_map/ppermute | solution.py:578
  28.9 0.2 collective-permute-start.11
  29.1 1.4 %solve.1 = (f32[72,128]{1,0:T(8,128)S(1)}, f32[1,2]{1,0:T(1,128)}) custom-call(f32[40,128]{1,0:T(8,128)S(1)} %add.52.sum_ref), custom_call_target="tpu_custom_call" | custom-call | flops 1000000 | tf_op jit(solution)/shard_map/solve/pallas_call | solution.py:664
  30.5 0.0 collective-permute-done.11
  30.5 0.7 %contract.1 = f32[2,8]{1,0:T(2,128)} custom-call(f32[72,128]{1,0:T(8,128)S(1)} %get-tuple-element.30.weight_ref, f32[80,128]{1,0:T(8,128)S(1)} %maximum_select_fusion.t_ref), custom_call_target="tpu_custom_call" | custom-call | tf_op jit(solution)/shard_map/contract/pallas_call | solution.py:677
  (26 shorter events, 0.1 us)
Async XLA Ops:
  1.8 3.6 %collective-permute-start = (s32[8,2432]{1,0:T(8,128)S(1)}, s32[8,2432]{1,0:T(8,128)S(1)}, u32[]{:S(2)}, u32[]{:S(2)}) collective-permute-start(s32[8,2432]{1,0:T(8,128)S(1)} %get-tuple-element.22), channel_id=1, source_target_pairs={{0,8},{8,0},{16,24},{24,16},{1,9},{9,1},{17,25},{25,17},{2,10},{10... | collective-permute-start | bytes 233480 | tf_op jit(solution)/shard_map/ppermute | solution.py:573
  2.3 5.5 %collective-permute-start.1 = (s32[8,2432]{1,0:T(8,128)S(1)}, s32[8,2432]{1,0:T(8,128)S(1)}, u32[]{:S(2)}, u32[]{:S(2)}) collective-permute-start(s32[8,2432]{1,0:T(8,128)S(1)} %get-tuple-element.24), channel_id=1, source_target_pairs={{0,16},{8,24},{16,0},{24,8},{1,17},{9,25},{17,1},{25,9},{2,18},{10... | collective-permute-start | bytes 233480 | tf_op jit(solution)/shard_map/ppermute | solution.py:573
  4.9 4.3 %collective-permute-start.2 = (s32[8,2432]{1,0:T(8,128)S(1)}, s32[8,2432]{1,0:T(8,128)S(1)}, u32[]{:S(2)}, u32[]{:S(2)}) collective-permute-start(s32[8,2432]{1,0:T(8,128)S(1)} %get-tuple-element.25), channel_id=1, source_target_pairs={{0,24},{8,16},{16,8},{24,0},{1,25},{9,17},{17,9},{25,1},{2,26},{10... | collective-permute-start | bytes 233480 | tf_op jit(solution)/shard_map/ppermute | solution.py:573
  5.4 5.9 %collective-permute-start.3 = (s32[8,1792]{1,0:T(8,128)S(1)}, s32[8,1792]{1,0:T(8,128)S(1)}, u32[]{:S(2)}, u32[]{:S(2)}) collective-permute-start(s32[8,1792]{1,0:T(8,128)S(1)} %get-tuple-element.27), channel_id=1, source_target_pairs={{0,8},{8,0},{16,24},{24,16},{1,9},{9,1},{17,25},{25,17},{2,10},{10... | collective-permute-start | bytes 172040 | tf_op jit(solution)/shard_map/ppermute | solution.py:573
  5.6 5.7 %collective-permute-start.4 = (s32[8,1792]{1,0:T(8,128)S(1)}, s32[8,1792]{1,0:T(8,128)S(1)}, u32[]{:S(2)}, u32[]{:S(2)}) collective-permute-start(s32[8,1792]{1,0:T(8,128)S(1)} %get-tuple-element.28), channel_id=1, source_target_pairs={{0,16},{8,24},{16,0},{24,8},{1,17},{9,25},{17,1},{25,9},{2,18},{10... | collective-permute-start | bytes 172040 | tf_op jit(solution)/shard_map/ppermute | solution.py:573
  7.5 4.3 %collective-permute-start.5 = (s32[8,1792]{1,0:T(8,128)S(1)}, s32[8,1792]{1,0:T(8,128)S(1)}, u32[]{:S(2)}, u32[]{:S(2)}) collective-permute-start(s32[8,1792]{1,0:T(8,128)S(1)} %get-tuple-element.29), channel_id=1, source_target_pairs={{0,24},{8,16},{16,8},{24,0},{1,25},{9,17},{17,9},{25,1},{2,26},{10... | collective-permute-start | bytes 172040 | tf_op jit(solution)/shard_map/ppermute | solution.py:573
  13.7 1.3 %collective-permute-start.6 = (f32[160,128]{1,0:T(8,128)S(1)}, f32[160,128]{1,0:T(8,128)S(1)}, u32[]{:S(2)}, u32[]{:S(2)}) collective-permute-start(f32[160,128]{1,0:T(8,128)S(1)} %bitcast_select_fusion), channel_id=1, source_target_pairs={{0,8},{8,0},{16,24},{24,16},{1,9},{9,1},{17,25},{25,17},{2,10},{10... | collective-permute-start | bytes 245768 | tf_op jit(solution)/shard_map/ppermute | solution.py:573
  15.0 3.3 %collective-permute-start.7 = (f32[40,128]{1,0:T(8,128)S(1)}, f32[40,128]{1,0:T(8,128)S(1)}, u32[]{:S(2)}, u32[]{:S(2)}) collective-permute-start(f32[40,128]{1,0:T(8,128)S(1)} %constant_dynamic-slice_fusion), channel_id=1, source_target_pairs={{0,24},{1,25},{2,26},{3,27},{4,28},{5,29},{6,30},{7,31},{8,16},{9,... | collective-permute-start | bytes 61448 | tf_op jit(solution)/shard_map/ppermute | solution.py:578
  18.3 3.2 %collective-permute-start.8 = (f32[40,128]{1,0:T(8,128)S(1)}, f32[40,128]{1,0:T(8,128)S(1)}, u32[]{:S(2)}, u32[]{:S(2)}) collective-permute-start(f32[40,128]{1,0:T(8,128)S(1)} %dynamic-slice_add_fusion), channel_id=1, source_target_pairs={{0,9},{1,8},{2,11},{3,10},{4,13},{5,12},{6,15},{7,14},{8,1},{9,0},... | collective-permute-start | bytes 61448 | tf_op jit(solution)/shard_map/ppermute | solution.py:578
  21.5 3.2 %collective-permute-start.9 = (f32[40,128]{1,0:T(8,128)S(1)}, f32[40,128]{1,0:T(8,128)S(1)}, u32[]{:S(2)}, u32[]{:S(2)}) collective-permute-start(f32[40,128]{1,0:T(8,128)S(1)} %add.50), channel_id=1, source_target_pairs={{0,10},{1,11},{2,8},{3,9},{4,14},{5,15},{6,12},{7,13},{8,2},{9,3},... | collective-permute-start | bytes 61448 | tf_op jit(solution)/shard_map/ppermute | solution.py:578
  24.7 4.1 %collective-permute-start.10 = (f32[40,128]{1,0:T(8,128)S(1)}, f32[40,128]{1,0:T(8,128)S(1)}, u32[]{:S(2)}, u32[]{:S(2)}) collective-permute-start(f32[40,128]{1,0:T(8,128)S(1)} %add.51), channel_id=1, source_target_pairs={{0,12},{1,13},{2,14},{3,15},{4,8},{5,9},{6,10},{7,11},{8,4},{9,5},... | collective-permute-start | bytes 61448 | tf_op jit(solution)/shard_map/ppermute | solution.py:578
  28.9 1.6 %collective-permute-start.11 = (f32[40,128]{1,0:T(8,128)S(1)}, f32[40,128]{1,0:T(8,128)S(1)}, u32[]{:S(2)}, u32[]{:S(2)}) collective-permute-start(f32[40,128]{1,0:T(8,128)S(1)} %add.52.sum_ref), channel_id=1, source_target_pairs={{0,8},{8,0},{16,24},{24,16},{1,9},{9,1},{17,25},{25,17},{2,10},{10... | collective-permute-start | bytes 61448 | tf_op jit(solution)/shard_map/ppermute | solution.py:573

commit v7 on v6

--- a/solution.py
+++ b/solution.py
@@ -295,9 +295,9 @@
         copy.wait()
 
 
-def window_kernel(step, *refs):
+def window_kernel(step, has_misc, *refs):
     pieces, geno_refs = refs[:GROUPS], refs[GROUPS : 2 * GROUPS]
-    t_ref, panel, genos, wide, left = refs[2 * GROUPS :]
+    misc_ref, t_ref, panel, genos, wide, left = refs[2 * GROUPS :]
     place = lax.axis_index("group")
     columns = panel.shape[1]
     for d in range(GROUPS):
@@ -380,6 +380,8 @@
         tile = tile + pltpu.roll(tile, LANES - ROWS, 1)
         return tile if shift == 0 else pltpu.roll(tile, shift % LANES, 1)
 
+    row = iota((ROWS, LANES), 0)
+    misc = misc_ref[...] if has_misc else jnp.zeros((ROWS, LANES), F32)
     sums_e = product(wide[1], wide[0])
     plain = [both_targets(sums_e, [b, GROUPS + b]) for b in range(GROUPS)]
     column = (lane % HALF) // (2 * ROWS)
@@ -399,11 +401,14 @@
                 value = fold(tiles[2 * q], tiles[2 * q + 1])
                 for here, moved in tucked.get(q, []):
                     value = jnp.where(here, moved, value)
+                if q == SPARE // 2:
+                    spare = row >= GROUPS if half == 0 else row < GROUPS
+                    value = jnp.where(spare & first, misc, value)
                 at = subset * SUBSET + q * ROWS
                 t_ref[half, at : at + ROWS, :] = value
 
 
-def solve_kernel(panel_size, copies, sum_ref, ends_ref, log_ref):
+def solve_kernel(panel_size, copies, sum_ref, ends_ref):
     low = lax.axis_index("group") < GROUPS // 2
     row, lane = iota((ROWS, LANES), 0), iota((ROWS, LANES), 1)
     target = lane // HALF
@@ -476,7 +481,6 @@
     for b in range(GROUPS):
         ends_ref[b * ROWS : (b + 1) * ROWS, :] = starts[b]
         ends_ref[MARKERS + b * ROWS : MARKERS + (b + 1) * ROWS, :] = ends[b]
-    ends_ref[2 * MARKERS :, :] = inverse / v
 
     stay = [jnp.log(1.0 - rate) for rate in rates]
     stay[0] = jnp.where(row == 0, 0.0, stay[0])
@@ -489,10 +493,10 @@
         seen = jnp.sum(seen, axis=1, keepdims=True) * (1.0 / copies)
         whole = jnp.log(v[0:1, h * HALF : h * HALF + 1]) + stay[:, 0:1] + seen * math.log(SCALE)
         logs.append(whole * (1.0 / MARKERS))
-    log_ref[...] = jnp.concatenate(logs, axis=1)
-
-
-def contract_kernel(weight_ref, t_ref, dose_ref):
+    ends_ref[2 * MARKERS :, :] = jnp.where(row == 0, inverse / v, jnp.where(target == 0, *logs))
+
+
+def contract_kernel(weight_ref, t_ref, dose_ref, log_ref):
     place = lax.axis_index("group")
     low = place < GROUPS // 2
     inward = (place == 1) | (place == GROUPS - 2)
@@ -566,6 +570,8 @@
         dose = jnp.sum(jnp.where(lane // HALF == h, total, 0.0), axis=1, keepdims=True)
         doses.append(jnp.sum(jnp.where(order == lane, dose, 0.0), axis=0, keepdims=True))
     dose_ref[...] = jnp.concatenate(doses, axis=0)[:, :ROWS]
+    logs = weight_ref[2 * MARKERS + 1 : 2 * MARKERS + 2, :]
+    log_ref[...] = jnp.concatenate([logs[:, :1], logs[:, HALF : HALF + 1]], axis=1)
 
 
 def exchange(x, axis, by):
@@ -624,9 +630,9 @@
         pieces = [cut[:, :part] for cut in cuts[p * GROUPS : (p + 1) * GROUPS]]
         sums.append(
             pl.pallas_call(
-                functools.partial(window_kernel, min(256, part)),
+                functools.partial(window_kernel, min(256, part), p == 0),
                 out_shape=jax.ShapeDtypeStruct((2, TALL, LANES), F32),
-                in_specs=[VMEM] * (2 * GROUPS),
+                in_specs=[VMEM] * (2 * GROUPS + 1),
                 out_specs=VMEM,
                 scratch_shapes=[
                     pltpu.VMEM((MARKERS, part), jnp.int32),
@@ -637,15 +643,10 @@
                 compiler_params=pltpu.CompilerParams(vmem_limit_bytes=40 * 1024 * 1024),
                 cost_estimate=pl.CostEstimate(flops=part * 900000, bytes_accessed=0, transcendentals=0),
                 name="windows",
-            )(*pieces, *tags)
+            )(*pieces, *tags, misc)
         )
     sums = sum(sums)
-    shape = (2, 2, SUBSET, LANES)
-    rows, lane = iota(shape, 2) - SPARE // 2 * ROWS, iota(shape, 3)
-    rows = jnp.where(iota(shape, 0) == 0, rows, ROWS - 1 - rows)
-    spare = (rows >= GROUPS) & (rows < ROWS) & (lane % (2 * ROWS) < ROWS)
-    misc = jnp.pad(misc, ((SPARE // 2 * ROWS, SUBSET - (SPARE // 2 + 1) * ROWS), (0, 0)))
-    sent = jnp.where(spare, misc, sums.reshape(shape)).reshape(2 * TALL, LANES)
+    sent = sums.reshape(2 * TALL, LANES)
     both = sent + exchange(sent, "group", 1)
     half = place // (GROUPS // 2)
     carried = is_odd(place ^ lax.axis_index("batch"))
@@ -661,24 +662,21 @@
         kept = kept + exchange_flat(kept, by + core)
         by *= 2
     theirs = exchange(kept, "group", 1)
-    weights, logs = pl.pallas_call(
+    weights = pl.pallas_call(
         functools.partial(solve_kernel, float(width * copies), float(copies)),
-        out_shape=[
-            jax.ShapeDtypeStruct((2 * MARKERS + ROWS, LANES), F32),
-            jax.ShapeDtypeStruct((1, 2), F32),
-        ],
+        out_shape=jax.ShapeDtypeStruct((2 * MARKERS + ROWS, LANES), F32),
         in_specs=[VMEM],
-        out_specs=[VMEM] * 2,
+        out_specs=VMEM,
         compiler_params=pltpu.CompilerParams(vmem_limit_bytes=4 * 1024 * 1024),
         cost_estimate=pl.CostEstimate(flops=1000000, bytes_accessed=0, transcendentals=0),
         name="solve",
     )(kept)
     whole = jnp.where(carried == 0, jnp.concatenate([kept, theirs], axis=0), jnp.concatenate([theirs, kept], axis=0))
-    dosage = pl.pallas_call(
+    dosage, logs = pl.pallas_call(
         contract_kernel,
-        out_shape=jax.ShapeDtypeStruct((2, ROWS), F32),
+        out_shape=[jax.ShapeDtypeStruct((2, ROWS), F32), jax.ShapeDtypeStruct((1, 2), F32)],
         in_specs=[VMEM] * 2,
-        out_specs=VMEM,
+        out_specs=[VMEM] * 2,
         compiler_params=pltpu.CompilerParams(vmem_limit_bytes=4 * 1024 * 1024),
         name="contract",
     )(weights, whole)

time: 31.4 us -> 30.8 us (0.981)
  starting transfers between devices: 12.7 us -> 13.5 us
  Pallas kernels: 7.03 us -> 6.55 us
  waiting for transfers between devices: 10.1 us -> 9.69 us
  local copies, waits for them, and re-layouts: 0.38 us -> 0.04 us
    ppermute x4, starting transfers between devices: 6.97 us -> 7.63 us  [exchange_flat(): lax.ppermute(x, ('group', 'batch'), [(i, i ^ by) for i in range(peers)])]
    ppermute x4, waiting for transfers between devices: 6.82 us -> 6.22 us  [exchange_flat(): lax.ppermute(x, ('group', 'batch'), [(i, i ^ by) for i in range(peers)])]
    pallas_call x1, Pallas kernels: 1.38 us -> 0.92 us  [on_device_windows(): pl.pallas_call(functools.partial(solve_kernel, float(width * copies), flo...]
    iota x6 -> x0, local copies, waits for them, and re-layouts: 0.33 us -> none  [iota(): return lax.broadcasted_iota(jnp.int32, shape, axis)]
  transfers between devices with their start and end apart: 12 -> 12, of which waited for: 8 -> 8; matrix products, arithmetic and copies ran while one was open for 1% -> 0% of each run, Pallas kernels for 11% -> 10%
where the time goes in v7:
time: 30.8 us; the launch traced here: 30.6 us
  starting transfers between devices  13.5 us (44%)
  waiting for transfers between devices  9.69 us (31%)
  Pallas kernels  6.55 us (21%)
  between operations  0.74 us (2%)
    ppermute x4, starting transfers between devices, exchange_flat(): lax.ppermute(x, ('group', 'batch'), [(i, i ^ by) for i in range(peers)])  7.63 us
    ppermute x4, waiting for transfers between devices, exchange_flat(): lax.ppermute(x, ('group', 'batch'), [(i, i ^ by) for i in range(peers)])  6.22 us
    ppermute x8, starting transfers between devices, exchange(): return lax.ppermute(x, axis, [(i, i ^ by) for i in range(peers)])  5.88 us
    pallas_call x2, Pallas kernels, on_device_windows(): pl.pallas_call(functools.partial(window_kernel, min(256, part), p == 0),...  3.78 us
    ppermute x8, waiting for transfers between devices, exchange(): return lax.ppermute(x, axis, [(i, i ^ by) for i in range(peers)])  3.47 us
    pallas_call x1, Pallas kernels, on_device_windows(): pl.pallas_call(functools.partial(pack_kernel, widths), out_shape=shapes +...  1.15 us
    pallas_call x1, Pallas kernels, on_device_windows(): pl.pallas_call(functools.partial(solve_kernel, float(width * copies), flo...  0.92 us
    pallas_call x1, Pallas kernels, on_device_windows(): pl.pallas_call(contract_kernel, out_shape=[jax.ShapeDtypeStruct((2, ROWS)...  0.71 us
  transfers between devices with their start and end apart: 12, of which 8 were waited for; matrix products, arithmetic and copies ran while one was open for 0% of the time, Pallas kernels for 10%

profile of v7, /device:TPU:0, one launch (start us, length us, event | category | flops | bytes accessed | tf_op | source)
XLA Modules:
  0.0 30.6 jit_solution(6701275363041903640)
XLA Ops:
  0.6 1.1 %pack.1 = (s32[8,2432]{1,0:T(8,128)S(1)}, s32[8,2432]{1,0:T(8,128)S(1)}, s32[8,2432]{1,0:T(8,128)S(1)}, s32[8,2432]{1,0:T(8,128)S(1)}, s32[8,1792]{1,0:T(8,128)S...) custom-call(s32[2,8]{1,0:T(2,128)} %geno_ref.1, ...), custom_call_target="tpu_custom_call" | custom-call | tf_op jit(solution)/shard_map/pack/pallas_call | solution.py:605
  1.8 0.5 %collective-permute-start = (s32[8,2432]{1,0:T(8,128)S(1)}, s32[8,2432]{1,0:T(8,128)S(1)}, u32[]{:S(2)}, u32[]{:S(2)}) collective-permute-start(s32[8,2432]{1,0:T(8,128)S(1)} %get-tuple-element.21), channel_id=1, source_target_pairs={{0,8},{8,0},{16,24},{24,16},{1,9},{9,1},{17,25},{25,17},{2,10},{10... | collective-permute-start | bytes 233480 | tf_op jit(solution)/shard_map/ppermute | solution.py:579
  2.3 2.6 %collective-permute-start.1 = (s32[8,2432]{1,0:T(8,128)S(1)}, s32[8,2432]{1,0:T(8,128)S(1)}, u32[]{:S(2)}, u32[]{:S(2)}) collective-permute-start(s32[8,2432]{1,0:T(8,128)S(1)} %get-tuple-element.23), channel_id=1, source_target_pairs={{0,16},{8,24},{16,0},{24,8},{1,17},{9,25},{17,1},{25,9},{2,18},{10... | collective-permute-start | bytes 233480 | tf_op jit(solution)/shard_map/ppermute | solution.py:579
  4.9 0.1 collective-permute-start.2
  4.9 0.0 collective-permute-done
  5.0 0.2 collective-permute-start.3
  5.2 1.9 %collective-permute-start.4 = (s32[8,1792]{1,0:T(8,128)S(1)}, s32[8,1792]{1,0:T(8,128)S(1)}, u32[]{:S(2)}, u32[]{:S(2)}) collective-permute-start(s32[8,1792]{1,0:T(8,128)S(1)} %get-tuple-element.28), channel_id=1, source_target_pairs={{0,16},{8,24},{16,0},{24,8},{1,17},{9,25},{17,1},{25,9},{2,18},{10... | collective-permute-start | bytes 172040 | tf_op jit(solution)/shard_map/ppermute | solution.py:579
  7.1 0.0 collective-permute-start.5
  7.1 0.7 %collective-permute-done.1 = s32[8,2432]{1,0:T(8,128)S(1)} collective-permute-done((s32[8,2432]{1,0:T(8,128)S(1)}, s32[8,2432]{1,0:T(8,128)S(1)}, u32[]{:S(2)}, u32[]{:S(2)}) %collective-permute-start.1) | collective-permute-done | bytes 77856 | tf_op jit(solution)/shard_map/ppermute | solution.py:579
  7.8 1.4 %collective-permute-done.2 = s32[8,2432]{1,0:T(8,128)S(1)} collective-permute-done((s32[8,2432]{1,0:T(8,128)S(1)}, s32[8,2432]{1,0:T(8,128)S(1)}, u32[]{:S(2)}, u32[]{:S(2)}) %collective-permute-start.2) | collective-permute-done | bytes 77856 | tf_op jit(solution)/shard_map/ppermute | solution.py:579
  9.2 2.1 %windows.2 = f32[2,80,128]{2,1,0:T(8,128)S(1)} custom-call(s32[8,2304]{1,0:T(8,128)S(1)} %slice.24.refs_0_, s32[8,2304]{1,0:T(8,128)S(1)} %slice.25.refs_1_, s32[8,2304]{1,0:T(8,128)S(1)} %slice.32.refs_2_, s32[8,2304]{1,0:T(8,128)S(1)} %slice.33.refs_3_, s32[8,128]{1,0:T(8,128)S(1)} %slice.28.refs_4_, s32[8,128]{1,0:T(8,128)S(1)} %slice.29.refs_5_, ...), custom_call_target="tpu_custom_call" | custom-call | flops 2073600000 | tf_op jit(solution)/shard_map/windows/pallas_call | solution.py:632
  11.3 0.0 collective-permute-done.3.refs_1_
  11.3 0.0 collective-permute-done.4.refs_2_
  11.3 0.3 collective-permute-done.5.refs_3_
  11.6 1.7 %windows.3 = f32[2,80,128]{2,1,0:T(8,128)S(1)} custom-call(s32[8,1792]{1,0:T(8,128)S(1)} %get-tuple-element.26.refs_0_, s32[8,1792]{1,0:T(8,128)S(1)} %collective-permute-done.3.refs_1_, s32[8,1792]{1,0:T(8,128)S(1)} %collective-permute-done.4.refs_2_, s32[8,1792]{1,0:T(8,128)S(1)} %collective-permute-done.5.refs_3_, s32[8,128]{1,0:T(8,128)S(1)} %slice.28.refs_4_, ...), custom_call_target="tpu_custom_call" | custom-call | flops 1612800000 | tf_op jit(solution)/shard_map/windows/pallas_call | solution.py:632
  13.3 0.3 collective-permute-start.6
  13.6 1.1 %collective-permute-done.6 = f32[160,128]{1,0:T(8,128)S(1)} collective-permute-done((f32[160,128]{1,0:T(8,128)S(1)}, f32[160,128]{1,0:T(8,128)S(1)}, u32[]{:S(2)}, u32[]{:S(2)}) %collective-permute-start.6) | collective-permute-done | bytes 81952 | tf_op jit(solution)/shard_map/ppermute | solution.py:579
  14.7 1.7 %collective-permute-start.7 = (f32[40,128]{1,0:T(8,128)S(1)}, f32[40,128]{1,0:T(8,128)S(1)}, u32[]{:S(2)}, u32[]{:S(2)}) collective-permute-start(f32[40,128]{1,0:T(8,128)S(1)} %constant_dynamic-slice_fusion), channel_id=1, source_target_pairs={{0,24},{1,25},{2,26},{3,27},{4,28},{5,29},{6,30},{7,31},{8,16},{9,... | collective-permute-start | bytes 61448 | tf_op jit(solution)/shard_map/ppermute | solution.py:584
  16.4 1.6 %collective-permute-done.7 = f32[40,128]{1,0:T(8,128)S(1)} collective-permute-done((f32[40,128]{1,0:T(8,128)S(1)}, f32[40,128]{1,0:T(8,128)S(1)}, u32[]{:S(2)}, u32[]{:S(2)}) %collective-permute-start.7) | collective-permute-done | bytes 20512 | tf_op jit(solution)/shard_map/ppermute | solution.py:584
  18.0 1.6 %collective-permute-start.8 = (f32[40,128]{1,0:T(8,128)S(1)}, f32[40,128]{1,0:T(8,128)S(1)}, u32[]{:S(2)}, u32[]{:S(2)}) collective-permute-start(f32[40,128]{1,0:T(8,128)S(1)} %dynamic-slice_add_fusion), channel_id=1, source_target_pairs={{0,9},{1,8},{2,11},{3,10},{4,13},{5,12},{6,15},{7,14},{8,1},{9,0},... | collective-permute-start | bytes 61448 | tf_op jit(solution)/shard_map/ppermute | solution.py:584
  19.6 1.6 %collective-permute-done.8 = f32[40,128]{1,0:T(8,128)S(1)} collective-permute-done((f32[40,128]{1,0:T(8,128)S(1)}, f32[40,128]{1,0:T(8,128)S(1)}, u32[]{:S(2)}, u32[]{:S(2)}) %collective-permute-start.8) | collective-permute-done | bytes 20512 | tf_op jit(solution)/shard_map/ppermute | solution.py:584
  21.2 1.7 %collective-permute-start.9 = (f32[40,128]{1,0:T(8,128)S(1)}, f32[40,128]{1,0:T(8,128)S(1)}, u32[]{:S(2)}, u32[]{:S(2)}) collective-permute-start(f32[40,128]{1,0:T(8,128)S(1)} %add.38), channel_id=1, source_target_pairs={{0,10},{1,11},{2,8},{3,9},{4,14},{5,15},{6,12},{7,13},{8,2},{9,3},... | collective-permute-start | bytes 61448 | tf_op jit(solution)/shard_map/ppermute | solution.py:584
  22.9 1.5 %collective-permute-done.9 = f32[40,128]{1,0:T(8,128)S(1)} collective-permute-done((f32[40,128]{1,0:T(8,128)S(1)}, f32[40,128]{1,0:T(8,128)S(1)}, u32[]{:S(2)}, u32[]{:S(2)}) %collective-permute-start.9) | collective-permute-done | bytes 20512 | tf_op jit(solution)/shard_map/ppermute | solution.py:584
  24.4 2.7 %collective-permute-start.10 = (f32[40,128]{1,0:T(8,128)S(1)}, f32[40,128]{1,0:T(8,128)S(1)}, u32[]{:S(2)}, u32[]{:S(2)}) collective-permute-start(f32[40,128]{1,0:T(8,128)S(1)} %add.39), channel_id=1, source_target_pairs={{0,12},{1,13},{2,14},{3,15},{4,8},{5,9},{6,10},{7,11},{8,4},{9,5},... | collective-permute-start | bytes 61448 | tf_op jit(solution)/shard_map/ppermute | solution.py:584
  27.1 1.5 %collective-permute-done.10 = f32[40,128]{1,0:T(8,128)S(1)} collective-permute-done((f32[40,128]{1,0:T(8,128)S(1)}, f32[40,128]{1,0:T(8,128)S(1)}, u32[]{:S(2)}, u32[]{:S(2)}) %collective-permute-start.10) | collective-permute-done | bytes 20512 | tf_op jit(solution)/shard_map/ppermute | solution.py:584
  28.6 0.3 %collective-permute-start.11 = (f32[40,128]{1,0:T(8,128)S(1)}, f32[40,128]{1,0:T(8,128)S(1)}, u32[]{:S(2)}, u32[]{:S(2)}) collective-permute-start(f32[40,128]{1,0:T(8,128)S(1)} %add.40.sum_ref), channel_id=1, source_target_pairs={{0,8},{8,0},{16,24},{24,16},{1,9},{9,1},{17,25},{25,17},{2,10},{10... | collective-permute-start | bytes 61448 | tf_op jit(solution)/shard_map/ppermute | solution.py:579
  28.9 0.9 %solve.1.weight_ref = f32[72,128]{1,0:T(8,128)S(1)} custom-call(f32[40,128]{1,0:T(8,128)S(1)} %add.40.sum_ref), custom_call_target="tpu_custom_call" | custom-call | flops 1000000 | tf_op jit(solution)/shard_map/solve/pallas_call | solution.py:665
  29.9 0.0 collective-permute-done.11
  29.9 0.7 %contract.1 = (f32[2,8]{1,0:T(2,128)}, f32[1,2]{1,0:T(1,128)}) custom-call(f32[72,128]{1,0:T(8,128)S(1)} %solve.1.weight_ref, f32[80,128]{1,0:T(8,128)S(1)} %maximum_select_fusion.t_ref), custom_call_target="tpu_custom_call" | custom-call | tf_op jit(solution)/shard_map/contract/pallas_call | solution.py:675
  (16 shorter events, 0.1 us)
Async XLA Ops:
  1.8 3.2 %collective-permute-start = (s32[8,2432]{1,0:T(8,128)S(1)}, s32[8,2432]{1,0:T(8,128)S(1)}, u32[]{:S(2)}, u32[]{:S(2)}) collective-permute-start(s32[8,2432]{1,0:T(8,128)S(1)} %get-tuple-element.21), channel_id=1, source_target_pairs={{0,8},{8,0},{16,24},{24,16},{1,9},{9,1},{17,25},{25,17},{2,10},{10... | collective-permute-start | bytes 233480 | tf_op jit(solution)/shard_map/ppermute | solution.py:579
  2.3 5.5 %collective-permute-start.1 = (s32[8,2432]{1,0:T(8,128)S(1)}, s32[8,2432]{1,0:T(8,128)S(1)}, u32[]{:S(2)}, u32[]{:S(2)}) collective-permute-start(s32[8,2432]{1,0:T(8,128)S(1)} %get-tuple-element.23), channel_id=1, source_target_pairs={{0,16},{8,24},{16,0},{24,8},{1,17},{9,25},{17,1},{25,9},{2,18},{10... | collective-permute-start | bytes 233480 | tf_op jit(solution)/shard_map/ppermute | solution.py:579
  4.9 4.3 %collective-permute-start.2 = (s32[8,2432]{1,0:T(8,128)S(1)}, s32[8,2432]{1,0:T(8,128)S(1)}, u32[]{:S(2)}, u32[]{:S(2)}) collective-permute-start(s32[8,2432]{1,0:T(8,128)S(1)} %get-tuple-element.24), channel_id=1, source_target_pairs={{0,24},{8,16},{16,8},{24,0},{1,25},{9,17},{17,9},{25,1},{2,26},{10... | collective-permute-start | bytes 233480 | tf_op jit(solution)/shard_map/ppermute | solution.py:579
  5.0 6.3 %collective-permute-start.3 = (s32[8,1792]{1,0:T(8,128)S(1)}, s32[8,1792]{1,0:T(8,128)S(1)}, u32[]{:S(2)}, u32[]{:S(2)}) collective-permute-start(s32[8,1792]{1,0:T(8,128)S(1)} %get-tuple-element.27), channel_id=1, source_target_pairs={{0,8},{8,0},{16,24},{24,16},{1,9},{9,1},{17,25},{25,17},{2,10},{10... | collective-permute-start | bytes 172040 | tf_op jit(solution)/shard_map/ppermute | solution.py:579
  5.2 6.1 %collective-permute-start.4 = (s32[8,1792]{1,0:T(8,128)S(1)}, s32[8,1792]{1,0:T(8,128)S(1)}, u32[]{:S(2)}, u32[]{:S(2)}) collective-permute-start(s32[8,1792]{1,0:T(8,128)S(1)} %get-tuple-element.28), channel_id=1, source_target_pairs={{0,16},{8,24},{16,0},{24,8},{1,17},{9,25},{17,1},{25,9},{2,18},{10... | collective-permute-start | bytes 172040 | tf_op jit(solution)/shard_map/ppermute | solution.py:579
  7.1 4.5 %collective-permute-start.5 = (s32[8,1792]{1,0:T(8,128)S(1)}, s32[8,1792]{1,0:T(8,128)S(1)}, u32[]{:S(2)}, u32[]{:S(2)}) collective-permute-start(s32[8,1792]{1,0:T(8,128)S(1)} %get-tuple-element.29), channel_id=1, source_target_pairs={{0,24},{8,16},{16,8},{24,0},{1,25},{9,17},{17,9},{25,1},{2,26},{10... | collective-permute-start | bytes 172040 | tf_op jit(solution)/shard_map/ppermute | solution.py:579
  13.3 1.3 %collective-permute-start.6 = (f32[160,128]{1,0:T(8,128)S(1)}, f32[160,128]{1,0:T(8,128)S(1)}, u32[]{:S(2)}, u32[]{:S(2)}) collective-permute-start(f32[160,128]{1,0:T(8,128)S(1)} %bitcast.3), channel_id=1, source_target_pairs={{0,8},{8,0},{16,24},{24,16},{1,9},{9,1},{17,25},{25,17},{2,10},{10... | collective-permute-start | bytes 245768 | tf_op jit(solution)/shard_map/ppermute | solution.py:579
  14.7 3.3 %collective-permute-start.7 = (f32[40,128]{1,0:T(8,128)S(1)}, f32[40,128]{1,0:T(8,128)S(1)}, u32[]{:S(2)}, u32[]{:S(2)}) collective-permute-start(f32[40,128]{1,0:T(8,128)S(1)} %constant_dynamic-slice_fusion), channel_id=1, source_target_pairs={{0,24},{1,25},{2,26},{3,27},{4,28},{5,29},{6,30},{7,31},{8,16},{9,... | collective-permute-start | bytes 61448 | tf_op jit(solution)/shard_map/ppermute | solution.py:584
  18.0 3.2 %collective-permute-start.8 = (f32[40,128]{1,0:T(8,128)S(1)}, f32[40,128]{1,0:T(8,128)S(1)}, u32[]{:S(2)}, u32[]{:S(2)}) collective-permute-start(f32[40,128]{1,0:T(8,128)S(1)} %dynamic-slice_add_fusion), channel_id=1, source_target_pairs={{0,9},{1,8},{2,11},{3,10},{4,13},{5,12},{6,15},{7,14},{8,1},{9,0},... | collective-permute-start | bytes 61448 | tf_op jit(solution)/shard_map/ppermute | solution.py:584
  21.2 3.2 %collective-permute-start.9 = (f32[40,128]{1,0:T(8,128)S(1)}, f32[40,128]{1,0:T(8,128)S(1)}, u32[]{:S(2)}, u32[]{:S(2)}) collective-permute-start(f32[40,128]{1,0:T(8,128)S(1)} %add.38), channel_id=1, source_target_pairs={{0,10},{1,11},{2,8},{3,9},{4,14},{5,15},{6,12},{7,13},{8,2},{9,3},... | collective-permute-start | bytes 61448 | tf_op jit(solution)/shard_map/ppermute | solution.py:584
  24.4 4.2 %collective-permute-start.10 = (f32[40,128]{1,0:T(8,128)S(1)}, f32[40,128]{1,0:T(8,128)S(1)}, u32[]{:S(2)}, u32[]{:S(2)}) collective-permute-start(f32[40,128]{1,0:T(8,128)S(1)} %add.39), channel_id=1, source_target_pairs={{0,12},{1,13},{2,14},{3,15},{4,8},{5,9},{6,10},{7,11},{8,4},{9,5},... | collective-permute-start | bytes 61448 | tf_op jit(solution)/shard_map/ppermute | solution.py:584
  28.6 1.3 %collective-permute-start.11 = (f32[40,128]{1,0:T(8,128)S(1)}, f32[40,128]{1,0:T(8,128)S(1)}, u32[]{:S(2)}, u32[]{:S(2)}) collective-permute-start(f32[40,128]{1,0:T(8,128)S(1)} %add.40.sum_ref), channel_id=1, source_target_pairs={{0,8},{8,0},{16,24},{24,16},{1,9},{9,1},{17,25},{25,17},{2,10},{10... | collective-permute-start | bytes 61448 | tf_op jit(solution)/shard_map/ppermute | solution.py:579

commit v8 on v7

--- a/solution.py
+++ b/solution.py
@@ -226,11 +226,11 @@
 HALF = LANES // 2
 GROUPS = 4
 SHARES = (9, 7)
+STEP = 2 * LANES
 MISSING = 2
 SCALE = math.sqrt(MISMATCH * (1.0 - MISMATCH))
 HALF_STEP = 0.5 * math.log((1.0 - MISMATCH) / MISMATCH)
 VMEM = pl.BlockSpec(memory_space=pltpu.VMEM)
-SMEM = pl.BlockSpec(memory_space=pltpu.SMEM)
 F32, BF16 = jnp.float32, jnp.bfloat16
 
 
@@ -239,7 +239,6 @@
 
 
 MARKERS = ROWS * GROUPS
-HALF_T = MARKERS // 2
 SUBSET = 5 * ROWS
 TALL = 2 * SUBSET
 TRIANGLE, SQUARE = 0, 1
@@ -630,7 +629,7 @@
         pieces = [cut[:, :part] for cut in cuts[p * GROUPS : (p + 1) * GROUPS]]
         sums.append(
             pl.pallas_call(
-                functools.partial(window_kernel, min(256, part), p == 0),
+                functools.partial(window_kernel, STEP, p == 0),
                 out_shape=jax.ShapeDtypeStruct((2, TALL, LANES), F32),
                 in_specs=[VMEM] * (2 * GROUPS + 1),
                 out_specs=VMEM,
@@ -646,17 +645,16 @@
             )(*pieces, *tags, misc)
         )
     sums = sum(sums)
-    sent = sums.reshape(2 * TALL, LANES)
-    both = sent + exchange(sent, "group", 1)
+    sums = sums.reshape(2, 2, SUBSET, LANES)
     half = place // (GROUPS // 2)
     carried = is_odd(place ^ lax.axis_index("batch"))
 
-    def part_of(which):
-        start = (2 * which + carried) * SUBSET
-        return lax.dynamic_slice_in_dim(both, start, SUBSET)
-
+    def pick(array, index, axis):
+        return lax.dynamic_index_in_dim(array, index, axis, False)
+
+    both = pick(sums, carried, 1) + exchange(pick(sums, 1 - carried, 1), "group", 1)
     core = copies
-    kept = part_of(half) + exchange_flat(part_of(1 - half), 2 * core + core)
+    kept = pick(both, half, 0) + exchange_flat(pick(both, 1 - half, 0), 2 * core + core)
     by = 1
     while by < copies:
         kept = kept + exchange_flat(kept, by + core)
@@ -690,7 +688,7 @@
         and copies & (copies - 1) == 0
         and markers == ROWS
         and genotypes.shape[0] == 2
-        and width % (GROUPS * LANES * 32) == 0
+        and width % (GROUPS * sum(SHARES) * STEP) == 0
     )
 
 

time: 30.8 us -> 30.7 us (level)
  no operation moved by 1% of the time
where the time goes in v8:
time: 30.7 us; the launch traced here: 30.5 us
  starting transfers between devices  13.5 us (44%)
  waiting for transfers between devices  9.62 us (31%)
  Pallas kernels  6.55 us (21%)
  between operations  0.76 us (2%)
    ppermute x4, starting transfers between devices, exchange_flat(): lax.ppermute(x, ('group', 'batch'), [(i, i ^ by) for i in range(peers)])  7.62 us
    ppermute x4, waiting for transfers between devices, exchange_flat(): lax.ppermute(x, ('group', 'batch'), [(i, i ^ by) for i in range(peers)])  6.22 us
    ppermute x8, starting transfers between devices, exchange(): return lax.ppermute(x, axis, [(i, i ^ by) for i in range(peers)])  5.89 us
    pallas_call x2, Pallas kernels, on_device_windows(): pl.pallas_call(functools.partial(window_kernel, STEP, p == 0), out_shape=...  3.78 us
    ppermute x8, waiting for transfers between devices, exchange(): return lax.ppermute(x, axis, [(i, i ^ by) for i in range(peers)])  3.4 us
    pallas_call x1, Pallas kernels, on_device_windows(): pl.pallas_call(functools.partial(pack_kernel, widths), out_shape=shapes +...  1.15 us
    pallas_call x1, Pallas kernels, on_device_windows(): pl.pallas_call(functools.partial(solve_kernel, float(width * copies), flo...  0.92 us
    pallas_call x1, Pallas kernels, on_device_windows(): pl.pallas_call(contract_kernel, out_shape=[jax.ShapeDtypeStruct((2, ROWS)...  0.71 us
  transfers between devices with their start and end apart: 12, of which 8 were waited for; matrix products, arithmetic and copies ran while one was open for 0% of the time, Pallas kernels for 10%

profile of v8, /device:TPU:0, one launch (start us, length us, event | category | flops | bytes accessed | tf_op | source)
XLA Modules:
  0.0 30.5 jit_solution(3457277390492563235)
XLA Ops:
  0.6 1.1 %pack.1 = (s32[8,2432]{1,0:T(8,128)S(1)}, s32[8,2432]{1,0:T(8,128)S(1)}, s32[8,2432]{1,0:T(8,128)S(1)}, s32[8,2432]{1,0:T(8,128)S(1)}, s32[8,1792]{1,0:T(8,128)S...) custom-call(s32[2,8]{1,0:T(2,128)} %geno_ref.1, ...), custom_call_target="tpu_custom_call" | custom-call | tf_op jit(solution)/shard_map/pack/pallas_call | solution.py:604
  1.8 0.5 %collective-permute-start = (s32[8,2432]{1,0:T(8,128)S(1)}, s32[8,2432]{1,0:T(8,128)S(1)}, u32[]{:S(2)}, u32[]{:S(2)}) collective-permute-start(s32[8,2432]{1,0:T(8,128)S(1)} %get-tuple-element.21), channel_id=1, source_target_pairs={{0,8},{8,0},{16,24},{24,16},{1,9},{9,1},{17,25},{25,17},{2,10},{10... | collective-permute-start | bytes 233480 | tf_op jit(solution)/shard_map/ppermute | solution.py:578
  2.3 2.6 %collective-permute-start.1 = (s32[8,2432]{1,0:T(8,128)S(1)}, s32[8,2432]{1,0:T(8,128)S(1)}, u32[]{:S(2)}, u32[]{:S(2)}) collective-permute-start(s32[8,2432]{1,0:T(8,128)S(1)} %get-tuple-element.23), channel_id=1, source_target_pairs={{0,16},{8,24},{16,0},{24,8},{1,17},{9,25},{17,1},{25,9},{2,18},{10... | collective-permute-start | bytes 233480 | tf_op jit(solution)/shard_map/ppermute | solution.py:578
  4.9 0.1 collective-permute-start.2
  5.0 0.0 collective-permute-done
  5.0 0.2 collective-permute-start.3
  5.2 1.9 %collective-permute-start.4 = (s32[8,1792]{1,0:T(8,128)S(1)}, s32[8,1792]{1,0:T(8,128)S(1)}, u32[]{:S(2)}, u32[]{:S(2)}) collective-permute-start(s32[8,1792]{1,0:T(8,128)S(1)} %get-tuple-element.28), channel_id=1, source_target_pairs={{0,16},{8,24},{16,0},{24,8},{1,17},{9,25},{17,1},{25,9},{2,18},{10... | collective-permute-start | bytes 172040 | tf_op jit(solution)/shard_map/ppermute | solution.py:578
  7.1 0.0 collective-permute-start.5
  7.1 0.7 %collective-permute-done.1 = s32[8,2432]{1,0:T(8,128)S(1)} collective-permute-done((s32[8,2432]{1,0:T(8,128)S(1)}, s32[8,2432]{1,0:T(8,128)S(1)}, u32[]{:S(2)}, u32[]{:S(2)}) %collective-permute-start.1) | collective-permute-done | bytes 77856 | tf_op jit(solution)/shard_map/ppermute | solution.py:578
  7.8 1.4 %collective-permute-done.2 = s32[8,2432]{1,0:T(8,128)S(1)} collective-permute-done((s32[8,2432]{1,0:T(8,128)S(1)}, s32[8,2432]{1,0:T(8,128)S(1)}, u32[]{:S(2)}, u32[]{:S(2)}) %collective-permute-start.2) | collective-permute-done | bytes 77856 | tf_op jit(solution)/shard_map/ppermute | solution.py:578
  9.2 2.1 %windows.2 = f32[2,80,128]{2,1,0:T(8,128)S(1)} custom-call(s32[8,2304]{1,0:T(8,128)S(1)} %slice.24.refs_0_, s32[8,2304]{1,0:T(8,128)S(1)} %slice.25.refs_1_, s32[8,2304]{1,0:T(8,128)S(1)} %slice.32.refs_2_, s32[8,2304]{1,0:T(8,128)S(1)} %slice.33.refs_3_, s32[8,128]{1,0:T(8,128)S(1)} %slice.28.refs_4_, s32[8,128]{1,0:T(8,128)S(1)} %slice.29.refs_5_, ...), custom_call_target="tpu_custom_call" | custom-call | flops 2073600000 | tf_op jit(solution)/shard_map/windows/pallas_call | solution.py:631
  11.3 0.0 collective-permute-done.3.refs_1_
  11.3 0.0 collective-permute-done.4.refs_2_
  11.3 0.3 collective-permute-done.5.refs_3_
  11.6 1.7 %windows.3 = f32[2,80,128]{2,1,0:T(8,128)S(1)} custom-call(s32[8,1792]{1,0:T(8,128)S(1)} %get-tuple-element.26.refs_0_, s32[8,1792]{1,0:T(8,128)S(1)} %collective-permute-done.3.refs_1_, s32[8,1792]{1,0:T(8,128)S(1)} %collective-permute-done.4.refs_2_, s32[8,1792]{1,0:T(8,128)S(1)} %collective-permute-done.5.refs_3_, s32[8,128]{1,0:T(8,128)S(1)} %slice.28.refs_4_, ...), custom_call_target="tpu_custom_call" | custom-call | flops 1612800000 | tf_op jit(solution)/shard_map/windows/pallas_call | solution.py:631
  13.4 0.3 collective-permute-start.6
  13.6 1.0 %collective-permute-done.6 = f32[2,40,128]{2,1,0:T(8,128)S(1)} collective-permute-done((f32[2,40,128]{2,1,0:T(8,128)S(1)}, f32[2,40,128]{2,1,0:T(8,128)S(1)}, u32[]{:S(2)}, u32[]{:S(2)}) %collective-permute-start.6) | collective-permute-done | bytes 40992 | tf_op jit(solution)/shard_map/ppermute | solution.py:578
  14.7 1.7 %collective-permute-start.7 = (f32[40,128]{1,0:T(8,128)S(1)}, f32[40,128]{1,0:T(8,128)S(1)}, u32[]{:S(2)}, u32[]{:S(2)}) collective-permute-start(f32[40,128]{1,0:T(8,128)S(1)} %dynamic-slice_bitcast_fusion.1), channel_id=1, source_target_pairs={{0,24},{1,25},{2,26},{3,27},{4,28},{5,29},{6,30},{7,31},{8,16},{9,... | collective-permute-start | bytes 61448 | tf_op jit(solution)/shard_map/ppermute | solution.py:583
  16.4 1.6 %collective-permute-done.7 = f32[40,128]{1,0:T(8,128)S(1)} collective-permute-done((f32[40,128]{1,0:T(8,128)S(1)}, f32[40,128]{1,0:T(8,128)S(1)}, u32[]{:S(2)}, u32[]{:S(2)}) %collective-permute-start.7) | collective-permute-done | bytes 20512 | tf_op jit(solution)/shard_map/ppermute | solution.py:583
  18.0 1.6 %collective-permute-start.8 = (f32[40,128]{1,0:T(8,128)S(1)}, f32[40,128]{1,0:T(8,128)S(1)}, u32[]{:S(2)}, u32[]{:S(2)}) collective-permute-start(f32[40,128]{1,0:T(8,128)S(1)} %bitcast_add_fusion.1), channel_id=1, source_target_pairs={{0,9},{1,8},{2,11},{3,10},{4,13},{5,12},{6,15},{7,14},{8,1},{9,0},... | collective-permute-start | bytes 61448 | tf_op jit(solution)/shard_map/ppermute | solution.py:583
  19.6 1.6 %collective-permute-done.8 = f32[40,128]{1,0:T(8,128)S(1)} collective-permute-done((f32[40,128]{1,0:T(8,128)S(1)}, f32[40,128]{1,0:T(8,128)S(1)}, u32[]{:S(2)}, u32[]{:S(2)}) %collective-permute-start.8) | collective-permute-done | bytes 20512 | tf_op jit(solution)/shard_map/ppermute | solution.py:583
  21.2 1.7 %collective-permute-start.9 = (f32[40,128]{1,0:T(8,128)S(1)}, f32[40,128]{1,0:T(8,128)S(1)}, u32[]{:S(2)}, u32[]{:S(2)}) collective-permute-start(f32[40,128]{1,0:T(8,128)S(1)} %add.42), channel_id=1, source_target_pairs={{0,10},{1,11},{2,8},{3,9},{4,14},{5,15},{6,12},{7,13},{8,2},{9,3},... | collective-permute-start | bytes 61448 | tf_op jit(solution)/shard_map/ppermute | solution.py:583
  22.8 1.5 %collective-permute-done.9 = f32[40,128]{1,0:T(8,128)S(1)} collective-permute-done((f32[40,128]{1,0:T(8,128)S(1)}, f32[40,128]{1,0:T(8,128)S(1)}, u32[]{:S(2)}, u32[]{:S(2)}) %collective-permute-start.9) | collective-permute-done | bytes 20512 | tf_op jit(solution)/shard_map/ppermute | solution.py:583
  24.4 2.7 %collective-permute-start.10 = (f32[40,128]{1,0:T(8,128)S(1)}, f32[40,128]{1,0:T(8,128)S(1)}, u32[]{:S(2)}, u32[]{:S(2)}) collective-permute-start(f32[40,128]{1,0:T(8,128)S(1)} %add.43), channel_id=1, source_target_pairs={{0,12},{1,13},{2,14},{3,15},{4,8},{5,9},{6,10},{7,11},{8,4},{9,5},... | collective-permute-start | bytes 61448 | tf_op jit(solution)/shard_map/ppermute | solution.py:583
  27.1 1.5 %collective-permute-done.10 = f32[40,128]{1,0:T(8,128)S(1)} collective-permute-done((f32[40,128]{1,0:T(8,128)S(1)}, f32[40,128]{1,0:T(8,128)S(1)}, u32[]{:S(2)}, u32[]{:S(2)}) %collective-permute-start.10) | collective-permute-done | bytes 20512 | tf_op jit(solution)/shard_map/ppermute | solution.py:583
  28.5 0.3 %collective-permute-start.11 = (f32[40,128]{1,0:T(8,128)S(1)}, f32[40,128]{1,0:T(8,128)S(1)}, u32[]{:S(2)}, u32[]{:S(2)}) collective-permute-start(f32[40,128]{1,0:T(8,128)S(1)} %add.44.sum_ref), channel_id=1, source_target_pairs={{0,8},{8,0},{16,24},{24,16},{1,9},{9,1},{17,25},{25,17},{2,10},{10... | collective-permute-start | bytes 61448 | tf_op jit(solution)/shard_map/ppermute | solution.py:578
  28.9 0.9 %solve.1.weight_ref = f32[72,128]{1,0:T(8,128)S(1)} custom-call(f32[40,128]{1,0:T(8,128)S(1)} %add.44.sum_ref), custom_call_target="tpu_custom_call" | custom-call | flops 1000000 | tf_op jit(solution)/shard_map/solve/pallas_call | solution.py:663
  29.8 0.0 collective-permute-done.11
  29.8 0.7 %contract.1 = (f32[2,8]{1,0:T(2,128)}, f32[1,2]{1,0:T(1,128)}) custom-call(f32[72,128]{1,0:T(8,128)S(1)} %solve.1.weight_ref, f32[80,128]{1,0:T(8,128)S(1)} %maximum_select_fusion.t_ref), custom_call_target="tpu_custom_call" | custom-call | tf_op jit(solution)/shard_map/contract/pallas_call | solution.py:673
  (17 shorter events, 0.1 us)
Async XLA Ops:
  1.8 3.2 %collective-permute-start = (s32[8,2432]{1,0:T(8,128)S(1)}, s32[8,2432]{1,0:T(8,128)S(1)}, u32[]{:S(2)}, u32[]{:S(2)}) collective-permute-start(s32[8,2432]{1,0:T(8,128)S(1)} %get-tuple-element.21), channel_id=1, source_target_pairs={{0,8},{8,0},{16,24},{24,16},{1,9},{9,1},{17,25},{25,17},{2,10},{10... | collective-permute-start | bytes 233480 | tf_op jit(solution)/shard_map/ppermute | solution.py:578
  2.3 5.5 %collective-permute-start.1 = (s32[8,2432]{1,0:T(8,128)S(1)}, s32[8,2432]{1,0:T(8,128)S(1)}, u32[]{:S(2)}, u32[]{:S(2)}) collective-permute-start(s32[8,2432]{1,0:T(8,128)S(1)} %get-tuple-element.23), channel_id=1, source_target_pairs={{0,16},{8,24},{16,0},{24,8},{1,17},{9,25},{17,1},{25,9},{2,18},{10... | collective-permute-start | bytes 233480 | tf_op jit(solution)/shard_map/ppermute | solution.py:578
  4.9 4.3 %collective-permute-start.2 = (s32[8,2432]{1,0:T(8,128)S(1)}, s32[8,2432]{1,0:T(8,128)S(1)}, u32[]{:S(2)}, u32[]{:S(2)}) collective-permute-start(s32[8,2432]{1,0:T(8,128)S(1)} %get-tuple-element.24), channel_id=1, source_target_pairs={{0,24},{8,16},{16,8},{24,0},{1,25},{9,17},{17,9},{25,1},{2,26},{10... | collective-permute-start | bytes 233480 | tf_op jit(solution)/shard_map/ppermute | solution.py:578
  5.0 6.3 %collective-permute-start.3 = (s32[8,1792]{1,0:T(8,128)S(1)}, s32[8,1792]{1,0:T(8,128)S(1)}, u32[]{:S(2)}, u32[]{:S(2)}) collective-permute-start(s32[8,1792]{1,0:T(8,128)S(1)} %get-tuple-element.27), channel_id=1, source_target_pairs={{0,8},{8,0},{16,24},{24,16},{1,9},{9,1},{17,25},{25,17},{2,10},{10... | collective-permute-start | bytes 172040 | tf_op jit(solution)/shard_map/ppermute | solution.py:578
  5.2 6.1 %collective-permute-start.4 = (s32[8,1792]{1,0:T(8,128)S(1)}, s32[8,1792]{1,0:T(8,128)S(1)}, u32[]{:S(2)}, u32[]{:S(2)}) collective-permute-start(s32[8,1792]{1,0:T(8,128)S(1)} %get-tuple-element.28), channel_id=1, source_target_pairs={{0,16},{8,24},{16,0},{24,8},{1,17},{9,25},{17,1},{25,9},{2,18},{10... | collective-permute-start | bytes 172040 | tf_op jit(solution)/shard_map/ppermute | solution.py:578
  7.1 4.5 %collective-permute-start.5 = (s32[8,1792]{1,0:T(8,128)S(1)}, s32[8,1792]{1,0:T(8,128)S(1)}, u32[]{:S(2)}, u32[]{:S(2)}) collective-permute-start(s32[8,1792]{1,0:T(8,128)S(1)} %get-tuple-element.29), channel_id=1, source_target_pairs={{0,24},{8,16},{16,8},{24,0},{1,25},{9,17},{17,9},{25,1},{2,26},{10... | collective-permute-start | bytes 172040 | tf_op jit(solution)/shard_map/ppermute | solution.py:578
  13.4 1.3 %collective-permute-start.6 = (f32[2,40,128]{2,1,0:T(8,128)S(1)}, f32[2,40,128]{2,1,0:T(8,128)S(1)}, u32[]{:S(2)}, u32[]{:S(2)}) collective-permute-start(f32[2,40,128]{2,1,0:T(8,128)S(1)} %dynamic-slice_bitcast_fusion), channel_id=1, source_target_pairs={{0,8},{8,0},{16,24},{24,16},{1,9},{9,1},{17,25},{25,17},{2,10},{10... | collective-permute-start | bytes 122888 | tf_op jit(solution)/shard_map/ppermute | solution.py:578
  14.7 3.3 %collective-permute-start.7 = (f32[40,128]{1,0:T(8,128)S(1)}, f32[40,128]{1,0:T(8,128)S(1)}, u32[]{:S(2)}, u32[]{:S(2)}) collective-permute-start(f32[40,128]{1,0:T(8,128)S(1)} %dynamic-slice_bitcast_fusion.1), channel_id=1, source_target_pairs={{0,24},{1,25},{2,26},{3,27},{4,28},{5,29},{6,30},{7,31},{8,16},{9,... | collective-permute-start | bytes 61448 | tf_op jit(solution)/shard_map/ppermute | solution.py:583
  18.0 3.2 %collective-permute-start.8 = (f32[40,128]{1,0:T(8,128)S(1)}, f32[40,128]{1,0:T(8,128)S(1)}, u32[]{:S(2)}, u32[]{:S(2)}) collective-permute-start(f32[40,128]{1,0:T(8,128)S(1)} %bitcast_add_fusion.1), channel_id=1, source_target_pairs={{0,9},{1,8},{2,11},{3,10},{4,13},{5,12},{6,15},{7,14},{8,1},{9,0},... | collective-permute-start | bytes 61448 | tf_op jit(solution)/shard_map/ppermute | solution.py:583
  21.2 3.2 %collective-permute-start.9 = (f32[40,128]{1,0:T(8,128)S(1)}, f32[40,128]{1,0:T(8,128)S(1)}, u32[]{:S(2)}, u32[]{:S(2)}) collective-permute-start(f32[40,128]{1,0:T(8,128)S(1)} %add.42), channel_id=1, source_target_pairs={{0,10},{1,11},{2,8},{3,9},{4,14},{5,15},{6,12},{7,13},{8,2},{9,3},... | collective-permute-start | bytes 61448 | tf_op jit(solution)/shard_map/ppermute | solution.py:583
  24.4 4.2 %collective-permute-start.10 = (f32[40,128]{1,0:T(8,128)S(1)}, f32[40,128]{1,0:T(8,128)S(1)}, u32[]{:S(2)}, u32[]{:S(2)}) collective-permute-start(f32[40,128]{1,0:T(8,128)S(1)} %add.43), channel_id=1, source_target_pairs={{0,12},{1,13},{2,14},{3,15},{4,8},{5,9},{6,10},{7,11},{8,4},{9,5},... | collective-permute-start | bytes 61448 | tf_op jit(solution)/shard_map/ppermute | solution.py:583
  28.5 1.3 %collective-permute-start.11 = (f32[40,128]{1,0:T(8,128)S(1)}, f32[40,128]{1,0:T(8,128)S(1)}, u32[]{:S(2)}, u32[]{:S(2)}) collective-permute-start(f32[40,128]{1,0:T(8,128)S(1)} %add.44.sum_ref), channel_id=1, source_target_pairs={{0,8},{8,0},{16,24},{24,16},{1,9},{9,1},{17,25},{25,17},{2,10},{10... | collective-permute-start | bytes 61448 | tf_op jit(solution)/shard_map/ppermute | solution.py:578

commit v9 on v8

--- a/solution.py
+++ b/solution.py
@@ -655,10 +655,9 @@
     both = pick(sums, carried, 1) + exchange(pick(sums, 1 - carried, 1), "group", 1)
     core = copies
     kept = pick(both, half, 0) + exchange_flat(pick(both, 1 - half, 0), 2 * core + core)
-    by = 1
-    while by < copies:
+    bits = [1 << n for n in range(copies.bit_length() - 1)]
+    for by in bits[1:] + bits[:1]:
         kept = kept + exchange_flat(kept, by + core)
-        by *= 2
     theirs = exchange(kept, "group", 1)
     weights = pl.pallas_call(
         functools.partial(solve_kernel, float(width * copies), float(copies)),

time: 30.7 us -> 30.7 us (level)
  no operation moved by 1% of the time
where the time goes in v9:
time: 30.7 us; the launch traced here: 30.5 us
  starting transfers between devices  13.5 us (44%)
  waiting for transfers between devices  9.66 us (31%)
  Pallas kernels  6.55 us (21%)
  between operations  0.76 us (2%)
    ppermute x4, starting transfers between devices, exchange_flat(): lax.ppermute(x, ('group', 'batch'), [(i, i ^ by) for i in range(peers)])  7.57 us
    ppermute x4, waiting for transfers between devices, exchange_flat(): lax.ppermute(x, ('group', 'batch'), [(i, i ^ by) for i in range(peers)])  6.27 us
    ppermute x8, starting transfers between devices, exchange(): return lax.ppermute(x, axis, [(i, i ^ by) for i in range(peers)])  5.89 us
    pallas_call x2, Pallas kernels, on_device_windows(): pl.pallas_call(functools.partial(window_kernel, STEP, p == 0), out_shape=...  3.78 us
    ppermute x8, waiting for transfers between devices, exchange(): return lax.ppermute(x, axis, [(i, i ^ by) for i in range(peers)])  3.4 us
    pallas_call x1, Pallas kernels, on_device_windows(): pl.pallas_call(functools.partial(pack_kernel, widths), out_shape=shapes +...  1.15 us
    pallas_call x1, Pallas kernels, on_device_windows(): pl.pallas_call(functools.partial(solve_kernel, float(width * copies), flo...  0.92 us
    pallas_call x1, Pallas kernels, on_device_windows(): pl.pallas_call(contract_kernel, out_shape=[jax.ShapeDtypeStruct((2, ROWS)...  0.71 us
  transfers between devices with their start and end apart: 12, of which 8 were waited for; matrix products, arithmetic and copies ran while one was open for 0% of the time, Pallas kernels for 10%

profile of v9, /device:TPU:0, one launch (start us, length us, event | category | flops | bytes accessed | tf_op | source)
XLA Modules:
  0.0 30.5 jit_solution(6333356918682108373)
XLA Ops:
  0.6 1.1 %pack.1 = (s32[8,2432]{1,0:T(8,128)S(1)}, s32[8,2432]{1,0:T(8,128)S(1)}, s32[8,2432]{1,0:T(8,128)S(1)}, s32[8,2432]{1,0:T(8,128)S(1)}, s32[8,1792]{1,0:T(8,128)S...) custom-call(s32[2,8]{1,0:T(2,128)} %geno_ref.1, ...), custom_call_target="tpu_custom_call" | custom-call | tf_op jit(solution)/shard_map/pack/pallas_call | solution.py:604
  1.8 0.5 %collective-permute-start = (s32[8,2432]{1,0:T(8,128)S(1)}, s32[8,2432]{1,0:T(8,128)S(1)}, u32[]{:S(2)}, u32[]{:S(2)}) collective-permute-start(s32[8,2432]{1,0:T(8,128)S(1)} %get-tuple-element.21), channel_id=1, source_target_pairs={{0,8},{8,0},{16,24},{24,16},{1,9},{9,1},{17,25},{25,17},{2,10},{10... | collective-permute-start | bytes 233480 | tf_op jit(solution)/shard_map/ppermute | solution.py:578
  2.3 2.6 %collective-permute-start.1 = (s32[8,2432]{1,0:T(8,128)S(1)}, s32[8,2432]{1,0:T(8,128)S(1)}, u32[]{:S(2)}, u32[]{:S(2)}) collective-permute-start(s32[8,2432]{1,0:T(8,128)S(1)} %get-tuple-element.23), channel_id=1, source_target_pairs={{0,16},{8,24},{16,0},{24,8},{1,17},{9,25},{17,1},{25,9},{2,18},{10... | collective-permute-start | bytes 233480 | tf_op jit(solution)/shard_map/ppermute | solution.py:578
  4.9 0.1 collective-permute-start.2
  5.0 0.0 collective-permute-done
  5.0 0.2 collective-permute-start.3
  5.2 1.9 %collective-permute-start.4 = (s32[8,1792]{1,0:T(8,128)S(1)}, s32[8,1792]{1,0:T(8,128)S(1)}, u32[]{:S(2)}, u32[]{:S(2)}) collective-permute-start(s32[8,1792]{1,0:T(8,128)S(1)} %get-tuple-element.28), channel_id=1, source_target_pairs={{0,16},{8,24},{16,0},{24,8},{1,17},{9,25},{17,1},{25,9},{2,18},{10... | collective-permute-start | bytes 172040 | tf_op jit(solution)/shard_map/ppermute | solution.py:578
  7.1 0.0 collective-permute-start.5
  7.1 0.7 %collective-permute-done.1 = s32[8,2432]{1,0:T(8,128)S(1)} collective-permute-done((s32[8,2432]{1,0:T(8,128)S(1)}, s32[8,2432]{1,0:T(8,128)S(1)}, u32[]{:S(2)}, u32[]{:S(2)}) %collective-permute-start.1) | collective-permute-done | bytes 77856 | tf_op jit(solution)/shard_map/ppermute | solution.py:578
  7.8 1.4 %collective-permute-done.2 = s32[8,2432]{1,0:T(8,128)S(1)} collective-permute-done((s32[8,2432]{1,0:T(8,128)S(1)}, s32[8,2432]{1,0:T(8,128)S(1)}, u32[]{:S(2)}, u32[]{:S(2)}) %collective-permute-start.2) | collective-permute-done | bytes 77856 | tf_op jit(solution)/shard_map/ppermute | solution.py:578
  9.2 2.1 %windows.2 = f32[2,80,128]{2,1,0:T(8,128)S(1)} custom-call(s32[8,2304]{1,0:T(8,128)S(1)} %slice.24.refs_0_, s32[8,2304]{1,0:T(8,128)S(1)} %slice.25.refs_1_, s32[8,2304]{1,0:T(8,128)S(1)} %slice.32.refs_2_, s32[8,2304]{1,0:T(8,128)S(1)} %slice.33.refs_3_, s32[8,128]{1,0:T(8,128)S(1)} %slice.28.refs_4_, s32[8,128]{1,0:T(8,128)S(1)} %slice.29.refs_5_, ...), custom_call_target="tpu_custom_call" | custom-call | flops 2073600000 | tf_op jit(solution)/shard_map/windows/pallas_call | solution.py:631
  11.3 0.0 collective-permute-done.3.refs_1_
  11.3 0.0 collective-permute-done.4.refs_2_
  11.3 0.3 collective-permute-done.5.refs_3_
  11.6 1.7 %windows.3 = f32[2,80,128]{2,1,0:T(8,128)S(1)} custom-call(s32[8,1792]{1,0:T(8,128)S(1)} %get-tuple-element.26.refs_0_, s32[8,1792]{1,0:T(8,128)S(1)} %collective-permute-done.3.refs_1_, s32[8,1792]{1,0:T(8,128)S(1)} %collective-permute-done.4.refs_2_, s32[8,1792]{1,0:T(8,128)S(1)} %collective-permute-done.5.refs_3_, s32[8,128]{1,0:T(8,128)S(1)} %slice.28.refs_4_, ...), custom_call_target="tpu_custom_call" | custom-call | flops 1612800000 | tf_op jit(solution)/shard_map/windows/pallas_call | solution.py:631
  13.4 0.3 collective-permute-start.6
  13.6 1.0 %collective-permute-done.6 = f32[2,40,128]{2,1,0:T(8,128)S(1)} collective-permute-done((f32[2,40,128]{2,1,0:T(8,128)S(1)}, f32[2,40,128]{2,1,0:T(8,128)S(1)}, u32[]{:S(2)}, u32[]{:S(2)}) %collective-permute-start.6) | collective-permute-done | bytes 40992 | tf_op jit(solution)/shard_map/ppermute | solution.py:578
  14.7 1.7 %collective-permute-start.7 = (f32[40,128]{1,0:T(8,128)S(1)}, f32[40,128]{1,0:T(8,128)S(1)}, u32[]{:S(2)}, u32[]{:S(2)}) collective-permute-start(f32[40,128]{1,0:T(8,128)S(1)} %dynamic-slice_bitcast_fusion.1), channel_id=1, source_target_pairs={{0,24},{1,25},{2,26},{3,27},{4,28},{5,29},{6,30},{7,31},{8,16},{9,... | collective-permute-start | bytes 61448 | tf_op jit(solution)/shard_map/ppermute | solution.py:583
  16.4 1.6 %collective-permute-done.7 = f32[40,128]{1,0:T(8,128)S(1)} collective-permute-done((f32[40,128]{1,0:T(8,128)S(1)}, f32[40,128]{1,0:T(8,128)S(1)}, u32[]{:S(2)}, u32[]{:S(2)}) %collective-permute-start.7) | collective-permute-done | bytes 20512 | tf_op jit(solution)/shard_map/ppermute | solution.py:583
  18.0 1.7 %collective-permute-start.8 = (f32[40,128]{1,0:T(8,128)S(1)}, f32[40,128]{1,0:T(8,128)S(1)}, u32[]{:S(2)}, u32[]{:S(2)}) collective-permute-start(f32[40,128]{1,0:T(8,128)S(1)} %bitcast_add_fusion.1), channel_id=1, source_target_pairs={{0,10},{1,11},{2,8},{3,9},{4,14},{5,15},{6,12},{7,13},{8,2},{9,3},... | collective-permute-start | bytes 61448 | tf_op jit(solution)/shard_map/ppermute | solution.py:583
  19.6 1.5 %collective-permute-done.8 = f32[40,128]{1,0:T(8,128)S(1)} collective-permute-done((f32[40,128]{1,0:T(8,128)S(1)}, f32[40,128]{1,0:T(8,128)S(1)}, u32[]{:S(2)}, u32[]{:S(2)}) %collective-permute-start.8) | collective-permute-done | bytes 20512 | tf_op jit(solution)/shard_map/ppermute | solution.py:583
  21.2 2.7 %collective-permute-start.9 = (f32[40,128]{1,0:T(8,128)S(1)}, f32[40,128]{1,0:T(8,128)S(1)}, u32[]{:S(2)}, u32[]{:S(2)}) collective-permute-start(f32[40,128]{1,0:T(8,128)S(1)} %add.42), channel_id=1, source_target_pairs={{0,12},{1,13},{2,14},{3,15},{4,8},{5,9},{6,10},{7,11},{8,4},{9,5},... | collective-permute-start | bytes 61448 | tf_op jit(solution)/shard_map/ppermute | solution.py:583
  23.8 1.5 %collective-permute-done.9 = f32[40,128]{1,0:T(8,128)S(1)} collective-permute-done((f32[40,128]{1,0:T(8,128)S(1)}, f32[40,128]{1,0:T(8,128)S(1)}, u32[]{:S(2)}, u32[]{:S(2)}) %collective-permute-start.9) | collective-permute-done | bytes 20512 | tf_op jit(solution)/shard_map/ppermute | solution.py:583
  25.3 1.6 %collective-permute-start.10 = (f32[40,128]{1,0:T(8,128)S(1)}, f32[40,128]{1,0:T(8,128)S(1)}, u32[]{:S(2)}, u32[]{:S(2)}) collective-permute-start(f32[40,128]{1,0:T(8,128)S(1)} %add.43), channel_id=1, source_target_pairs={{0,9},{1,8},{2,11},{3,10},{4,13},{5,12},{6,15},{7,14},{8,1},{9,0},... | collective-permute-start | bytes 61448 | tf_op jit(solution)/shard_map/ppermute | solution.py:583
  26.9 1.7 %collective-permute-done.10 = f32[40,128]{1,0:T(8,128)S(1)} collective-permute-done((f32[40,128]{1,0:T(8,128)S(1)}, f32[40,128]{1,0:T(8,128)S(1)}, u32[]{:S(2)}, u32[]{:S(2)}) %collective-permute-start.10) | collective-permute-done | bytes 20512 | tf_op jit(solution)/shard_map/ppermute | solution.py:583
  28.5 0.3 %collective-permute-start.11 = (f32[40,128]{1,0:T(8,128)S(1)}, f32[40,128]{1,0:T(8,128)S(1)}, u32[]{:S(2)}, u32[]{:S(2)}) collective-permute-start(f32[40,128]{1,0:T(8,128)S(1)} %add.44.sum_ref), channel_id=1, source_target_pairs={{0,8},{8,0},{16,24},{24,16},{1,9},{9,1},{17,25},{25,17},{2,10},{10... | collective-permute-start | bytes 61448 | tf_op jit(solution)/shard_map/ppermute | solution.py:578
  28.9 0.9 %solve.1.weight_ref = f32[72,128]{1,0:T(8,128)S(1)} custom-call(f32[40,128]{1,0:T(8,128)S(1)} %add.44.sum_ref), custom_call_target="tpu_custom_call" | custom-call | flops 1000000 | tf_op jit(solution)/shard_map/solve/pallas_call | solution.py:662
  29.8 0.0 collective-permute-done.11
  29.8 0.7 %contract.1 = (f32[2,8]{1,0:T(2,128)}, f32[1,2]{1,0:T(1,128)}) custom-call(f32[72,128]{1,0:T(8,128)S(1)} %solve.1.weight_ref, f32[80,128]{1,0:T(8,128)S(1)} %maximum_select_fusion.t_ref), custom_call_target="tpu_custom_call" | custom-call | tf_op jit(solution)/shard_map/contract/pallas_call | solution.py:672
  (17 shorter events, 0.1 us)
Async XLA Ops:
  1.8 3.2 %collective-permute-start = (s32[8,2432]{1,0:T(8,128)S(1)}, s32[8,2432]{1,0:T(8,128)S(1)}, u32[]{:S(2)}, u32[]{:S(2)}) collective-permute-start(s32[8,2432]{1,0:T(8,128)S(1)} %get-tuple-element.21), channel_id=1, source_target_pairs={{0,8},{8,0},{16,24},{24,16},{1,9},{9,1},{17,25},{25,17},{2,10},{10... | collective-permute-start | bytes 233480 | tf_op jit(solution)/shard_map/ppermute | solution.py:578
  2.3 5.5 %collective-permute-start.1 = (s32[8,2432]{1,0:T(8,128)S(1)}, s32[8,2432]{1,0:T(8,128)S(1)}, u32[]{:S(2)}, u32[]{:S(2)}) collective-permute-start(s32[8,2432]{1,0:T(8,128)S(1)} %get-tuple-element.23), channel_id=1, source_target_pairs={{0,16},{8,24},{16,0},{24,8},{1,17},{9,25},{17,1},{25,9},{2,18},{10... | collective-permute-start | bytes 233480 | tf_op jit(solution)/shard_map/ppermute | solution.py:578
  4.9 4.3 %collective-permute-start.2 = (s32[8,2432]{1,0:T(8,128)S(1)}, s32[8,2432]{1,0:T(8,128)S(1)}, u32[]{:S(2)}, u32[]{:S(2)}) collective-permute-start(s32[8,2432]{1,0:T(8,128)S(1)} %get-tuple-element.24), channel_id=1, source_target_pairs={{0,24},{8,16},{16,8},{24,0},{1,25},{9,17},{17,9},{25,1},{2,26},{10... | collective-permute-start | bytes 233480 | tf_op jit(solution)/shard_map/ppermute | solution.py:578
  5.0 6.3 %collective-permute-start.3 = (s32[8,1792]{1,0:T(8,128)S(1)}, s32[8,1792]{1,0:T(8,128)S(1)}, u32[]{:S(2)}, u32[]{:S(2)}) collective-permute-start(s32[8,1792]{1,0:T(8,128)S(1)} %get-tuple-element.27), channel_id=1, source_target_pairs={{0,8},{8,0},{16,24},{24,16},{1,9},{9,1},{17,25},{25,17},{2,10},{10... | collective-permute-start | bytes 172040 | tf_op jit(solution)/shard_map/ppermute | solution.py:578
  5.2 6.1 %collective-permute-start.4 = (s32[8,1792]{1,0:T(8,128)S(1)}, s32[8,1792]{1,0:T(8,128)S(1)}, u32[]{:S(2)}, u32[]{:S(2)}) collective-permute-start(s32[8,1792]{1,0:T(8,128)S(1)} %get-tuple-element.28), channel_id=1, source_target_pairs={{0,16},{8,24},{16,0},{24,8},{1,17},{9,25},{17,1},{25,9},{2,18},{10... | collective-permute-start | bytes 172040 | tf_op jit(solution)/shard_map/ppermute | solution.py:578
  7.1 4.5 %collective-permute-start.5 = (s32[8,1792]{1,0:T(8,128)S(1)}, s32[8,1792]{1,0:T(8,128)S(1)}, u32[]{:S(2)}, u32[]{:S(2)}) collective-permute-start(s32[8,1792]{1,0:T(8,128)S(1)} %get-tuple-element.29), channel_id=1, source_target_pairs={{0,24},{8,16},{16,8},{24,0},{1,25},{9,17},{17,9},{25,1},{2,26},{10... | collective-permute-start | bytes 172040 | tf_op jit(solution)/shard_map/ppermute | solution.py:578
  13.4 1.3 %collective-permute-start.6 = (f32[2,40,128]{2,1,0:T(8,128)S(1)}, f32[2,40,128]{2,1,0:T(8,128)S(1)}, u32[]{:S(2)}, u32[]{:S(2)}) collective-permute-start(f32[2,40,128]{2,1,0:T(8,128)S(1)} %dynamic-slice_bitcast_fusion), channel_id=1, source_target_pairs={{0,8},{8,0},{16,24},{24,16},{1,9},{9,1},{17,25},{25,17},{2,10},{10... | collective-permute-start | bytes 122888 | tf_op jit(solution)/shard_map/ppermute | solution.py:578
  14.7 3.3 %collective-permute-start.7 = (f32[40,128]{1,0:T(8,128)S(1)}, f32[40,128]{1,0:T(8,128)S(1)}, u32[]{:S(2)}, u32[]{:S(2)}) collective-permute-start(f32[40,128]{1,0:T(8,128)S(1)} %dynamic-slice_bitcast_fusion.1), channel_id=1, source_target_pairs={{0,24},{1,25},{2,26},{3,27},{4,28},{5,29},{6,30},{7,31},{8,16},{9,... | collective-permute-start | bytes 61448 | tf_op jit(solution)/shard_map/ppermute | solution.py:583
  18.0 3.2 %collective-permute-start.8 = (f32[40,128]{1,0:T(8,128)S(1)}, f32[40,128]{1,0:T(8,128)S(1)}, u32[]{:S(2)}, u32[]{:S(2)}) collective-permute-start(f32[40,128]{1,0:T(8,128)S(1)} %bitcast_add_fusion.1), channel_id=1, source_target_pairs={{0,10},{1,11},{2,8},{3,9},{4,14},{5,15},{6,12},{7,13},{8,2},{9,3},... | collective-permute-start | bytes 61448 | tf_op jit(solution)/shard_map/ppermute | solution.py:583
  21.2 4.2 %collective-permute-start.9 = (f32[40,128]{1,0:T(8,128)S(1)}, f32[40,128]{1,0:T(8,128)S(1)}, u32[]{:S(2)}, u32[]{:S(2)}) collective-permute-start(f32[40,128]{1,0:T(8,128)S(1)} %add.42), channel_id=1, source_target_pairs={{0,12},{1,13},{2,14},{3,15},{4,8},{5,9},{6,10},{7,11},{8,4},{9,5},... | collective-permute-start | bytes 61448 | tf_op jit(solution)/shard_map/ppermute | solution.py:583
  25.3 3.2 %collective-permute-start.10 = (f32[40,128]{1,0:T(8,128)S(1)}, f32[40,128]{1,0:T(8,128)S(1)}, u32[]{:S(2)}, u32[]{:S(2)}) collective-permute-start(f32[40,128]{1,0:T(8,128)S(1)} %add.43), channel_id=1, source_target_pairs={{0,9},{1,8},{2,11},{3,10},{4,13},{5,12},{6,15},{7,14},{8,1},{9,0},... | collective-permute-start | bytes 61448 | tf_op jit(solution)/shard_map/ppermute | solution.py:583
  28.5 1.3 %collective-permute-start.11 = (f32[40,128]{1,0:T(8,128)S(1)}, f32[40,128]{1,0:T(8,128)S(1)}, u32[]{:S(2)}, u32[]{:S(2)}) collective-permute-start(f32[40,128]{1,0:T(8,128)S(1)} %add.44.sum_ref), channel_id=1, source_target_pairs={{0,8},{8,0},{16,24},{24,16},{1,9},{9,1},{17,25},{25,17},{2,10},{10... | collective-permute-start | bytes 61448 | tf_op jit(solution)/shard_map/ppermute | solution.py:578

commit v10 on v8

--- a/solution.py
+++ b/solution.py
@@ -629,7 +629,7 @@
         pieces = [cut[:, :part] for cut in cuts[p * GROUPS : (p + 1) * GROUPS]]
         sums.append(
             pl.pallas_call(
-                functools.partial(window_kernel, STEP, p == 0),
+                functools.partial(window_kernel, part, p == 0),
                 out_shape=jax.ShapeDtypeStruct((2, TALL, LANES), F32),
                 in_specs=[VMEM] * (2 * GROUPS + 1),
                 out_specs=VMEM,

time: 30.7 us -> 30.7 us (level)
  no operation moved by 1% of the time
where the time goes in v10:
time: 30.7 us; the launch traced here: 30.6 us
  starting transfers between devices  13.5 us (44%)
  waiting for transfers between devices  9.62 us (31%)
  Pallas kernels  6.58 us (21%)
  between operations  0.75 us (2%)
    ppermute x4, starting transfers between devices, exchange_flat(): lax.ppermute(x, ('group', 'batch'), [(i, i ^ by) for i in range(peers)])  7.64 us
    ppermute x4, waiting for transfers between devices, exchange_flat(): lax.ppermute(x, ('group', 'batch'), [(i, i ^ by) for i in range(peers)])  6.21 us
    ppermute x8, starting transfers between devices, exchange(): return lax.ppermute(x, axis, [(i, i ^ by) for i in range(peers)])  5.88 us
    pallas_call x2, Pallas kernels, on_device_windows(): pl.pallas_call(functools.partial(window_kernel, part, p == 0), out_shape=...  3.81 us
    ppermute x8, waiting for transfers between devices, exchange(): return lax.ppermute(x, axis, [(i, i ^ by) for i in range(peers)])  3.42 us
    pallas_call x1, Pallas kernels, on_device_windows(): pl.pallas_call(functools.partial(pack_kernel, widths), out_shape=shapes +...  1.15 us
    pallas_call x1, Pallas kernels, on_device_windows(): pl.pallas_call(functools.partial(solve_kernel, float(width * copies), flo...  0.92 us
    pallas_call x1, Pallas kernels, on_device_windows(): pl.pallas_call(contract_kernel, out_shape=[jax.ShapeDtypeStruct((2, ROWS)...  0.71 us
  transfers between devices with their start and end apart: 12, of which 8 were waited for; matrix products, arithmetic and copies ran while one was open for 0% of the time, Pallas kernels for 10%

profile of v10, /device:TPU:0, one launch (start us, length us, event | category | flops | bytes accessed | tf_op | source)
XLA Modules:
  0.0 30.6 jit_solution(15696050453609859607)
XLA Ops:
  0.6 1.1 %pack.1 = (s32[8,2432]{1,0:T(8,128)S(1)}, s32[8,2432]{1,0:T(8,128)S(1)}, s32[8,2432]{1,0:T(8,128)S(1)}, s32[8,2432]{1,0:T(8,128)S(1)}, s32[8,1792]{1,0:T(8,128)S...) custom-call(s32[2,8]{1,0:T(2,128)} %geno_ref.1, ...), custom_call_target="tpu_custom_call" | custom-call | tf_op jit(solution)/shard_map/pack/pallas_call | solution.py:604
  1.8 0.5 %collective-permute-start = (s32[8,2432]{1,0:T(8,128)S(1)}, s32[8,2432]{1,0:T(8,128)S(1)}, u32[]{:S(2)}, u32[]{:S(2)}) collective-permute-start(s32[8,2432]{1,0:T(8,128)S(1)} %get-tuple-element.21), channel_id=1, source_target_pairs={{0,8},{8,0},{16,24},{24,16},{1,9},{9,1},{17,25},{25,17},{2,10},{10... | collective-permute-start | bytes 233480 | tf_op jit(solution)/shard_map/ppermute | solution.py:578
  2.3 2.6 %collective-permute-start.1 = (s32[8,2432]{1,0:T(8,128)S(1)}, s32[8,2432]{1,0:T(8,128)S(1)}, u32[]{:S(2)}, u32[]{:S(2)}) collective-permute-start(s32[8,2432]{1,0:T(8,128)S(1)} %get-tuple-element.23), channel_id=1, source_target_pairs={{0,16},{8,24},{16,0},{24,8},{1,17},{9,25},{17,1},{25,9},{2,18},{10... | collective-permute-start | bytes 233480 | tf_op jit(solution)/shard_map/ppermute | solution.py:578
  4.9 0.1 collective-permute-start.2
  5.0 0.0 collective-permute-done
  5.0 0.2 collective-permute-start.3
  5.2 1.9 %collective-permute-start.4 = (s32[8,1792]{1,0:T(8,128)S(1)}, s32[8,1792]{1,0:T(8,128)S(1)}, u32[]{:S(2)}, u32[]{:S(2)}) collective-permute-start(s32[8,1792]{1,0:T(8,128)S(1)} %get-tuple-element.28), channel_id=1, source_target_pairs={{0,16},{8,24},{16,0},{24,8},{1,17},{9,25},{17,1},{25,9},{2,18},{10... | collective-permute-start | bytes 172040 | tf_op jit(solution)/shard_map/ppermute | solution.py:578
  7.1 0.0 collective-permute-start.5
  7.1 0.7 %collective-permute-done.1 = s32[8,2432]{1,0:T(8,128)S(1)} collective-permute-done((s32[8,2432]{1,0:T(8,128)S(1)}, s32[8,2432]{1,0:T(8,128)S(1)}, u32[]{:S(2)}, u32[]{:S(2)}) %collective-permute-start.1) | collective-permute-done | bytes 77856 | tf_op jit(solution)/shard_map/ppermute | solution.py:578
  7.8 1.4 %collective-permute-done.2 = s32[8,2432]{1,0:T(8,128)S(1)} collective-permute-done((s32[8,2432]{1,0:T(8,128)S(1)}, s32[8,2432]{1,0:T(8,128)S(1)}, u32[]{:S(2)}, u32[]{:S(2)}) %collective-permute-start.2) | collective-permute-done | bytes 77856 | tf_op jit(solution)/shard_map/ppermute | solution.py:578
  9.2 2.1 %windows.2 = f32[2,80,128]{2,1,0:T(8,128)S(1)} custom-call(s32[8,2304]{1,0:T(8,128)S(1)} %slice.24.refs_0_, s32[8,2304]{1,0:T(8,128)S(1)} %slice.25.refs_1_, s32[8,2304]{1,0:T(8,128)S(1)} %slice.32.refs_2_, s32[8,2304]{1,0:T(8,128)S(1)} %slice.33.refs_3_, s32[8,128]{1,0:T(8,128)S(1)} %slice.28.refs_4_, s32[8,128]{1,0:T(8,128)S(1)} %slice.29.refs_5_, ...), custom_call_target="tpu_custom_call" | custom-call | flops 2073600000 | tf_op jit(solution)/shard_map/windows/pallas_call | solution.py:631
  11.3 0.0 collective-permute-done.3.refs_1_
  11.3 0.0 collective-permute-done.4.refs_2_
  11.3 0.3 %collective-permute-done.5.refs_3_ = s32[8,1792]{1,0:T(8,128)S(1)} collective-permute-done((s32[8,1792]{1,0:T(8,128)S(1)}, s32[8,1792]{1,0:T(8,128)S(1)}, u32[]{:S(2)}, u32[]{:S(2)}) %collective-permute-start.5) | collective-permute-done | bytes 57376 | tf_op jit(solution)/shard_map/ppermute | solution.py:578
  11.6 1.7 %windows.3 = f32[2,80,128]{2,1,0:T(8,128)S(1)} custom-call(s32[8,1792]{1,0:T(8,128)S(1)} %get-tuple-element.26.refs_0_, s32[8,1792]{1,0:T(8,128)S(1)} %collective-permute-done.3.refs_1_, s32[8,1792]{1,0:T(8,128)S(1)} %collective-permute-done.4.refs_2_, s32[8,1792]{1,0:T(8,128)S(1)} %collective-permute-done.5.refs_3_, s32[8,128]{1,0:T(8,128)S(1)} %slice.28.refs_4_, ...), custom_call_target="tpu_custom_call" | custom-call | flops 1612800000 | tf_op jit(solution)/shard_map/windows/pallas_call | solution.py:631
  13.4 0.2 collective-permute-start.6
  13.7 1.0 %collective-permute-done.6 = f32[2,40,128]{2,1,0:T(8,128)S(1)} collective-permute-done((f32[2,40,128]{2,1,0:T(8,128)S(1)}, f32[2,40,128]{2,1,0:T(8,128)S(1)}, u32[]{:S(2)}, u32[]{:S(2)}) %collective-permute-start.6) | collective-permute-done | bytes 40992 | tf_op jit(solution)/shard_map/ppermute | solution.py:578
  14.7 1.7 %collective-permute-start.7 = (f32[40,128]{1,0:T(8,128)S(1)}, f32[40,128]{1,0:T(8,128)S(1)}, u32[]{:S(2)}, u32[]{:S(2)}) collective-permute-start(f32[40,128]{1,0:T(8,128)S(1)} %dynamic-slice_bitcast_fusion.1), channel_id=1, source_target_pairs={{0,24},{1,25},{2,26},{3,27},{4,28},{5,29},{6,30},{7,31},{8,16},{9,... | collective-permute-start | bytes 61448 | tf_op jit(solution)/shard_map/ppermute | solution.py:583
  16.4 1.6 %collective-permute-done.7 = f32[40,128]{1,0:T(8,128)S(1)} collective-permute-done((f32[40,128]{1,0:T(8,128)S(1)}, f32[40,128]{1,0:T(8,128)S(1)}, u32[]{:S(2)}, u32[]{:S(2)}) %collective-permute-start.7) | collective-permute-done | bytes 20512 | tf_op jit(solution)/shard_map/ppermute | solution.py:583
  18.0 1.6 %collective-permute-start.8 = (f32[40,128]{1,0:T(8,128)S(1)}, f32[40,128]{1,0:T(8,128)S(1)}, u32[]{:S(2)}, u32[]{:S(2)}) collective-permute-start(f32[40,128]{1,0:T(8,128)S(1)} %bitcast_add_fusion.1), channel_id=1, source_target_pairs={{0,9},{1,8},{2,11},{3,10},{4,13},{5,12},{6,15},{7,14},{8,1},{9,0},... | collective-permute-start | bytes 61448 | tf_op jit(solution)/shard_map/ppermute | solution.py:583
  19.6 1.6 %collective-permute-done.8 = f32[40,128]{1,0:T(8,128)S(1)} collective-permute-done((f32[40,128]{1,0:T(8,128)S(1)}, f32[40,128]{1,0:T(8,128)S(1)}, u32[]{:S(2)}, u32[]{:S(2)}) %collective-permute-start.8) | collective-permute-done | bytes 20512 | tf_op jit(solution)/shard_map/ppermute | solution.py:583
  21.2 1.7 %collective-permute-start.9 = (f32[40,128]{1,0:T(8,128)S(1)}, f32[40,128]{1,0:T(8,128)S(1)}, u32[]{:S(2)}, u32[]{:S(2)}) collective-permute-start(f32[40,128]{1,0:T(8,128)S(1)} %add.42), channel_id=1, source_target_pairs={{0,10},{1,11},{2,8},{3,9},{4,14},{5,15},{6,12},{7,13},{8,2},{9,3},... | collective-permute-start | bytes 61448 | tf_op jit(solution)/shard_map/ppermute | solution.py:583
  22.9 1.5 %collective-permute-done.9 = f32[40,128]{1,0:T(8,128)S(1)} collective-permute-done((f32[40,128]{1,0:T(8,128)S(1)}, f32[40,128]{1,0:T(8,128)S(1)}, u32[]{:S(2)}, u32[]{:S(2)}) %collective-permute-start.9) | collective-permute-done | bytes 20512 | tf_op jit(solution)/shard_map/ppermute | solution.py:583
  24.4 2.7 %collective-permute-start.10 = (f32[40,128]{1,0:T(8,128)S(1)}, f32[40,128]{1,0:T(8,128)S(1)}, u32[]{:S(2)}, u32[]{:S(2)}) collective-permute-start(f32[40,128]{1,0:T(8,128)S(1)} %add.43), channel_id=1, source_target_pairs={{0,12},{1,13},{2,14},{3,15},{4,8},{5,9},{6,10},{7,11},{8,4},{9,5},... | collective-permute-start | bytes 61448 | tf_op jit(solution)/shard_map/ppermute | solution.py:583
  27.1 1.5 %collective-permute-done.10 = f32[40,128]{1,0:T(8,128)S(1)} collective-permute-done((f32[40,128]{1,0:T(8,128)S(1)}, f32[40,128]{1,0:T(8,128)S(1)}, u32[]{:S(2)}, u32[]{:S(2)}) %collective-permute-start.10) | collective-permute-done | bytes 20512 | tf_op jit(solution)/shard_map/ppermute | solution.py:583
  28.6 0.3 %collective-permute-start.11 = (f32[40,128]{1,0:T(8,128)S(1)}, f32[40,128]{1,0:T(8,128)S(1)}, u32[]{:S(2)}, u32[]{:S(2)}) collective-permute-start(f32[40,128]{1,0:T(8,128)S(1)} %add.44.sum_ref), channel_id=1, source_target_pairs={{0,8},{8,0},{16,24},{24,16},{1,9},{9,1},{17,25},{25,17},{2,10},{10... | collective-permute-start | bytes 61448 | tf_op jit(solution)/shard_map/ppermute | solution.py:578
  28.9 0.9 %solve.1.weight_ref = f32[72,128]{1,0:T(8,128)S(1)} custom-call(f32[40,128]{1,0:T(8,128)S(1)} %add.44.sum_ref), custom_call_target="tpu_custom_call" | custom-call | flops 1000000 | tf_op jit(solution)/shard_map/solve/pallas_call | solution.py:663
  29.8 0.0 collective-permute-done.11
  29.9 0.7 %contract.1 = (f32[2,8]{1,0:T(2,128)}, f32[1,2]{1,0:T(1,128)}) custom-call(f32[72,128]{1,0:T(8,128)S(1)} %solve.1.weight_ref, f32[80,128]{1,0:T(8,128)S(1)} %maximum_select_fusion.t_ref), custom_call_target="tpu_custom_call" | custom-call | tf_op jit(solution)/shard_map/contract/pallas_call | solution.py:673
  (17 shorter events, 0.1 us)
Async XLA Ops:
  1.8 3.2 %collective-permute-start = (s32[8,2432]{1,0:T(8,128)S(1)}, s32[8,2432]{1,0:T(8,128)S(1)}, u32[]{:S(2)}, u32[]{:S(2)}) collective-permute-start(s32[8,2432]{1,0:T(8,128)S(1)} %get-tuple-element.21), channel_id=1, source_target_pairs={{0,8},{8,0},{16,24},{24,16},{1,9},{9,1},{17,25},{25,17},{2,10},{10... | collective-permute-start | bytes 233480 | tf_op jit(solution)/shard_map/ppermute | solution.py:578
  2.3 5.5 %collective-permute-start.1 = (s32[8,2432]{1,0:T(8,128)S(1)}, s32[8,2432]{1,0:T(8,128)S(1)}, u32[]{:S(2)}, u32[]{:S(2)}) collective-permute-start(s32[8,2432]{1,0:T(8,128)S(1)} %get-tuple-element.23), channel_id=1, source_target_pairs={{0,16},{8,24},{16,0},{24,8},{1,17},{9,25},{17,1},{25,9},{2,18},{10... | collective-permute-start | bytes 233480 | tf_op jit(solution)/shard_map/ppermute | solution.py:578
  4.9 4.3 %collective-permute-start.2 = (s32[8,2432]{1,0:T(8,128)S(1)}, s32[8,2432]{1,0:T(8,128)S(1)}, u32[]{:S(2)}, u32[]{:S(2)}) collective-permute-start(s32[8,2432]{1,0:T(8,128)S(1)} %get-tuple-element.24), channel_id=1, source_target_pairs={{0,24},{8,16},{16,8},{24,0},{1,25},{9,17},{17,9},{25,1},{2,26},{10... | collective-permute-start | bytes 233480 | tf_op jit(solution)/shard_map/ppermute | solution.py:578
  5.0 6.3 %collective-permute-start.3 = (s32[8,1792]{1,0:T(8,128)S(1)}, s32[8,1792]{1,0:T(8,128)S(1)}, u32[]{:S(2)}, u32[]{:S(2)}) collective-permute-start(s32[8,1792]{1,0:T(8,128)S(1)} %get-tuple-element.27), channel_id=1, source_target_pairs={{0,8},{8,0},{16,24},{24,16},{1,9},{9,1},{17,25},{25,17},{2,10},{10... | collective-permute-start | bytes 172040 | tf_op jit(solution)/shard_map/ppermute | solution.py:578
  5.2 6.1 %collective-permute-start.4 = (s32[8,1792]{1,0:T(8,128)S(1)}, s32[8,1792]{1,0:T(8,128)S(1)}, u32[]{:S(2)}, u32[]{:S(2)}) collective-permute-start(s32[8,1792]{1,0:T(8,128)S(1)} %get-tuple-element.28), channel_id=1, source_target_pairs={{0,16},{8,24},{16,0},{24,8},{1,17},{9,25},{17,1},{25,9},{2,18},{10... | collective-permute-start | bytes 172040 | tf_op jit(solution)/shard_map/ppermute | solution.py:578
  7.1 4.5 %collective-permute-start.5 = (s32[8,1792]{1,0:T(8,128)S(1)}, s32[8,1792]{1,0:T(8,128)S(1)}, u32[]{:S(2)}, u32[]{:S(2)}) collective-permute-start(s32[8,1792]{1,0:T(8,128)S(1)} %get-tuple-element.29), channel_id=1, source_target_pairs={{0,24},{8,16},{16,8},{24,0},{1,25},{9,17},{17,9},{25,1},{2,26},{10... | collective-permute-start | bytes 172040 | tf_op jit(solution)/shard_map/ppermute | solution.py:578
  13.4 1.3 %collective-permute-start.6 = (f32[2,40,128]{2,1,0:T(8,128)S(1)}, f32[2,40,128]{2,1,0:T(8,128)S(1)}, u32[]{:S(2)}, u32[]{:S(2)}) collective-permute-start(f32[2,40,128]{2,1,0:T(8,128)S(1)} %dynamic-slice_bitcast_fusion), channel_id=1, source_target_pairs={{0,8},{8,0},{16,24},{24,16},{1,9},{9,1},{17,25},{25,17},{2,10},{10... | collective-permute-start | bytes 122888 | tf_op jit(solution)/shard_map/ppermute | solution.py:578
  14.7 3.3 %collective-permute-start.7 = (f32[40,128]{1,0:T(8,128)S(1)}, f32[40,128]{1,0:T(8,128)S(1)}, u32[]{:S(2)}, u32[]{:S(2)}) collective-permute-start(f32[40,128]{1,0:T(8,128)S(1)} %dynamic-slice_bitcast_fusion.1), channel_id=1, source_target_pairs={{0,24},{1,25},{2,26},{3,27},{4,28},{5,29},{6,30},{7,31},{8,16},{9,... | collective-permute-start | bytes 61448 | tf_op jit(solution)/shard_map/ppermute | solution.py:583
  18.0 3.2 %collective-permute-start.8 = (f32[40,128]{1,0:T(8,128)S(1)}, f32[40,128]{1,0:T(8,128)S(1)}, u32[]{:S(2)}, u32[]{:S(2)}) collective-permute-start(f32[40,128]{1,0:T(8,128)S(1)} %bitcast_add_fusion.1), channel_id=1, source_target_pairs={{0,9},{1,8},{2,11},{3,10},{4,13},{5,12},{6,15},{7,14},{8,1},{9,0},... | collective-permute-start | bytes 61448 | tf_op jit(solution)/shard_map/ppermute | solution.py:583
  21.2 3.2 %collective-permute-start.9 = (f32[40,128]{1,0:T(8,128)S(1)}, f32[40,128]{1,0:T(8,128)S(1)}, u32[]{:S(2)}, u32[]{:S(2)}) collective-permute-start(f32[40,128]{1,0:T(8,128)S(1)} %add.42), channel_id=1, source_target_pairs={{0,10},{1,11},{2,8},{3,9},{4,14},{5,15},{6,12},{7,13},{8,2},{9,3},... | collective-permute-start | bytes 61448 | tf_op jit(solution)/shard_map/ppermute | solution.py:583
  24.4 4.2 %collective-permute-start.10 = (f32[40,128]{1,0:T(8,128)S(1)}, f32[40,128]{1,0:T(8,128)S(1)}, u32[]{:S(2)}, u32[]{:S(2)}) collective-permute-start(f32[40,128]{1,0:T(8,128)S(1)} %add.43), channel_id=1, source_target_pairs={{0,12},{1,13},{2,14},{3,15},{4,8},{5,9},{6,10},{7,11},{8,4},{9,5},... | collective-permute-start | bytes 61448 | tf_op jit(solution)/shard_map/ppermute | solution.py:583
  28.6 1.3 %collective-permute-start.11 = (f32[40,128]{1,0:T(8,128)S(1)}, f32[40,128]{1,0:T(8,128)S(1)}, u32[]{:S(2)}, u32[]{:S(2)}) collective-permute-start(f32[40,128]{1,0:T(8,128)S(1)} %add.44.sum_ref), channel_id=1, source_target_pairs={{0,8},{8,0},{16,24},{24,16},{1,9},{9,1},{17,25},{25,17},{2,10},{10... | collective-permute-start | bytes 61448 | tf_op jit(solution)/shard_map/ppermute | solution.py:578
